TPU v7x, 512 devices: a whole 4x4x16 slice. The times are simulated.
512 devices in a mesh: bins: 128 (over z, y_lo, x), lat: 4 (over y_hi, core).
Axes of the slice: x: 4, y: 4 (y_hi: 2, y_lo: 2; y = y_hi * 2 + y_lo), z: 16, core: 2. Of those that a mesh axis runs over, the one named last changes fastest.
Arguments:
- spectrum: float32 [1152, 64, 384], P('bins', 'lat'), may hold values from 0.05 to 2
- sea_mask: int32 [64, 384], P('lat'), may hold values 0 or 1
- current: float32 [768, 128], P('bins', 'lat'), may hold values from -0.6 to 0.6
- partner_plus: int32 [1152], replicated, may hold values from 0 to 1151
- partner_minus: int32 [1152], replicated, may hold values from 0 to 1151
- source_map: int32 [768, 128], P('bins', 'lat'), may hold values from 0 to 8
Outputs:
- spectrum_out: float32 [1152, 64, 384], P('bins', 'lat')
- stokes: float32 [2, 64, 768, 128], P(None, None, 'bins', 'lat')
All inputs are finite; a program needn't handle non-finite values. No bound on the sum of `sea_mask` on one device may be relied on, other than what follows from the above.
Results may differ from a plain program's by a relative error of at most 0.000086.
Values sent between devices are 32-bit elements; how exact they have to be, the bound alone decides.
No kernel may reach another device: no remote copies, remote signals or barrier semaphores. Data moves between devices by JAX's collectives and lax.ppermute only.
A program may use at most 64 MiB of HBM per device.

v0:
```python
import math

import jax
import jax.numpy as jnp
from jax import lax
from jax.sharding import Mesh
from jax.sharding import PartitionSpec as P

NDIR = 36
NFREQ = 32
LEV = 64
BINS = ("bins_0", "bins_1", "bins_2")


HIGHEST = lax.Precision.HIGHEST


def laid_out(blocks, dim):
    blocks = jnp.moveaxis(blocks, 0, dim)
    shape = blocks.shape
    return blocks.reshape(*shape[:dim], shape[dim] * shape[dim + 1], *shape[dim + 2 :])


def gather_in_order(shard, axes, sequence):
    blocks = shard[None]
    for k in sequence:
        blocks = lax.all_gather(blocks, axes[k], axis=0, tiled=True)
    current = [lax.axis_size(axes[k]) for k in reversed(sequence)]
    blocks = blocks.reshape(*current, *shard.shape)
    turned = sorted(range(len(sequence)), key=lambda place: sequence[len(sequence) - 1 - place])
    return blocks.transpose(*turned, *range(len(sequence), blocks.ndim)).reshape(-1, *shard.shape)


def gather_axes(shard, axes, sequence, dim):
    return laid_out(gather_in_order(shard, axes, sequence), dim)


def extended(block, sides, width):
    for axis, dim in sides:
        count = lax.axis_size(axis)
        forward = [(i, i + 1) for i in range(count - 1)]
        backward = [(target, source) for source, target in forward]
        low = lax.ppermute(
            lax.slice_in_dim(block, block.shape[dim] - width, None, axis=dim), axis, forward
        )
        high = lax.ppermute(lax.slice_in_dim(block, 0, width, axis=dim), axis, backward)
        block = jnp.concatenate([low, block, high], axis=dim)
    return block


def bin_tables():
    dir_index = jnp.arange(NDIR, dtype=jnp.float32)
    freq_index = jnp.arange(NFREQ, dtype=jnp.float32)
    angles = 2.0 * math.pi * (dir_index + 0.5) / NDIR
    speeds = 0.12 + 0.25 * (NFREQ - 1 - freq_index) / (NFREQ - 1)
    along_x = jnp.repeat(speeds, NDIR) * jnp.tile(jnp.cos(angles), NFREQ)
    along_y = jnp.repeat(speeds, NDIR) * jnp.tile(jnp.sin(angles), NFREQ)
    strength = jnp.repeat(0.06 * (1.0 + freq_index / (NFREQ - 1)), NDIR)
    levels = jnp.arange(LEV, dtype=jnp.float32) + 0.5
    wavenumber = 0.02 * jnp.power(1.15, freq_index)
    decay = jnp.repeat(jnp.exp(-levels[:, None] * wavenumber[None, :]), NDIR, axis=1)
    amplitude = 2.0 / math.sqrt(NDIR * NFREQ)
    cosines = jnp.tile(jnp.cos(angles), NFREQ)
    sines = jnp.tile(jnp.sin(angles), NFREQ)
    drift_table = amplitude * jnp.concatenate(
        [decay * cosines[None, :], decay * sines[None, :]], axis=0
    )
    return (along_x, along_y, strength, drift_table)


def cell_means(current_cells):
    lon_count = current_cells.shape[0] // 2
    lat_count = current_cells.shape[1] // 2
    return current_cells.reshape(lon_count, 2, lat_count, 2).mean(axis=(1, 3))


def face_fluxes(padded, velocity, dimension):
    face_count = padded.shape[dimension] - 3

    def section(low_edge):
        return lax.slice_in_dim(padded, low_edge, low_edge + face_count, axis=dimension)

    left_value = (-section(0) + 5.0 * section(1) + 2.0 * section(2)) / 6.0
    right_value = (2.0 * section(1) + 5.0 * section(2) - section(3)) / 6.0
    return jnp.maximum(velocity, 0.0) * left_value + jnp.minimum(velocity, 0.0) * right_value


def transport(padded_rows, zonal_flow, along_x, along_y, sea_cells):
    row_count = padded_rows.shape[1] - 4
    spectra = padded_rows[:, 2 : 2 + row_count, :]
    padded_cols = jnp.pad(spectra, ((0, 0), (0, 0), (2, 2)))
    zonal_padded = jnp.pad(zonal_flow, ((0, 0), (1, 1)))
    face_zonal = 0.5 * (zonal_padded[:, :-1] + zonal_padded[:, 1:])
    speed_x = along_x[:, None, None] + face_zonal[None, :, :]
    flux_x = face_fluxes(padded_cols, speed_x, 2)
    flux_y = face_fluxes(padded_rows, along_y[:, None, None], 1)
    change = flux_x[:, :, 1:] - flux_x[:, :, :-1] + flux_y[:, 1:, :] - flux_y[:, :-1, :]
    return sea_cells[None, :, :] * (spectra - change)


def spread_to_ocean(rim, source_map):
    row_count = rim.shape[1] - 2
    col_count = rim.shape[2] - 2
    result = jnp.zeros((rim.shape[0], 2 * col_count, 2 * row_count), jnp.float32)
    for offset in range(9):
        row_shift = offset // 3 - 1
        col_shift = offset % 3 - 1
        shifted = rim[
            :, 1 + row_shift : 1 + row_shift + row_count, 1 + col_shift : 1 + col_shift + col_count
        ]
        shifted = jnp.swapaxes(shifted, 1, 2)
        shifted = jnp.repeat(jnp.repeat(shifted, 2, axis=1), 2, axis=2)
        result = result + jnp.where(source_map[None, :, :] == offset, shifted, jnp.float32(0.0))
    return result


def on_device(spectrum, sea_mask, current, partner_plus, partner_minus, source_map):
    along_x, along_y, strength, drift_table = bin_tables()
    bin_count = NDIR * NFREQ
    local_bins = spectrum.shape[0]
    first_bin = lax.axis_index(BINS) * local_bins
    local_x = lax.dynamic_slice_in_dim(along_x, first_bin, local_bins)
    local_y = lax.dynamic_slice_in_dim(along_y, first_bin, local_bins)
    sea_cells = sea_mask.astype(jnp.float32)
    strip_flow = cell_means(current)
    zonal_flow = gather_axes(strip_flow, BINS, (1, 2, 0), 0).T
    masked = spectrum * sea_cells[None, :, :]
    padded = extended(masked, (("lat", 1),), 2)
    after_first = transport(padded, zonal_flow, local_x, local_y, sea_cells)
    bin_ids = jnp.arange(bin_count, dtype=jnp.int32)
    plus_table = (partner_plus[:, None] == bin_ids[None, :]).astype(jnp.float32)
    minus_table = (partner_minus[:, None] == bin_ids[None, :]).astype(jnp.float32)
    contract_first = (((0,), (0,)), ((), ()))
    arrived = lax.all_to_all(after_first, BINS, split_axis=2, concat_axis=0, tiled=True)
    row_count = arrived.shape[1]
    col_count = arrived.shape[2]
    flat_rows = arrived.reshape(bin_count, row_count * col_count)
    plus_part = jnp.dot(plus_table, flat_rows, precision=HIGHEST)
    minus_part = jnp.dot(minus_table, flat_rows, precision=HIGHEST)
    source = strength[:, None] * (
        flat_rows * flat_rows * (plus_part + minus_part) - 2.0 * flat_rows * plus_part * minus_part
    )
    back = lax.dot_general(plus_table, source, contract_first, precision=HIGHEST) + lax.dot_general(
        minus_table, source, contract_first, precision=HIGHEST
    )
    middle = flat_rows + (source - 0.5 * back)
    drift_rows = jnp.dot(drift_table, middle, precision=HIGHEST)
    middle, drift_rows = (
        middle.reshape(bin_count, row_count, col_count),
        drift_rows.reshape(2 * LEV, row_count, col_count),
    )
    rim = extended(drift_rows, ((BINS, 2), ("lat", 1)), 1)
    ocean = spread_to_ocean(rim, source_map)
    stokes = ocean.reshape(2, LEV, ocean.shape[1], ocean.shape[2])
    returned = lax.all_to_all(middle, BINS, split_axis=0, concat_axis=2, tiled=True)
    padded_again = extended(returned, (("lat", 1),), 2)
    second = transport(padded_again, zonal_flow, local_x, local_y, sea_cells)
    return (second, stokes)


def solution(mesh):
    finer = Mesh(
        mesh.devices.reshape(16, 2, 4, mesh.shape["lat"]), ("bins_0", "bins_1", "bins_2", "lat")
    )
    in_specs = (P(BINS, "lat", None), P("lat", None), P(BINS, "lat"), P(), P(), P(BINS, "lat"))
    out_specs = (P(BINS, "lat", None), P(None, None, BINS, "lat"))
    return jax.shard_map(
        on_device, mesh=finer, in_specs=in_specs, out_specs=out_specs, check_vma=False
    )
```

profile of v0, /device:TPU:33, one launch (start us, length us, event | category | flops | bytes accessed | tf_op | source)
XLA Modules:
  0.0 191.0 jit_solution(7363701047894608623)
XLA Ops:
  2.4 5.4 %collective-permute-start = (f32[9,2,384]{2,1,0:T(2,128)S(1)}, f32[9,2,384]{2,1,0:T(2,128)S(1)}, u32[]{:S(2)}, u32[]{:S(2)}) collective-permute-start(f32[9,2,384]{2,1,0:T(2,128)S(1)} %get-tuple-element.18), channel_id=1, source_target_pairs={{0,1},{1,2},{2,3},{4,5},{5,6},{6,7},{8,9},{9,10},{10,11},{12,13},{... | collective-permute-start | bytes 82952 | tf_op jit(solution)/shard_map/ppermute | solution.py:43
  7.8 1.9 %collective-permute-start.1 = (f32[9,2,384]{2,1,0:T(2,128)S(1)}, f32[9,2,384]{2,1,0:T(2,128)S(1)}, u32[]{:S(2)}, u32[]{:S(2)}) collective-permute-start(f32[9,2,384]{2,1,0:T(2,128)S(1)} %get-tuple-element.19), channel_id=1, source_target_pairs={{1,0},{2,1},{3,2},{5,4},{6,5},{7,6},{9,8},{10,9},{11,10},{13,12},{... | collective-permute-start | bytes 82952 | tf_op jit(solution)/shard_map/ppermute | solution.py:46
  11.2 3.2 %all-gather.1 = f32[2,3,16]{2,1,0:T(4,128)S(1)} all-gather(f32[1,3,16]{2,1,0:T(4,128)S(1)} %multiply_bitcast_fusion), channel_id=2, replica_groups=mesh['bins_0'=16,'bins_1'=2,'bins_2'=4,'lat'=4] {'bins_1'}, dimensions={0}, use_global_device_ids=true | all-gather | bytes 576 | tf_op jit(solution)/shard_map/all_gather | solution.py:27
  14.4 9.4 %all_gather.10 = f32[8,3,16]{2,1,0:T(4,128)S(1)} all-gather(f32[2,3,16]{2,1,0:T(4,128)S(1)} %all-gather.1), channel_id=1, replica_groups=mesh['bins_0'=16,'bins_1'=2,'bins_2'=4,'lat'=4] {'bins_2'}, dimensions={0}, use_global_device_ids=true | all-gather | bytes 1920 | tf_op jit(solution)/shard_map/all_gather | solution.py:27
  23.8 27.8 %all_gather.11 = f32[128,3,16]{2,0,1:T(8,128)S(1)} all-gather(f32[8,3,16]{2,0,1:T(8,128)S(1)} %copy.139), channel_id=1, replica_groups=mesh['bins_0'=16,'bins_1'=2,'bins_2'=4,'lat'=4] {'bins_0'}, dimensions={0}, use_global_device_ids=true | all-gather | bytes 26112 | tf_op jit(solution)/shard_map/all_gather | solution.py:27
  54.1 1.9 reshape.183
  55.9 11.6 %all-to-all-start = ((f32[128,1,432]{2,1,0:T(1,128)}), f32[128,1,432]{2,1,0:T(1,128)S(1)}, u32[]{:S(2)}, u32[]{:S(2)}) async-start(f32[128,1,432]{2,1,0:T(1,128)} %reshape.183), calls=%async_computation | async-start | bytes 524288 | tf_op jit(solution)/shard_map/all_to_all | solution.py:134
  69.3 16.0 %all-to-all-done = f32[128,1,432]{2,1,0:T(1,128)S(1)} async-done(((f32[128,1,432]{2,1,0:T(1,128)}), f32[128,1,432]{2,1,0:T(1,128)S(1)}, u32[]{:S(2)}, u32[]{:S(2)}) %all-to-all-start) | async-done | bytes 221216 | tf_op jit(solution)/shard_map/all_to_all | solution.py:134
  88.0 2.3 %copy.168 = f32[9,16,128,3]{1,3,2,0:T(4,128)} copy(f32[9,16,128,3]{1,0,3,2:T(8,128)S(1)} %bitcast.79) | data formatting | bytes 442368 | tf_op jit(solution)/shard_map/all_to_all | solution.py:134
  90.3 4.4 %copy.144 = f32[128,9,16,3]{1,0,3,2:T(8,128)S(1)} copy(f32[128,9,16,3]{2,3,0,1:T(4,128)} %bitcast.83) | data formatting | bytes 442368 | tf_op jit(solution)/shard_map/all_to_all | solution.py:134
  94.7 1.5 reshape.157
  96.2 2.7 %fusion.1 = f32[1152,48]{0,1:T(8,128)S(1)} fusion(f32[1152,48]{0,1:T(8,128)S(1)} %reshape.157, s32[1152]{0:T(1024)S(1)} %copy-done.9), kind=kOutput, calls=%fused_computation.2 | convolution fusion | flops 765739008 | bytes 446976 | tf_op jit(solution)/shard_map/dot_general | solution.py:139
  99.0 2.7 %subtract_multiply_fusion = f32[1152,48]{0,1:T(8,128)S(1)} fusion(f32[1152,48]{0,1:T(8,128)S(1)} %fusion.1, f32[1152,48]{0,1:T(8,128)S(1)} %reshape.157, s32[1152]{0:T(1024)S(1)} %copy-done.10, f32[1152]{0:T(1024)S(1)} %mul.258), kind=kOutput, calls=%fused_computation.81 | convolution fusion | flops 766181376 | bytes 672768 | tf_op jit(solution)/shard_map/dot_general | solution.py:138
  101.7 2.0 %fusion = f32[1152,48]{0,1:T(8,128)S(1)} fusion(f32[1152,48]{0,1:T(8,128)S(1)} %subtract_multiply_fusion, s32[1152]{0:T(1024)S(1)} %copy-done.9), kind=kOutput, calls=%fused_computation.1 | convolution fusion | flops 765739008 | bytes 446976 | tf_op jit(solution)/shard_map/dot_general | solution.py:143
  103.7 2.0 %fusion.11 = f32[1152,48]{0,1:T(8,128)S(1)} fusion(f32[1152,48]{0,1:T(8,128)S(1)} %reshape.157, f32[1152,48]{0,1:T(8,128)S(1)} %subtract_multiply_fusion, f32[1152,48]{0,1:T(8,128)S(1)} %fusion, s32[1152]{0:T(1024)S(1)} %copy-done.10), kind=kOutput, calls=%fused_computation.14 | convolution fusion | flops 765960192 | bytes 889344 | tf_op jit(solution)/shard_map/dot_general | solution.py:143
  106.3 2.1 %collective-permute-start.4 = (f32[128,16,1]{0,2,1:T(1,128)S(1)}, f32[128,16,1]{0,2,1:T(1,128)S(1)}, u32[]{:S(2)}, u32[]{:S(2)}) collective-permute-start(f32[128,16,1]{0,2,1:T(1,128)S(1)} %get-tuple-element.32), channel_id=1, source_target_pairs={{0,4},{4,8},{8,12},{12,16},{16,20},{20,24},{24,28},{28,32},{32,36}... | collective-permute-start | bytes 24584 | tf_op jit(solution)/shard_map/ppermute | solution.py:43
  108.4 6.2 %collective-permute-start.5 = (f32[128,16,1]{0,2,1:T(1,128)S(1)}, f32[128,16,1]{0,2,1:T(1,128)S(1)}, u32[]{:S(2)}, u32[]{:S(2)}) collective-permute-start(f32[128,16,1]{0,2,1:T(1,128)S(1)} %get-tuple-element.33), channel_id=1, source_target_pairs={{4,0},{8,4},{12,8},{16,12},{20,16},{24,20},{28,24},{32,28},{36,32}... | collective-permute-start | bytes 24584 | tf_op jit(solution)/shard_map/ppermute | solution.py:46
  116.5 2.3 %reshape.185 = f32[128,1,432]{2,1,0:T(1,128)} reshape(f32[1152,3,16]{2,1,0:T(4,128)S(1)} %bitcast.81) | data formatting | bytes 442368
  118.8 6.0 %all-to-all-start.1 = ((f32[128,1,432]{2,1,0:T(1,128)}), f32[128,1,432]{2,1,0:T(1,128)S(1)}, u32[]{:S(2)}, u32[]{:S(2)}) async-start(f32[128,1,432]{2,1,0:T(1,128)} %reshape.185), calls=%async_computation.1 | async-start | bytes 524288 | tf_op jit(solution)/shard_map/all_to_all | solution.py:155
  124.9 18.8 %collective-permute-start.6 = (f32[128,1,5]{0,2,1:T(8,128)S(1)}, f32[128,1,5]{0,2,1:T(8,128)S(1)}, u32[]{:S(2)}, u32[]{:S(2)}) collective-permute-start(f32[128,1,5]{0,2,1:T(8,128)S(1)} %get-tuple-element.28), channel_id=1, source_target_pairs={{0,1},{1,2},{2,3},{4,5},{5,6},{6,7},{8,9},{9,10},{10,11},{12,13},{... | collective-permute-start | bytes 7688 | tf_op jit(solution)/shard_map/ppermute | solution.py:43
  143.7 1.9 %collective-permute-start.7 = (f32[128,1,5]{0,2,1:T(8,128)S(1)}, f32[128,1,5]{0,2,1:T(8,128)S(1)}, u32[]{:S(2)}, u32[]{:S(2)}) collective-permute-start(f32[128,1,5]{0,2,1:T(8,128)S(1)} %get-tuple-element.29), channel_id=1, source_target_pairs={{1,0},{2,1},{3,2},{5,4},{6,5},{7,6},{9,8},{10,9},{11,10},{13,12},{... | collective-permute-start | bytes 7688 | tf_op jit(solution)/shard_map/ppermute | solution.py:46
  146.2 4.2 %collective-permute-done.7 = f32[128,1,5]{0,2,1:T(8,128)S(1)} collective-permute-done((f32[128,1,5]{0,2,1:T(8,128)S(1)}, f32[128,1,5]{0,2,1:T(8,128)S(1)}, u32[]{:S(2)}, u32[]{:S(2)}) %collective-permute-start.7) | collective-permute-done | bytes 2592 | tf_op jit(solution)/shard_map/ppermute | solution.py:46
  152.0 2.3 %select_add_fusion = f32[2,64,6,32]{1,0,3,2:T(2,128)S(1)} fusion(f32[2,64,6,32]{1,0,3,2:T(2,128)S(1)} %reshape.178, f32[2,64,6,32]{1,0,3,2:T(2,128)S(1)} %reshape.176, f32[2,64,6,32]{1,0,3,2:T(2,128)S(1)} %reshape.174, f32[2,64,6,32]{1,0,3,2:T(2,128)S(1)} %reshape.172, f32[2,64,6,32]{1,0,3,2:T(2,128)S(1)} %reshape.170, f32[2,64,6,32]{1,0,3,2:T(2,128)S(1)} %reshape.168, ...), kind=kLoop, calls=%fused_computation.83 | loop fusion | flops 417792 | bytes 984768 | tf_op jit(solution)/shard_map/add | solution.py:113
  156.4 2.2 %reshape.186 = f32[1152,3,16]{2,1,0:T(4,128)} reshape(f32[128,432]{1,0:T(8,128)S(1)} %reduce.1) | data formatting | bytes 442368
  158.6 4.2 %copy.165 = f32[128,9,16,3]{1,0,2,3:T(8,128)S(1)} copy(f32[128,9,16,3]{2,3,1,0:T(4,128)} %bitcast.82) | data formatting | bytes 442368 | tf_op jit(solution)/shard_map/all_to_all | solution.py:155
  162.8 4.8 %copy.147 = f32[9,16,128,3]{1,3,2,0:T(4,128)} copy(f32[9,16,128,3]{0,2,1,3:T(8,128)S(1)} %bitcast.80) | data formatting | bytes 442368 | tf_op jit(solution)/shard_map/all_to_all | solution.py:155
  167.6 2.9 %all_to_all.30 = f32[9,16,384]{1,2,0:T(8,128)S(1)} reshape(f32[9,16,128,3]{1,3,2,0:T(4,128)} %copy.147) | data formatting | bytes 442368 | tf_op jit(solution)/shard_map/all_to_all | solution.py:155
  170.5 1.8 fusion.56
  173.5 2.0 %copy.149 = f32[9,2,384]{2,1,0:T(2,128)S(1)} copy(f32[9,2,384]{1,2,0:T(8,128)} %get-tuple-element.14) | data formatting | bytes 55296 | tf_op jit(solution)/shard_map/slice | solution.py:44
  175.5 7.2 %collective-permute-start.2 = (f32[9,2,384]{2,1,0:T(2,128)S(1)}, f32[9,2,384]{2,1,0:T(2,128)S(1)}, u32[]{:S(2)}, u32[]{:S(2)}) collective-permute-start(f32[9,2,384]{2,1,0:T(2,128)S(1)} %copy.149), channel_id=1, source_target_pairs={{0,1},{1,2},{2,3},{4,5},{5,6},{6,7},{8,9},{9,10},{10,11},{12,13},{... | collective-permute-start | bytes 82952 | tf_op jit(solution)/shard_map/ppermute | solution.py:43
  183.2 1.9 %collective-permute-start.3 = (f32[9,2,384]{2,1,0:T(2,128)S(1)}, f32[9,2,384]{2,1,0:T(2,128)S(1)}, u32[]{:S(2)}, u32[]{:S(2)}) collective-permute-start(f32[9,2,384]{2,1,0:T(2,128)S(1)} %copy.151), channel_id=1, source_target_pairs={{1,0},{2,1},{3,2},{5,4},{6,5},{7,6},{9,8},{10,9},{11,10},{13,12},{... | collective-permute-start | bytes 82952 | tf_op jit(solution)/shard_map/ppermute | solution.py:46
  185.5 4.4 %collective-permute-done.3 = f32[9,2,384]{2,1,0:T(2,128)S(1)} collective-permute-done((f32[9,2,384]{2,1,0:T(2,128)S(1)}, f32[9,2,384]{2,1,0:T(2,128)S(1)}, u32[]{:S(2)}, u32[]{:S(2)}) %collective-permute-start.3) | collective-permute-done | bytes 27680 | tf_op jit(solution)/shard_map/ppermute | solution.py:46
  (120 shorter events, 19.4 us)
Async XLA Ops:
  0.6 52.0 %copy-start.3 = (f32[9,16,384]{2,1,0:T(8,128)S(1)}, f32[9,16,384]{2,1,0:T(8,128)}, u32[]{:S(2)}) copy-start(f32[9,16,384]{2,1,0:T(8,128)} %param.6) | copy-start | bytes 663556
  1.4 51.1 %copy-start.4 = (f32[16,384]{1,0:T(8,128)}, f32[16,384]{1,0:T(8,128)S(1)}, u32[]{:S(2)}) copy-start(f32[16,384]{1,0:T(8,128)S(1)} %convert_element_type.11) | copy-start | bytes 73732
  2.4 49.9 %collective-permute-start = (f32[9,2,384]{2,1,0:T(2,128)S(1)}, f32[9,2,384]{2,1,0:T(2,128)S(1)}, u32[]{:S(2)}, u32[]{:S(2)}) collective-permute-start(f32[9,2,384]{2,1,0:T(2,128)S(1)} %get-tuple-element.18), channel_id=1, source_target_pairs={{0,1},{1,2},{2,3},{4,5},{5,6},{6,7},{8,9},{9,10},{10,11},{12,13},{... | collective-permute-start | bytes 82952 | tf_op jit(solution)/shard_map/ppermute | solution.py:43
  7.8 44.5 %collective-permute-start.1 = (f32[9,2,384]{2,1,0:T(2,128)S(1)}, f32[9,2,384]{2,1,0:T(2,128)S(1)}, u32[]{:S(2)}, u32[]{:S(2)}) collective-permute-start(f32[9,2,384]{2,1,0:T(2,128)S(1)} %get-tuple-element.19), channel_id=1, source_target_pairs={{1,0},{2,1},{3,2},{5,4},{6,5},{7,6},{9,8},{10,9},{11,10},{13,12},{... | collective-permute-start | bytes 82952 | tf_op jit(solution)/shard_map/ppermute | solution.py:46
  52.0 0.6 copy-start.6
  55.9 29.4 %all-to-all-start = ((f32[128,1,432]{2,1,0:T(1,128)}), f32[128,1,432]{2,1,0:T(1,128)S(1)}, u32[]{:S(2)}, u32[]{:S(2)}) async-start(f32[128,1,432]{2,1,0:T(1,128)} %reshape.183), calls=%async_computation | async-start | bytes 524288 | tf_op jit(solution)/shard_map/all_to_all | solution.py:134
  94.7 1.5 copy-start.9
  94.7 4.2 %copy-start.10 = (s32[1152]{0:T(1024)S(1)}, s32[1152]{0:T(1024)}, u32[]{:S(2)}) copy-start(s32[1152]{0:T(1024)} %param.9) | copy-start | bytes 13828
  98.9 6.7 %copy-start.1 = (f32[64,1152]{0,1:T(8,128)S(1)}, f32[64,1152]{0,1:T(8,128)}, u32[]{:S(2)}) copy-start(f32[64,1152]{0,1:T(8,128)} %get-tuple-element.16) | copy-start | bytes 884740
  98.9 6.7 %copy-start.2 = (f32[64,1152]{0,1:T(8,128)S(1)}, f32[64,1152]{0,1:T(8,128)}, u32[]{:S(2)}) copy-start(f32[64,1152]{0,1:T(8,128)} %get-tuple-element.17) | copy-start | bytes 884740
  101.7 12.9 %copy-start.8 = (s32[6,32]{1,0:T(8,128)S(1)}, s32[6,32]{1,0:T(8,128)}, u32[]{:S(2)}) copy-start(s32[6,32]{1,0:T(8,128)} %param.11) | copy-start | bytes 2308
  106.3 18.5 %collective-permute-start.4 = (f32[128,16,1]{0,2,1:T(1,128)S(1)}, f32[128,16,1]{0,2,1:T(1,128)S(1)}, u32[]{:S(2)}, u32[]{:S(2)}) collective-permute-start(f32[128,16,1]{0,2,1:T(1,128)S(1)} %get-tuple-element.32), channel_id=1, source_target_pairs={{0,4},{4,8},{8,12},{12,16},{16,20},{20,24},{24,28},{28,32},{32,36}... | collective-permute-start | bytes 24584 | tf_op jit(solution)/shard_map/ppermute | solution.py:43
  108.4 16.4 %collective-permute-start.5 = (f32[128,16,1]{0,2,1:T(1,128)S(1)}, f32[128,16,1]{0,2,1:T(1,128)S(1)}, u32[]{:S(2)}, u32[]{:S(2)}) collective-permute-start(f32[128,16,1]{0,2,1:T(1,128)S(1)} %get-tuple-element.33), channel_id=1, source_target_pairs={{4,0},{8,4},{12,8},{16,12},{20,16},{24,20},{28,24},{32,28},{36,32}... | collective-permute-start | bytes 24584 | tf_op jit(solution)/shard_map/ppermute | solution.py:46
  118.8 36.3 %all-to-all-start.1 = ((f32[128,1,432]{2,1,0:T(1,128)}), f32[128,1,432]{2,1,0:T(1,128)S(1)}, u32[]{:S(2)}, u32[]{:S(2)}) async-start(f32[128,1,432]{2,1,0:T(1,128)} %reshape.185), calls=%async_computation.1 | async-start | bytes 524288 | tf_op jit(solution)/shard_map/all_to_all | solution.py:155
  124.9 21.3 %collective-permute-start.6 = (f32[128,1,5]{0,2,1:T(8,128)S(1)}, f32[128,1,5]{0,2,1:T(8,128)S(1)}, u32[]{:S(2)}, u32[]{:S(2)}) collective-permute-start(f32[128,1,5]{0,2,1:T(8,128)S(1)} %get-tuple-element.28), channel_id=1, source_target_pairs={{0,1},{1,2},{2,3},{4,5},{5,6},{6,7},{8,9},{9,10},{10,11},{12,13},{... | collective-permute-start | bytes 7688 | tf_op jit(solution)/shard_map/ppermute | solution.py:43
  143.7 6.7 %collective-permute-start.7 = (f32[128,1,5]{0,2,1:T(8,128)S(1)}, f32[128,1,5]{0,2,1:T(8,128)S(1)}, u32[]{:S(2)}, u32[]{:S(2)}) collective-permute-start(f32[128,1,5]{0,2,1:T(8,128)S(1)} %get-tuple-element.29), channel_id=1, source_target_pairs={{1,0},{2,1},{3,2},{5,4},{6,5},{7,6},{9,8},{10,9},{11,10},{13,12},{... | collective-permute-start | bytes 7688 | tf_op jit(solution)/shard_map/ppermute | solution.py:46
  173.5 11.7 %copy-start = (f32[9,16,384]{2,1,0:T(8,128)S(1)}, f32[9,16,384]{2,1,0:T(8,128)}, u32[]{:S(2)}) copy-start(f32[9,16,384]{2,1,0:T(8,128)} %copy.153) | copy-start | bytes 663556
  173.5 11.7 %copy-start.7 = (f32[16,385]{1,0:T(8,128)S(1)}, f32[16,385]{1,0:T(8,128)}, u32[]{:S(2)}) copy-start(f32[16,385]{1,0:T(8,128)} %copy-done.6) | copy-start | bytes 73924
  173.5 16.7 %copy-start.5 = (f32[16,384]{1,0:T(8,128)S(1)}, f32[16,384]{1,0:T(8,128)}, u32[]{:S(2)}) copy-start(f32[16,384]{1,0:T(8,128)} %copy-done.4) | copy-start | bytes 73732
  175.5 10.0 %collective-permute-start.2 = (f32[9,2,384]{2,1,0:T(2,128)S(1)}, f32[9,2,384]{2,1,0:T(2,128)S(1)}, u32[]{:S(2)}, u32[]{:S(2)}) collective-permute-start(f32[9,2,384]{2,1,0:T(2,128)S(1)} %copy.149), channel_id=1, source_target_pairs={{0,1},{1,2},{2,3},{4,5},{5,6},{6,7},{8,9},{9,10},{10,11},{12,13},{... | collective-permute-start | bytes 82952 | tf_op jit(solution)/shard_map/ppermute | solution.py:43
  183.2 6.7 %collective-permute-start.3 = (f32[9,2,384]{2,1,0:T(2,128)S(1)}, f32[9,2,384]{2,1,0:T(2,128)S(1)}, u32[]{:S(2)}, u32[]{:S(2)}) collective-permute-start(f32[9,2,384]{2,1,0:T(2,128)S(1)} %copy.151), channel_id=1, source_target_pairs={{1,0},{2,1},{3,2},{5,4},{6,5},{7,6},{9,8},{10,9},{11,10},{13,12},{... | collective-permute-start | bytes 82952 | tf_op jit(solution)/shard_map/ppermute | solution.py:46
where the time goes:
time: 192 us; the launch traced here: 191 us
  starting transfers between devices  63.1 us (33%)
  local copies, waits for them, and re-layouts  41 us (21%)
  blocking collectives  40.3 us (21%)
  waiting for transfers between devices  24.6 us (13%)
  other arithmetic  10.6 us (6%)
  matrix products  9.96 us (5%)
    all_gather x3, blocking collectives, gather_in_order(): blocks = lax.all_gather(blocks, axes[k], axis=0, tiled=True)  40.3 us
    ppermute x4, starting transfers between devices, extended(): lax.ppermute(lax.slice_in_dim(block, block.shape[dim] - width, None, axis...  33.5 us
    all_to_all x1, waiting for transfers between devices, on_device(): lax.all_to_all(after_first, BINS, split_axis=2, concat_axis=0, tiled=True)  16 us
    all_to_all x4, local copies, waits for them, and re-layouts, on_device(): lax.all_to_all(middle, BINS, split_axis=0, concat_axis=2, tiled=True)  13.1 us
    ppermute x4, starting transfers between devices, extended(): lax.ppermute(lax.slice_in_dim(block, 0, width, axis=dim), axis, backward)  12 us
    all_to_all x1, starting transfers between devices, on_device(): lax.all_to_all(after_first, BINS, split_axis=2, concat_axis=0, tiled=True)  11.6 us
    ppermute x4, waiting for transfers between devices, extended(): lax.ppermute(lax.slice_in_dim(block, 0, width, axis=dim), axis, backward)  8.66 us
    unnamed x27, local copies, waits for them, and re-layouts  8.04 us
  transfers between devices with their start and end apart: 10, of which 3 were waited for; matrix products, arithmetic and copies ran while one was open for 7% of the time, Pallas kernels for 0%

commit v1 on v0

v1 whole, which is shorter than its diff:
```python
import math

import jax
import jax.numpy as jnp
import numpy as np
from jax import lax
from jax.experimental import pallas as pl
from jax.experimental.pallas import tpu as pltpu
from jax.sharding import PartitionSpec as P

NDIR = 36
NFREQ = 32
LEV = 64
BINS = NDIR * NFREQ
OWN = 9
ROWS = 16
NLON = 384
OWNERS = 128
COLS = 3
F32 = jnp.float32
BF16 = jnp.bfloat16
HIGHEST = lax.Precision.HIGHEST

GROUP_COLUMNS = (0, 1, 2, -2, -1, 3, 4)


def bin_values():
    j = np.arange(NFREQ, dtype=np.float64)
    angles = 2.0 * math.pi * (np.arange(NDIR) + 0.5) / NDIR
    speeds = np.repeat(0.12 + 0.25 * (NFREQ - 1 - j) / (NFREQ - 1), NDIR)
    cosines, sines = np.tile(np.cos(angles), NFREQ), np.tile(np.sin(angles), NFREQ)
    strength = np.repeat(0.06 * (1.0 + j / (NFREQ - 1)), NDIR)
    levels = np.arange(LEV) + 0.5
    decay = np.repeat(np.exp(-levels[:, None] * (0.02 * 1.15**j)[None, :]), NDIR, axis=1)
    drift = 2.0 / math.sqrt(BINS) * np.concatenate([decay * cosines, decay * sines], axis=0)
    return speeds * cosines, speeds * sines, strength, drift


def stencils():
    lane = {}
    for group, column in enumerate(GROUP_COLUMNS):
        for r in range(ROWS):
            lane[column, r] = 16 * group + r
    for column in range(COLS):
        for k, r in enumerate((-2, -1, 16, 17)):
            lane[column, r] = 112 + 4 * column + k
    table = np.zeros((128, 256), np.float32)
    for r in range(ROWS):
        for face in range(COLS + 1):
            at = 16 * face + r
            for d, w in ((-2, -1), (-1, 5), (0, 2)):
                table[lane[face + d, r], at] += w
            for d, w in ((-1, 2), (0, 5), (1, -1)):
                table[lane[face + d, r], 128 + at] += w
        for column in range(COLS):
            at = 64 + 16 * column + r
            for d, w in ((-2, 1), (-1, -6), (0, 3), (1, 2)):
                table[lane[column, r + d], at] += w
            for d, w in ((-1, -2), (0, -3), (1, 6), (2, -1)):
                table[lane[column, r + d], 128 + at] += w
    return table


def lanes(rows=1):
    return lax.broadcasted_iota(jnp.int32, (rows, 128), 1)


def split_beside(x):
    upper = x.astype(BF16).astype(F32)
    return (upper + pltpu.roll(x - upper, 64, 1)).astype(BF16)


def pack_kernel(spec, mask, low, high, current, out, mask_out, zonal_out, stack, turned, turned2):
    sea = mask[...].astype(F32)
    masked = spec[...] * sea[None]
    stack[...] = jnp.zeros_like(stack)
    stack[0:16, :] = masked[8]
    stack[16:32, :] = sea
    for i in range(OWN):
        stack[32 + 4 * i : 34 + 4 * i, :] = low[2 * i : 2 * i + 2, :]
        stack[34 + 4 * i : 36 + 4 * i, :] = high[2 * i : 2 * i + 2, :]
    for ref in (turned, turned2):
        ref[0:8, :] = jnp.zeros((8, 128), F32)
        ref[392:400, :] = jnp.zeros((8, 128), F32)
    turned[8:392, :] = masked[0:8].reshape(128, NLON).T
    turned2[8:392, :] = stack[...].T

    pair = lax.broadcasted_iota(jnp.int32, (32, 128), 0) // 2
    means = jnp.where(pair == lax.broadcasted_iota(jnp.int32, (32, 128), 1) % 16, 0.25, 0.0)
    sums = jnp.dot(current[...], means, precision=HIGHEST, preferred_element_type=F32)
    zonal = [sums[2 * c : 2 * c + 1] + sums[2 * c + 1 : 2 * c + 2] for c in range(COLS)]
    zonal_out[...] = jnp.concatenate(zonal + [jnp.zeros((5, 128), F32)], axis=0)

    lane = lanes(OWNERS)
    group = lane // 16

    def column(ref, offset):
        return ref[pl.ds(8 + offset, OWNERS, stride=COLS), :]

    for i in range(OWN):
        source, at = (turned, 16 * i) if i < 8 else (turned2, 0)
        acc = jnp.zeros((OWNERS, 128), F32)
        for g, offset in enumerate(GROUP_COLUMNS):
            acc = jnp.where(group == g, pltpu.roll(column(source, offset), (16 * g - at) % 128, 1), acc)
        for c in range(COLS):
            beyond = pltpu.roll(column(turned2, c), (80 + 4 * c - 4 * i) % 128, 1)
            acc = jnp.where((lane >= 112 + 4 * c) & (lane < 116 + 4 * c), beyond, acc)
        if i < 8:
            flow = pltpu.roll(zonal[0] if i < 4 else zonal[2], (124 - 4 * (i % 4)) % 128, 1)
            acc = jnp.where(lane >= 124, jnp.broadcast_to(flow, acc.shape), acc)
        out[pl.ds(i, OWNERS, stride=OWN), :] = acc
    acc = jnp.zeros((OWNERS, 128), F32)
    for c in range(COLS):
        acc = jnp.where(group == c, pltpu.roll(column(turned2, c), (16 * c - 16) % 128, 1), acc)
    mask_out[...] = acc


def points_kernel(
    me, arrived, masks, zonal, plus, minus, speeds, stencil, table,
    out, drift_out, first, source, middle, halves, plus_col, minus_col,
):
    device = me[0]
    lane1 = lanes()
    below = jnp.zeros((1, 128), F32)
    above = jnp.zeros((1, 128), F32)
    left = jnp.maximum(device - 1, 0) * OWN + 4
    right = jnp.minimum(device + 1, OWNERS - 1) * OWN
    for k in range(4):
        here = (lane1 >= 4 * k) & (lane1 < 4 * k + 4)
        below = jnp.where(here, pltpu.roll(arrived[pl.ds(left + k, 1), :], 4 + 4 * k, 1), below)
        above = jnp.where(here, pltpu.roll(arrived[pl.ds(right + k, 1), :], 4 + 4 * k, 1), above)
    below = jnp.where(device > 0, below, 0.0)
    above = pltpu.roll(jnp.where(device < OWNERS - 1, above, 0.0), 48, 1)
    group1 = lane1 // 16
    columns = [zonal[c : c + 1, :] for c in range(COLS)]
    lower = below
    upper = above
    for c in range(COLS):
        lower = jnp.where(group1 == c + 1, columns[c], lower)
        upper = jnp.where(group1 == c, columns[c], upper)
    faces = jnp.where(lane1 < 64, 0.5 * (lower + upper), 0.0)
    sea = masks[pl.ds(device, 1), :]

    def chunk(t):
        return slice(128 * t, 128 * t + 128)

    for t in range(OWN):
        value = arrived[chunk(t), :]
        upper_half = value.astype(BF16)
        lower_half = (value - upper_half.astype(F32)).astype(BF16)
        sums = jnp.dot(upper_half, stencil[...], preferred_element_type=F32) + jnp.dot(
            lower_half, stencil[...], preferred_element_type=F32
        )
        speed = (speeds[chunk(t), :] + faces) * (1.0 / 6.0)
        flux = jnp.maximum(speed, 0.0) * sums[:, 0:128] + jnp.minimum(speed, 0.0) * sums[:, 128:256]
        change = (pltpu.roll(flux, 112, 1) - flux) + pltpu.roll(flux, 64, 1)
        moved = sea * (value - change)
        moved = jnp.where(lanes(128) < 48, moved, 0.0)
        first[chunk(t), :] = moved
        halves[chunk(t), :] = split_beside(moved)
        for row, col in ((plus, plus_col), (minus, minus_col)):
            part = jnp.broadcast_to(row[:, chunk(t)].astype(F32), (128, 128))
            col[chunk(t), :] = part.T

    numbers = lax.broadcasted_iota(jnp.int32, (128, BINS), 1).astype(F32)

    def gathered(col, t):
        wide = jnp.concatenate([col[chunk(t), :]] * OWN, axis=1)
        chosen = jnp.where(wide == numbers, 1.0, 0.0).astype(BF16)
        both = jnp.dot(chosen, halves[...], preferred_element_type=F32)
        return both + pltpu.roll(both, 64, 1)

    for t in range(OWN):
        ahead = gathered(plus_col, t)
        behind = gathered(minus_col, t)
        f = first[chunk(t), :]
        strength = jnp.broadcast_to(speeds[chunk(t), 127:128], (128, 128))
        source[chunk(t), :] = strength * (f * f * (ahead + behind) - 2.0 * f * ahead * behind)
    for t in range(OWN):
        halves[chunk(t), :] = split_beside(source[chunk(t), :])
    for t in range(OWN):
        names = lax.broadcasted_iota(jnp.int32, (128, BINS), 0) + 128 * t
        hits = jnp.where(plus[...] == names, 1.0, 0.0) + jnp.where(minus[...] == names, 1.0, 0.0)
        both = jnp.dot(hits.astype(BF16), halves[...], preferred_element_type=F32)
        back = both + pltpu.roll(both, 64, 1)
        m = first[chunk(t), :] + (source[chunk(t), :] - 0.5 * back)
        middle[chunk(t), :] = jnp.where(lanes(128) < 48, m, 0.0)
    for t in range(OWN):
        halves[chunk(t), :] = split_beside(middle[chunk(t), :])
    sums = jnp.dot(table[...], halves[...], preferred_element_type=F32)
    drift = sums[0:128] + pltpu.roll(sums[0:128], 64, 1) + sums[128:256]
    drift_out[...] = drift.T[0:48]

    group = lanes(OWNERS) // 16
    for c in range(COLS):
        acc = jnp.zeros((OWNERS, 128), F32)
        for i in range(8):
            part = pltpu.roll(middle[pl.ds(i, OWNERS, stride=OWN), :], (16 * (i - c)) % 128, 1)
            acc = jnp.where(group == i, part, acc)
        out[pl.ds(c, OWNERS, stride=4), :] = acc
    acc = jnp.zeros((OWNERS, 128), F32)
    last = middle[pl.ds(8, OWNERS, stride=OWN), :]
    for c in range(COLS):
        acc = jnp.where(group == 2 * c, pltpu.roll(last, 16 * c, 1), acc)
        acc = jnp.where(group == 2 * c + 1, jnp.broadcast_to(columns[c], acc.shape), acc)
    out[pl.ds(3, OWNERS, stride=4), :] = acc


def unpack_kernel(arrived, drift, drift_low, drift_high, middle, zonal, low, high, turned, turned2):
    for c in range(COLS):
        turned[pl.ds(c, OWNERS, stride=COLS), :] = arrived[pl.ds(c, OWNERS, stride=4), :]
        rest = arrived[pl.ds(3, OWNERS, stride=4), :]
        turned2[pl.ds(c, OWNERS, stride=COLS), :] = pltpu.roll(rest, (128 - 32 * c) % 128, 1)
    middle[0:128, :] = turned[...].T
    rest = turned2[...].T
    middle[128:144, :] = rest[0:16]
    zonal[...] = rest[16:32]
    for i in range(OWN):
        low[2 * i : 2 * i + 2, :] = middle[16 * i : 16 * i + 2, :]
        high[2 * i : 2 * i + 2, :] = middle[16 * i + 14 : 16 * i + 16, :]
    for ref, r in ((low, 0), (high, 15)):
        pieces = [drift_low[r : r + 1, :]] + [drift[16 * c + r : 16 * c + r + 1, :] for c in range(COLS)]
        pieces += [drift_high[r : r + 1, :], jnp.zeros((1, 128), F32)]
        ref[18:19, :] = jnp.concatenate(pieces[0:3], axis=1)
        ref[19:20, :] = jnp.concatenate(pieces[3:6], axis=1)
        ref[20:24, :] = jnp.zeros((4, NLON), F32)


def final_kernel(
    me, speeds, middle, zonal, low, high, mask, drift, drift_low, drift_high, place, out, stokes, rows, near
):
    first_bin = me[0] * OWN
    sea = mask[...].astype(F32)
    column = lax.broadcasted_iota(jnp.int32, (ROWS, NLON), 1)

    def beside(x, d):
        moved = pltpu.roll(x, (-d) % NLON, 1)
        return jnp.where((column + d >= 0) & (column + d < NLON), moved, 0.0)

    flow = zonal[...]
    lower_flow = 0.5 * (beside(flow, -1) + flow)
    upper_flow = 0.5 * (flow + beside(flow, 1))
    for i in range(OWN):
        f = middle[16 * i : 16 * i + 16, :]
        rows[8:24, :] = f
        rows[6:8, :] = low[2 * i : 2 * i + 2, :]
        rows[24:26, :] = high[2 * i : 2 * i + 2, :]
        along_x = speeds[first_bin + i]
        along_y = speeds[BINS + first_bin + i]
        r2, r1, u1, u2 = rows[6:22, :], rows[7:23, :], rows[9:25, :], rows[10:26, :]
        forward = jnp.maximum(along_y, 0.0) * (1.0 / 6.0)
        backward = jnp.minimum(along_y, 0.0) * (1.0 / 6.0)
        change = forward * ((r2 - 6.0 * r1) + (3.0 * f + 2.0 * u1)) + backward * (
            (6.0 * u1 - u2) - (2.0 * r1 + 3.0 * f)
        )
        a2, a1, b1, b2 = beside(f, -2), beside(f, -1), beside(f, 1), beside(f, 2)
        speed = (along_x + upper_flow) * (1.0 / 6.0)
        change = change + (
            jnp.maximum(speed, 0.0) * (5.0 * f + 2.0 * b1 - a1) + jnp.minimum(speed, 0.0) * (2.0 * f + 5.0 * b1 - b2)
        )
        speed = (along_x + lower_flow) * (1.0 / 6.0)
        change = change - (
            jnp.maximum(speed, 0.0) * (5.0 * a1 + 2.0 * f - a2) + jnp.minimum(speed, 0.0) * (2.0 * a1 + 5.0 * f - b1)
        )
        out[i] = sea * (f - change)

    near[...] = jnp.zeros_like(near)
    near[0:16, :] = drift_low[...]
    near[16:64, :] = drift[...]
    near[64:80, :] = drift_high[...]
    for ref, at in ((low, 80), (high, 88)):
        for k in range(5):
            near[at + k : at + k + 1, :] = ref[18 + k // 3 : 19 + k // 3, 128 * (k % 3) : 128 * (k % 3) + 128]
    wanted = jnp.broadcast_to(place[...], (128, 256)).T[0:192]
    chosen = jnp.where(wanted == lanes(192).astype(F32), 1.0, 0.0).astype(BF16)
    rest = near[...]
    total = jnp.zeros((192, 128), F32)
    for _ in range(3):
        part = rest.astype(BF16)
        rest = rest - part.astype(F32)
        total = total + jnp.dot(chosen, part, preferred_element_type=F32)
    stokes[0] = total[:, 0:64]
    stokes[1] = total[:, 64:128]


def shapes(*sizes):
    return [jax.ShapeDtypeStruct(size, F32) for size in sizes]


def on_device(spectrum, sea_mask, current, partner_plus, partner_minus, source_map):
    along_x, along_y, strength, drift_table = bin_values()
    speeds = np.zeros((BINS, 128), np.float32)
    speeds[:, 0:64] = along_x[:, None]
    speeds[:, 64:112] = along_y[:, None]
    speeds[:, 127] = strength
    speed_list = np.concatenate([along_x, along_y]).astype(np.float32)
    drift_upper = drift_table.astype(np.float32).astype(BF16)
    drift_lower = (drift_table.astype(np.float32) - drift_upper.astype(np.float32)).astype(BF16)
    table = np.concatenate([drift_upper, drift_lower], axis=0)
    stencil = stencils().astype(BF16)

    device = lax.axis_index("bins").reshape(1)
    bands = lax.axis_size("lat")
    up = [(i, i + 1) for i in range(bands - 1)]
    down = [(i + 1, i) for i in range(bands - 1)]
    east = [(i, i + 1) for i in range(OWNERS - 1)]
    west = [(i + 1, i) for i in range(OWNERS - 1)]

    def edge(start):
        rows = spectrum[:, start : start + 2] * sea_mask[None, start : start + 2].astype(F32)
        return rows.reshape(2 * OWN, NLON)

    from_below = lax.ppermute(edge(14), "lat", up)
    from_above = lax.ppermute(edge(0), "lat", down)

    smem = pl.BlockSpec(memory_space=pltpu.SMEM)
    vmem = pl.BlockSpec(memory_space=pltpu.VMEM)
    sent, masks, zonal = pl.pallas_call(
        pack_kernel,
        out_shape=shapes((BINS, 128), (OWNERS, 128), (8, 128)),
        scratch_shapes=[pltpu.VMEM((128, NLON), F32), pltpu.VMEM((400, 128), F32), pltpu.VMEM((400, 128), F32)],
    )(spectrum, sea_mask, from_below, from_above, current)

    arrived = lax.all_to_all(sent.reshape(OWNERS, 1, OWN * 128), "bins", 0, 0).reshape(BINS, 128)

    big = pltpu.VMEM((BINS, 128), F32)
    sent, drift = pl.pallas_call(
        points_kernel,
        out_shape=shapes((4 * OWNERS, 128), (48, 128)),
        in_specs=[smem] + [vmem] * 8,
        scratch_shapes=[big, big, big, pltpu.VMEM((BINS, 128), BF16), big, big],
        compiler_params=pltpu.CompilerParams(vmem_limit_bytes=40 * 1024 * 1024),
    )(
        device, arrived, masks, zonal, partner_plus.reshape(1, BINS), partner_minus.reshape(1, BINS),
        jnp.asarray(speeds), jnp.asarray(stencil), jnp.asarray(table),
    )

    arrived = lax.all_to_all(sent.reshape(OWNERS, 1, 512), "bins", 0, 0).reshape(4 * OWNERS, 128)
    drift_low = lax.ppermute(drift[32:48], "bins", east)
    drift_high = lax.ppermute(drift[0:16], "bins", west)

    middle, zonal_all, low, high = pl.pallas_call(
        unpack_kernel,
        out_shape=shapes((OWN * ROWS, NLON), (ROWS, NLON), (24, NLON), (24, NLON)),
        scratch_shapes=[pltpu.VMEM((NLON, 128), F32), pltpu.VMEM((NLON, 128), F32)],
    )(arrived, drift, drift_low, drift_high)
    from_below = lax.ppermute(high, "lat", up)
    from_above = lax.ppermute(low, "lat", down)

    row = jnp.arange(32, dtype=jnp.int32)[None, :] // 2 + source_map // 3 - 1
    col = jnp.arange(6, dtype=jnp.int32)[:, None] // 2 + source_map % 3
    place = jnp.where(row < 0, 80 + col, jnp.where(row > 15, 88 + col, 16 * col + row))
    place = jnp.pad(place.reshape(1, 192), ((0, 0), (0, 64))).astype(F32)
    second, stokes = pl.pallas_call(
        final_kernel,
        out_shape=shapes((OWN, ROWS, NLON), (2, 192, 64)),
        in_specs=[smem, smem] + [vmem] * 9,
        scratch_shapes=[pltpu.VMEM((32, NLON), F32), pltpu.VMEM((128, 128), F32)],
    )(
        device, jnp.asarray(speed_list), middle, zonal_all, from_below, from_above, sea_mask,
        drift, drift_low, drift_high, place,
    )
    return second, stokes.reshape(2, 6, 32, LEV).transpose(0, 3, 1, 2)


def solution(mesh):
    in_specs = (P("bins", "lat", None), P("lat", None), P("bins", "lat"), P(), P(), P("bins", "lat"))
    out_specs = (P("bins", "lat", None), P(None, None, "bins", "lat"))
    return jax.shard_map(on_device, mesh=mesh, in_specs=in_specs, out_specs=out_specs, check_vma=False)
```

time: 192 us -> 122 us (0.64)
  the two profiles are of different devices: /device:TPU:33 before, /device:TPU:9 now
where the time goes in v1:
time: 122 us; the launch traced here: 121 us
  waiting for transfers between devices  56.6 us (46%)
  starting transfers between devices  44.3 us (36%)
  Pallas kernels  13.2 us (11%)
  local copies, waits for them, and re-layouts  3.58 us (3%)
  other arithmetic  2.38 us (2%)
    all_to_all x1, waiting for transfers between devices, on_device(): lax.all_to_all(sent.reshape(OWNERS, 1, OWN * 128), 'bins', 0, 0)  32.9 us
    all_to_all x1, starting transfers between devices, on_device(): lax.all_to_all(sent.reshape(OWNERS, 1, OWN * 128), 'bins', 0, 0)  19.9 us
    all_to_all x1, waiting for transfers between devices, on_device(): lax.all_to_all(sent.reshape(OWNERS, 1, 512), 'bins', 0, 0)  14.2 us
    all_to_all x1, starting transfers between devices, on_device(): lax.all_to_all(sent.reshape(OWNERS, 1, 512), 'bins', 0, 0)  6.28 us
    pallas_call x1, Pallas kernels, on_device(): pl.pallas_call(points_kernel, out_shape=shapes((4 * OWNERS, 128), (48, 12...  5.28 us
    ppermute x1, waiting for transfers between devices, on_device(): from_above = lax.ppermute(edge(0), 'lat', down)  4.83 us
    ppermute x1, starting transfers between devices, on_device(): from_below = lax.ppermute(edge(14), 'lat', up)  4.48 us
    ppermute x1, starting transfers between devices, on_device(): drift_high = lax.ppermute(drift[0:16], 'bins', west)  4.3 us
  transfers between devices with their start and end apart: 8, of which 5 were waited for; matrix products, arithmetic and copies ran while one was open for 1% of the time, Pallas kernels for 0%

profile of v1, /device:TPU:9, one launch (start us, length us, event | category | flops | bytes accessed | tf_op | source)
XLA Modules:
  0.0 120.9 jit_solution(12184372695443137449)
XLA Ops:
  0.6 0.7 slice_convert_fusion
  1.4 1.0 slice_multiply_fusion
  2.4 4.5 %collective-permute-start = (f32[18,384]{1,0:T(8,128)S(1)}, f32[18,384]{1,0:T(8,128)S(1)}, u32[]{:S(2)}, u32[]{:S(2)}) collective-permute-start(f32[18,384]{1,0:T(8,128)S(1)} %reshape.116), channel_id=1, source_target_pairs={{0,1},{1,2},{2,3},{4,5},{5,6},{6,7},{8,9},{9,10},{10,11},{12,13},{... | collective-permute-start | bytes 82952 | tf_op jit(solution)/shard_map/ppermute | solution.py:313
  6.9 1.9 %collective-permute-start.1 = (f32[18,384]{1,0:T(8,128)S(1)}, f32[18,384]{1,0:T(8,128)S(1)}, u32[]{:S(2)}, u32[]{:S(2)}) collective-permute-start(f32[18,384]{1,0:T(8,128)S(1)} %reshape.117), channel_id=1, source_target_pairs={{1,0},{2,1},{3,2},{5,4},{6,5},{7,6},{9,8},{10,9},{11,10},{13,12},{... | collective-permute-start | bytes 82952 | tf_op jit(solution)/shard_map/ppermute | solution.py:314
  8.8 0.0 collective-permute-done.low
  8.8 0.0 copy-start.9
  8.8 4.8 %collective-permute-done.1.high = f32[18,384]{1,0:T(8,128)S(1)} collective-permute-done((f32[18,384]{1,0:T(8,128)S(1)}, f32[18,384]{1,0:T(8,128)S(1)}, u32[]{:S(2)}, u32[]{:S(2)}) %collective-permute-start.1) | collective-permute-done | bytes 27680 | tf_op jit(solution)/shard_map/ppermute | solution.py:314
  13.7 0.6 copy-done.10
  14.3 3.5 %shard_map.113 = (f32[1152,128]{1,0:T(8,128)}, f32[128,128]{1,0:T(8,128)}, f32[8,128]{1,0:T(8,128)}) custom-call(f32[9,16,384]{2,1,0:T(8,128)} %spec.1, s32[16,384]{1,0:T(8,128)} %mask.3, f32[18,384]{1,0:T(8,128)} %copy-done.9, f32[18,384]{1,0:T(8,128)} %copy-done.10, f32[6,32]{1,0:T(8,128)} %current.1), custom_call_target="tpu_custom_call" | custom-call | tf_op jit(solution)/shard_map/pallas_call | solution.py:318
  17.8 19.9 %all-to-all-start = ((f32[128,1,1152]{2,1,0:T(1,128)}), f32[128,1,1152]{2,1,0:T(1,128)S(1)}, u32[]{:S(2)}, u32[]{:S(2)}) async-start(f32[128,1,1152]{2,1,0:T(1,128)} %bitcast.10), calls=%async_computation | async-start | bytes 1179648 | tf_op jit(solution)/shard_map/all_to_all | solution.py:324
  37.7 0.0 copy-start.14
  37.8 0.7 copy-done.14
  38.5 32.9 %all-to-all-done = f32[128,1,1152]{2,1,0:T(1,128)S(1)} async-done(((f32[128,1,1152]{2,1,0:T(1,128)}), f32[128,1,1152]{2,1,0:T(1,128)S(1)}, u32[]{:S(2)}, u32[]{:S(2)}) %all-to-all-start) | async-done | bytes 589856 | tf_op jit(solution)/shard_map/all_to_all | solution.py:324
  71.4 0.0 copy-start.4
  71.4 0.8 copy-done.4
  72.2 5.3 %shard_map.114 = (f32[512,128]{1,0:T(8,128)}, f32[48,128]{1,0:T(8,128)S(1)}) custom-call(s32[1]{0:T(128)} %bitcast.me, f32[1152,128]{1,0:T(8,128)S(1)} %bitcast.8, f32[128,128]{1,0:T(8,128)S(1)} %copy-done.4, f32[8,128]{1,0:T(8,128)S(1)} %copy-done.5, s32[1,1152]{1,0:T(1,128)S(1)} %reshape.120.plus, s32[1,1152]{1,0:T(1,128)S(1)} %reshape.121.minus, ...), custom_call_target="tpu_custom_call" | custom-call | tf_op jit(solution)/shard_map/pallas_call | solution.py:327
  77.5 6.3 %all-to-all-start.1 = ((f32[128,1,512]{2,1,0:T(1,128)}), f32[128,1,512]{2,1,0:T(1,128)S(1)}, u32[]{:S(2)}, u32[]{:S(2)}) async-start(f32[128,1,512]{2,1,0:T(1,128)} %bitcast.3), calls=%async_computation.1 | async-start | bytes 524288 | tf_op jit(solution)/shard_map/all_to_all | solution.py:338
  83.8 0.0 copy-start.15
  83.9 3.1 %collective-permute-start.2 = (f32[16,128]{1,0:T(8,128)S(1)}, f32[16,128]{1,0:T(8,128)S(1)}, u32[]{:S(2)}, u32[]{:S(2)}) collective-permute-start(f32[16,128]{1,0:T(8,128)S(1)} %get-tuple-element.27), channel_id=1, source_target_pairs={{0,4},{4,8},{8,12},{12,16},{16,20},{20,24},{24,28},{28,32},{32,36}... | collective-permute-start | bytes 24584 | tf_op jit(solution)/shard_map/ppermute | solution.py:339
  87.0 4.3 %collective-permute-start.3 = (f32[16,128]{1,0:T(8,128)S(1)}, f32[16,128]{1,0:T(8,128)S(1)}, u32[]{:S(2)}, u32[]{:S(2)}) collective-permute-start(f32[16,128]{1,0:T(8,128)S(1)} %get-tuple-element.26), channel_id=1, source_target_pairs={{4,0},{8,4},{12,8},{16,12},{20,16},{24,20},{28,24},{32,28},{36,32}... | collective-permute-start | bytes 24584 | tf_op jit(solution)/shard_map/ppermute | solution.py:340
  91.3 0.1 select_select_fusion
  91.4 0.1 reshape.124
  91.4 0.6 collective-permute-done.3.drift_high
  92.1 14.2 %all-to-all-done.1 = f32[128,1,512]{2,1,0:T(1,128)S(1)} async-done(((f32[128,1,512]{2,1,0:T(1,128)}), f32[128,1,512]{2,1,0:T(1,128)S(1)}, u32[]{:S(2)}, u32[]{:S(2)}) %all-to-all-start.1) | async-done | bytes 262176 | tf_op jit(solution)/shard_map/all_to_all | solution.py:338
  106.3 0.7 copy-done.6
  107.0 1.9 %shard_map.115 = (f32[144,384]{1,0:T(8,128)}, f32[16,384]{1,0:T(8,128)}, f32[24,384]{1,0:T(8,128)}, f32[24,384]{1,0:T(8,128)}) custom-call(f32[512,128]{1,0:T(8,128)} %bitcast.9, f32[48,128]{1,0:T(8,128)} %copy-done.2, f32[16,128]{1,0:T(8,128)} %copy-done.11, f32[16,128]{1,0:T(8,128)} %copy-done.12), custom_call_target="tpu_custom_call" | custom-call | tf_op jit(solution)/shard_map/pallas_call | solution.py:342
  108.9 1.9 %collective-permute-start.4 = (f32[24,384]{1,0:T(8,128)}, f32[24,384]{1,0:T(8,128)S(1)}, u32[]{:S(2)}, u32[]{:S(2)}) collective-permute-start(f32[24,384]{1,0:T(8,128)} %get-tuple-element.20), channel_id=1, source_target_pairs={{0,1},{1,2},{2,3},{4,5},{5,6},{6,7},{8,9},{9,10},{10,11},{12,13},{... | collective-permute-start | bytes 110600 | tf_op jit(solution)/shard_map/ppermute | solution.py:347
  110.8 2.4 %collective-permute-start.5 = (f32[24,384]{1,0:T(8,128)}, f32[24,384]{1,0:T(8,128)S(1)}, u32[]{:S(2)}, u32[]{:S(2)}) collective-permute-start(f32[24,384]{1,0:T(8,128)} %get-tuple-element.21), channel_id=1, source_target_pairs={{1,0},{2,1},{3,2},{5,4},{6,5},{7,6},{9,8},{10,9},{11,10},{13,12},{... | collective-permute-start | bytes 110600 | tf_op jit(solution)/shard_map/ppermute | solution.py:348
  113.2 0.6 pad_convert_fusion.place
  113.8 4.0 %collective-permute-done.5.high = f32[24,384]{1,0:T(8,128)S(1)} collective-permute-done((f32[24,384]{1,0:T(8,128)}, f32[24,384]{1,0:T(8,128)S(1)}, u32[]{:S(2)}, u32[]{:S(2)}) %collective-permute-start.5) | collective-permute-done | bytes 36896 | tf_op jit(solution)/shard_map/ppermute | solution.py:348
  117.8 0.6 copy-done.8
  118.4 2.5 %shard_map.116 = (f32[9,16,384]{2,1,0:T(8,128)}, f32[2,192,64]{2,1,0:T(8,128)}) custom-call(s32[1]{0:T(128)} %bitcast.me, f32[2304]{0:T(1024)} %constant.73.clone.speeds, f32[144,384]{1,0:T(8,128)} %get-tuple-element.18.middle, f32[16,384]{1,0:T(8,128)} %get-tuple-element.19.zonal, f32[24,384]{1,0:T(8,128)} %copy-done.7, f32[24,384]{1,0:T(8,128)} %copy-done.8, ...), custom_call_target="tpu_custom_call" | custom-call | tf_op jit(solution)/shard_map/pallas_call | solution.py:354
  (32 shorter events, 0.1 us)
Async XLA Ops:
  2.4 6.5 %collective-permute-start = (f32[18,384]{1,0:T(8,128)S(1)}, f32[18,384]{1,0:T(8,128)S(1)}, u32[]{:S(2)}, u32[]{:S(2)}) collective-permute-start(f32[18,384]{1,0:T(8,128)S(1)} %reshape.116), channel_id=1, source_target_pairs={{0,1},{1,2},{2,3},{4,5},{5,6},{6,7},{8,9},{9,10},{10,11},{12,13},{... | collective-permute-start | bytes 82952 | tf_op jit(solution)/shard_map/ppermute | solution.py:313
  6.9 6.8 %collective-permute-start.1 = (f32[18,384]{1,0:T(8,128)S(1)}, f32[18,384]{1,0:T(8,128)S(1)}, u32[]{:S(2)}, u32[]{:S(2)}) collective-permute-start(f32[18,384]{1,0:T(8,128)S(1)} %reshape.117), channel_id=1, source_target_pairs={{1,0},{2,1},{3,2},{5,4},{6,5},{7,6},{9,8},{10,9},{11,10},{13,12},{... | collective-permute-start | bytes 82952 | tf_op jit(solution)/shard_map/ppermute | solution.py:314
  8.8 4.8 %copy-start.9 = (f32[18,384]{1,0:T(8,128)}, f32[18,384]{1,0:T(8,128)S(1)}, u32[]{:S(2)}) copy-start(f32[18,384]{1,0:T(8,128)S(1)} %collective-permute-done.low) | copy-start | bytes 82948
  13.7 0.6 copy-start.10
  14.3 57.1 %copy-start.3 = (bf16[128,256]{1,0:T(8,128)(2,1)S(1)}, bf16[128,256]{1,0:T(8,128)(2,1)}, u32[]{:S(2)}) copy-start(bf16[128,256]{1,0:T(8,128)(2,1)} %constant.71.clone.stencil) | copy-start | bytes 196612
  17.8 20.0 %copy-start.13 = (s32[1152]{0:T(1024)S(1)}, s32[1152]{0:T(1024)}, u32[]{:S(2)}) copy-start(s32[1152]{0:T(1024)} %param.13) | copy-start | bytes 13828
  17.8 53.6 %copy-start = (f32[1152,128]{1,0:T(8,128)S(1)}, f32[1152,128]{1,0:T(8,128)}, u32[]{:S(2)}) copy-start(f32[1152,128]{1,0:T(8,128)} %constant.70.clone.speeds) | copy-start | bytes 1769476
  17.8 53.6 %copy-start.1 = (bf16[256,1152]{1,0:T(8,128)(2,1)S(1)}, bf16[256,1152]{1,0:T(8,128)(2,1)}, u32[]{:S(2)}) copy-start(bf16[256,1152]{1,0:T(8,128)(2,1)} %constant.72.clone.table) | copy-start | bytes 1769476
  17.8 53.6 %all-to-all-start = ((f32[128,1,1152]{2,1,0:T(1,128)}), f32[128,1,1152]{2,1,0:T(1,128)S(1)}, u32[]{:S(2)}, u32[]{:S(2)}) async-start(f32[128,1,1152]{2,1,0:T(1,128)} %bitcast.10), calls=%async_computation | async-start | bytes 1179648 | tf_op jit(solution)/shard_map/all_to_all | solution.py:324
  37.7 0.7 copy-start.14
  38.5 32.9 %copy-start.5 = (f32[8,128]{1,0:T(8,128)S(1)}, f32[8,128]{1,0:T(8,128)}, u32[]{:S(2)}) copy-start(f32[8,128]{1,0:T(8,128)} %get-tuple-element.15.zonal) | copy-start | bytes 12292
  71.4 0.8 copy-start.4
  77.5 6.3 %copy-start.2 = (f32[48,128]{1,0:T(8,128)}, f32[48,128]{1,0:T(8,128)S(1)}, u32[]{:S(2)}) copy-start(f32[48,128]{1,0:T(8,128)S(1)} %get-tuple-element.17.drift) | copy-start | bytes 73732
  77.5 28.7 %all-to-all-start.1 = ((f32[128,1,512]{2,1,0:T(1,128)}), f32[128,1,512]{2,1,0:T(1,128)S(1)}, u32[]{:S(2)}, u32[]{:S(2)}) async-start(f32[128,1,512]{2,1,0:T(1,128)} %bitcast.3), calls=%async_computation.1 | async-start | bytes 524288 | tf_op jit(solution)/shard_map/all_to_all | solution.py:338
  83.8 7.4 %copy-start.15 = (s32[6,32]{1,0:T(8,128)S(1)}, s32[6,32]{1,0:T(8,128)}, u32[]{:S(2)}) copy-start(s32[6,32]{1,0:T(8,128)} %param.15) | copy-start | bytes 2308
  83.9 7.6 %collective-permute-start.2 = (f32[16,128]{1,0:T(8,128)S(1)}, f32[16,128]{1,0:T(8,128)S(1)}, u32[]{:S(2)}, u32[]{:S(2)}) collective-permute-start(f32[16,128]{1,0:T(8,128)S(1)} %get-tuple-element.27), channel_id=1, source_target_pairs={{0,4},{4,8},{8,12},{12,16},{16,20},{20,24},{24,28},{28,32},{32,36}... | collective-permute-start | bytes 24584 | tf_op jit(solution)/shard_map/ppermute | solution.py:339
  87.0 5.1 %collective-permute-start.3 = (f32[16,128]{1,0:T(8,128)S(1)}, f32[16,128]{1,0:T(8,128)S(1)}, u32[]{:S(2)}, u32[]{:S(2)}) collective-permute-start(f32[16,128]{1,0:T(8,128)S(1)} %get-tuple-element.26), channel_id=1, source_target_pairs={{4,0},{8,4},{12,8},{16,12},{20,16},{24,20},{28,24},{32,28},{36,32}... | collective-permute-start | bytes 24584 | tf_op jit(solution)/shard_map/ppermute | solution.py:340
  91.4 14.8 %copy-start.11 = (f32[16,128]{1,0:T(8,128)}, f32[16,128]{1,0:T(8,128)S(1)}, u32[]{:S(2)}) copy-start(f32[16,128]{1,0:T(8,128)S(1)} %collective-permute-done.2.drift_low) | copy-start | bytes 24580
  92.0 14.2 %copy-start.12 = (f32[16,128]{1,0:T(8,128)}, f32[16,128]{1,0:T(8,128)S(1)}, u32[]{:S(2)}) copy-start(f32[16,128]{1,0:T(8,128)S(1)} %collective-permute-done.3.drift_high) | copy-start | bytes 24580
  106.3 0.7 copy-start.6
  108.9 4.9 %collective-permute-start.4 = (f32[24,384]{1,0:T(8,128)}, f32[24,384]{1,0:T(8,128)S(1)}, u32[]{:S(2)}, u32[]{:S(2)}) collective-permute-start(f32[24,384]{1,0:T(8,128)} %get-tuple-element.20), channel_id=1, source_target_pairs={{0,1},{1,2},{2,3},{4,5},{5,6},{6,7},{8,9},{9,10},{10,11},{12,13},{... | collective-permute-start | bytes 110600 | tf_op jit(solution)/shard_map/ppermute | solution.py:347
  110.8 7.0 %collective-permute-start.5 = (f32[24,384]{1,0:T(8,128)}, f32[24,384]{1,0:T(8,128)S(1)}, u32[]{:S(2)}, u32[]{:S(2)}) collective-permute-start(f32[24,384]{1,0:T(8,128)} %get-tuple-element.21), channel_id=1, source_target_pairs={{1,0},{2,1},{3,2},{5,4},{6,5},{7,6},{9,8},{10,9},{11,10},{13,12},{... | collective-permute-start | bytes 110600 | tf_op jit(solution)/shard_map/ppermute | solution.py:348
  113.8 4.0 %copy-start.7 = (f32[24,384]{1,0:T(8,128)}, f32[24,384]{1,0:T(8,128)S(1)}, u32[]{:S(2)}) copy-start(f32[24,384]{1,0:T(8,128)S(1)} %collective-permute-done.4.low) | copy-start | bytes 110596
  117.8 0.6 copy-start.8

commit v2 on v1

--- a/solution.py
+++ b/solution.py
@@ -42,8 +42,9 @@
         for r in range(ROWS):
             lane[column, r] = 16 * group + r
     for column in range(COLS):
-        for k, r in enumerate((-2, -1, 16, 17)):
-            lane[column, r] = 112 + 4 * column + k
+        for k in range(2):
+            lane[column, k - 2] = 112 + 2 * column + k
+            lane[column, 16 + k] = 118 + 2 * column + k
     table = np.zeros((128, 256), np.float32)
     for r in range(ROWS):
         for face in range(COLS + 1):
@@ -70,82 +71,112 @@
     return (upper + pltpu.roll(x - upper, 64, 1)).astype(BF16)
 
 
-def pack_kernel(spec, mask, low, high, current, out, mask_out, zonal_out, stack, turned, turned2):
+def pack_kernel(spec, mask, current, out, mask_out, stack, turned, turned2):
     sea = mask[...].astype(F32)
     masked = spec[...] * sea[None]
-    stack[...] = jnp.zeros_like(stack)
     stack[0:16, :] = masked[8]
     stack[16:32, :] = sea
-    for i in range(OWN):
-        stack[32 + 4 * i : 34 + 4 * i, :] = low[2 * i : 2 * i + 2, :]
-        stack[34 + 4 * i : 36 + 4 * i, :] = high[2 * i : 2 * i + 2, :]
-    for ref in (turned, turned2):
-        ref[0:8, :] = jnp.zeros((8, 128), F32)
-        ref[392:400, :] = jnp.zeros((8, 128), F32)
-    turned[8:392, :] = masked[0:8].reshape(128, NLON).T
-    turned2[8:392, :] = stack[...].T
+    stack[32:128, :] = jnp.zeros((96, NLON), F32)
+    turned[...] = masked[0:8].reshape(128, NLON).T
+    turned2[...] = stack[...].T
 
     pair = lax.broadcasted_iota(jnp.int32, (32, 128), 0) // 2
     means = jnp.where(pair == lax.broadcasted_iota(jnp.int32, (32, 128), 1) % 16, 0.25, 0.0)
     sums = jnp.dot(current[...], means, precision=HIGHEST, preferred_element_type=F32)
-    zonal = [sums[2 * c : 2 * c + 1] + sums[2 * c + 1 : 2 * c + 2] for c in range(COLS)]
-    zonal_out[...] = jnp.concatenate(zonal + [jnp.zeros((5, 128), F32)], axis=0)
+    group = lanes(OWNERS) // 16
+    rest = jnp.zeros((OWNERS, 128), F32)
+    sea_rows = jnp.zeros((OWNERS, 128), F32)
+    for c in range(COLS):
+        out[pl.ds(c, OWNERS, stride=4), :] = turned[pl.ds(c, OWNERS, stride=COLS), :]
+        column = turned2[pl.ds(c, OWNERS, stride=COLS), :]
+        zonal = sums[2 * c : 2 * c + 1] + sums[2 * c + 1 : 2 * c + 2]
+        rest = jnp.where(group == 2 * c, pltpu.roll(column, 32 * c, 1), rest)
+        rest = jnp.where(group == 2 * c + 1, jnp.broadcast_to(zonal, rest.shape), rest)
+        sea_rows = jnp.where(group == c, pltpu.roll(column, (16 * c - 16) % 128, 1), sea_rows)
+    out[pl.ds(3, OWNERS, stride=4), :] = rest
+    mask_out[...] = sea_rows
+
+
+def edges_kernel(arrived, to_east, to_west, to_above, to_below):
+    def part(c):
+        return arrived[pl.ds(c, OWNERS, stride=4), :]
 
     lane = lanes(OWNERS)
     group = lane // 16
-
-    def column(ref, offset):
-        return ref[pl.ds(8 + offset, OWNERS, stride=COLS), :]
-
-    for i in range(OWN):
-        source, at = (turned, 16 * i) if i < 8 else (turned2, 0)
+    inside = lane % 16
+    rest = part(3)
+    for ref, c in ((to_east, 1), (to_west, 0)):
+        ref[0:128, :] = part(c)
+        ref[128:256, :] = part(c + 1)
+        pair = jnp.where(
+            group == 0, pltpu.roll(rest, (-32 * c) % 128, 1), pltpu.roll(rest, (16 - 32 * (c + 1)) % 128, 1)
+        )
+        last = jnp.zeros((32, 128), F32)
+        for q in range(4):
+            moved = pltpu.roll(pair[32 * q : 32 * q + 32], 32 * q, 1)
+            last = jnp.where(group[0:32] // 2 == q, moved, last)
+        ref[256:288, :] = last
+    for ref, r in ((to_above, 14), (to_below, 0)):
         acc = jnp.zeros((OWNERS, 128), F32)
-        for g, offset in enumerate(GROUP_COLUMNS):
-            acc = jnp.where(group == g, pltpu.roll(column(source, offset), (16 * g - at) % 128, 1), acc)
         for c in range(COLS):
-            beyond = pltpu.roll(column(turned2, c), (80 + 4 * c - 4 * i) % 128, 1)
-            acc = jnp.where((lane >= 112 + 4 * c) & (lane < 116 + 4 * c), beyond, acc)
-        if i < 8:
-            flow = pltpu.roll(zonal[0] if i < 4 else zonal[2], (124 - 4 * (i % 4)) % 128, 1)
-            acc = jnp.where(lane >= 124, jnp.broadcast_to(flow, acc.shape), acc)
-        out[pl.ds(i, OWNERS, stride=OWN), :] = acc
-    acc = jnp.zeros((OWNERS, 128), F32)
-    for c in range(COLS):
-        acc = jnp.where(group == c, pltpu.roll(column(turned2, c), (16 * c - 16) % 128, 1), acc)
-    mask_out[...] = acc
+            moved = pltpu.roll(part(c), (2 * c - r) % 128, 1)
+            acc = jnp.where((inside >= 2 * c) & (inside < 2 * c + 2), moved, acc)
+        for c in range(COLS):
+            moved = pltpu.roll(rest, (6 + 2 * c - 32 * c - r) % 128, 1)
+            acc = jnp.where((lane >= 6 + 2 * c) & (lane < 8 + 2 * c), moved, acc)
+        ref[...] = acc
 
 
 def points_kernel(
-    me, arrived, masks, zonal, plus, minus, speeds, stencil, table,
+    me, arrived, from_west, from_east, from_below, from_above, masks, plus, minus, speeds, stencil, table,
     out, drift_out, first, source, middle, halves, plus_col, minus_col,
 ):
     device = me[0]
+    lane = lanes(OWNERS)
+    group = lane // 16
+
+    flow = arrived[pl.ds(4 * device + 3, 1), :]
+    below = arrived[pl.ds(4 * jnp.maximum(device - 1, 0) + 3, 1), :]
+    above = arrived[pl.ds(4 * jnp.minimum(device + 1, OWNERS - 1) + 3, 1), :]
+    lower = jnp.where(device > 0, pltpu.roll(below, 48, 1), 0.0)
+    upper = jnp.where(device < OWNERS - 1, pltpu.roll(above, 32, 1), 0.0)
     lane1 = lanes()
-    below = jnp.zeros((1, 128), F32)
-    above = jnp.zeros((1, 128), F32)
-    left = jnp.maximum(device - 1, 0) * OWN + 4
-    right = jnp.minimum(device + 1, OWNERS - 1) * OWN
-    for k in range(4):
-        here = (lane1 >= 4 * k) & (lane1 < 4 * k + 4)
-        below = jnp.where(here, pltpu.roll(arrived[pl.ds(left + k, 1), :], 4 + 4 * k, 1), below)
-        above = jnp.where(here, pltpu.roll(arrived[pl.ds(right + k, 1), :], 4 + 4 * k, 1), above)
-    below = jnp.where(device > 0, below, 0.0)
-    above = pltpu.roll(jnp.where(device < OWNERS - 1, above, 0.0), 48, 1)
     group1 = lane1 // 16
-    columns = [zonal[c : c + 1, :] for c in range(COLS)]
-    lower = below
-    upper = above
     for c in range(COLS):
-        lower = jnp.where(group1 == c + 1, columns[c], lower)
-        upper = jnp.where(group1 == c, columns[c], upper)
+        lower = jnp.where(group1 == c + 1, pltpu.roll(flow, (-16 * c) % 128, 1), lower)
+        upper = jnp.where(group1 == c, pltpu.roll(flow, (-16 * (c + 1)) % 128, 1), upper)
     faces = jnp.where(lane1 < 64, 0.5 * (lower + upper), 0.0)
     sea = masks[pl.ds(device, 1), :]
 
     def chunk(t):
         return slice(128 * t, 128 * t + 128)
 
+    for i in range(OWN):
+        acc = jnp.zeros((OWNERS, 128), F32)
+        for g in range(7):
+            if i == 8:
+                if g < 3:
+                    part = pltpu.roll(arrived[pl.ds(3, OWNERS, stride=4), :], (-16 * g) % 128, 1)
+                else:
+                    ref, at = (from_west, 48) if g < 5 else (from_east, 80)
+                    piece = ref[256:288, :]
+                    part = jnp.concatenate([pltpu.roll(piece, (at - 32 * q) % 128, 1) for q in range(4)], axis=0)
+            else:
+                if g < 3:
+                    part = arrived[pl.ds(g, OWNERS, stride=4), :]
+                elif g < 5:
+                    part = from_west[chunk(g - 3), :]
+                else:
+                    part = from_east[chunk(g - 5), :]
+                part = pltpu.roll(part, (16 * g - 16 * i) % 128, 1)
+            acc = jnp.where(group == g, part, acc)
+        held = 16 * i if i < 8 else 6
+        for ref, at in ((from_below, 112), (from_above, 118)):
+            acc = jnp.where((lane >= at) & (lane < at + 6), pltpu.roll(ref[...], (at - held) % 128, 1), acc)
+        middle[pl.ds(i, OWNERS, stride=OWN), :] = acc
+
     for t in range(OWN):
-        value = arrived[chunk(t), :]
+        value = middle[chunk(t), :]
         upper_half = value.astype(BF16)
         lower_half = (value - upper_half.astype(F32)).astype(BF16)
         sums = jnp.dot(upper_half, stencil[...], preferred_element_type=F32) + jnp.dot(
@@ -155,7 +186,7 @@
         flux = jnp.maximum(speed, 0.0) * sums[:, 0:128] + jnp.minimum(speed, 0.0) * sums[:, 128:256]
         change = (pltpu.roll(flux, 112, 1) - flux) + pltpu.roll(flux, 64, 1)
         moved = sea * (value - change)
-        moved = jnp.where(lanes(128) < 48, moved, 0.0)
+        moved = jnp.where(lane < 48, moved, 0.0)
         first[chunk(t), :] = moved
         halves[chunk(t), :] = split_beside(moved)
         for row, col in ((plus, plus_col), (minus, minus_col)):
@@ -184,25 +215,23 @@
         both = jnp.dot(hits.astype(BF16), halves[...], preferred_element_type=F32)
         back = both + pltpu.roll(both, 64, 1)
         m = first[chunk(t), :] + (source[chunk(t), :] - 0.5 * back)
-        middle[chunk(t), :] = jnp.where(lanes(128) < 48, m, 0.0)
+        middle[chunk(t), :] = jnp.where(lane < 48, m, 0.0)
     for t in range(OWN):
         halves[chunk(t), :] = split_beside(middle[chunk(t), :])
     sums = jnp.dot(table[...], halves[...], preferred_element_type=F32)
     drift = sums[0:128] + pltpu.roll(sums[0:128], 64, 1) + sums[128:256]
     drift_out[...] = drift.T[0:48]
 
-    group = lanes(OWNERS) // 16
     for c in range(COLS):
         acc = jnp.zeros((OWNERS, 128), F32)
         for i in range(8):
             part = pltpu.roll(middle[pl.ds(i, OWNERS, stride=OWN), :], (16 * (i - c)) % 128, 1)
             acc = jnp.where(group == i, part, acc)
         out[pl.ds(c, OWNERS, stride=4), :] = acc
-    acc = jnp.zeros((OWNERS, 128), F32)
+    acc = jnp.broadcast_to(flow, (OWNERS, 128))
     last = middle[pl.ds(8, OWNERS, stride=OWN), :]
     for c in range(COLS):
         acc = jnp.where(group == 2 * c, pltpu.roll(last, 16 * c, 1), acc)
-        acc = jnp.where(group == 2 * c + 1, jnp.broadcast_to(columns[c], acc.shape), acc)
     out[pl.ds(3, OWNERS, stride=4), :] = acc
 
 
@@ -306,32 +335,37 @@
     east = [(i, i + 1) for i in range(OWNERS - 1)]
     west = [(i + 1, i) for i in range(OWNERS - 1)]
 
-    def edge(start):
-        rows = spectrum[:, start : start + 2] * sea_mask[None, start : start + 2].astype(F32)
-        return rows.reshape(2 * OWN, NLON)
-
-    from_below = lax.ppermute(edge(14), "lat", up)
-    from_above = lax.ppermute(edge(0), "lat", down)
-
     smem = pl.BlockSpec(memory_space=pltpu.SMEM)
     vmem = pl.BlockSpec(memory_space=pltpu.VMEM)
-    sent, masks, zonal = pl.pallas_call(
+    grant = pltpu.CompilerParams(vmem_limit_bytes=16 * 1024 * 1024)
+    sent, masks = pl.pallas_call(
         pack_kernel,
-        out_shape=shapes((BINS, 128), (OWNERS, 128), (8, 128)),
-        scratch_shapes=[pltpu.VMEM((128, NLON), F32), pltpu.VMEM((400, 128), F32), pltpu.VMEM((400, 128), F32)],
-    )(spectrum, sea_mask, from_below, from_above, current)
-
-    arrived = lax.all_to_all(sent.reshape(OWNERS, 1, OWN * 128), "bins", 0, 0).reshape(BINS, 128)
+        out_shape=shapes((4 * OWNERS, 128), (OWNERS, 128)),
+        scratch_shapes=[pltpu.VMEM((128, NLON), F32), pltpu.VMEM((NLON, 128), F32), pltpu.VMEM((NLON, 128), F32)],
+        compiler_params=grant,
+    )(spectrum, sea_mask, current)
+
+    arrived = lax.all_to_all(sent.reshape(OWNERS, 1, 512), "bins", 0, 0).reshape(4 * OWNERS, 128)
+    to_east, to_west, to_above, to_below = pl.pallas_call(
+        edges_kernel,
+        out_shape=shapes((288, 128), (288, 128), (OWNERS, 128), (OWNERS, 128)),
+        compiler_params=grant,
+    )(arrived)
+    from_west = lax.ppermute(to_east, "bins", east)
+    from_east = lax.ppermute(to_west, "bins", west)
+    from_below = lax.ppermute(to_above, "lat", up)
+    from_above = lax.ppermute(to_below, "lat", down)
 
     big = pltpu.VMEM((BINS, 128), F32)
     sent, drift = pl.pallas_call(
         points_kernel,
         out_shape=shapes((4 * OWNERS, 128), (48, 128)),
-        in_specs=[smem] + [vmem] * 8,
+        in_specs=[smem] + [vmem] * 11,
         scratch_shapes=[big, big, big, pltpu.VMEM((BINS, 128), BF16), big, big],
-        compiler_params=pltpu.CompilerParams(vmem_limit_bytes=40 * 1024 * 1024),
+        compiler_params=pltpu.CompilerParams(vmem_limit_bytes=32 * 1024 * 1024),
     )(
-        device, arrived, masks, zonal, partner_plus.reshape(1, BINS), partner_minus.reshape(1, BINS),
+        device, arrived, from_west, from_east, from_below, from_above, masks,
+        partner_plus.reshape(1, BINS), partner_minus.reshape(1, BINS),
         jnp.asarray(speeds), jnp.asarray(stencil), jnp.asarray(table),
     )
 
@@ -343,6 +377,7 @@
         unpack_kernel,
         out_shape=shapes((OWN * ROWS, NLON), (ROWS, NLON), (24, NLON), (24, NLON)),
         scratch_shapes=[pltpu.VMEM((NLON, 128), F32), pltpu.VMEM((NLON, 128), F32)],
+        compiler_params=grant,
     )(arrived, drift, drift_low, drift_high)
     from_below = lax.ppermute(high, "lat", up)
     from_above = lax.ppermute(low, "lat", down)
@@ -356,6 +391,7 @@
         out_shape=shapes((OWN, ROWS, NLON), (2, 192, 64)),
         in_specs=[smem, smem] + [vmem] * 9,
         scratch_shapes=[pltpu.VMEM((32, NLON), F32), pltpu.VMEM((128, 128), F32)],
+        compiler_params=grant,
     )(
         device, jnp.asarray(speed_list), middle, zonal_all, from_below, from_above, sea_mask,
         drift, drift_low, drift_high, place,

time: 122 us -> 114 us (0.934)
  blocking collectives: 0 us -> 40.6 us
  waiting for transfers between devices: 56.6 us -> 22.6 us
  starting transfers between devices: 44.3 us -> 35.8 us
  Pallas kernels: 13.2 us -> 9.57 us
  other arithmetic: 2.38 us -> 0.09 us
    all_to_all x0 -> x1, blocking collectives: none -> 40.6 us  [on_device(): lax.all_to_all(sent.reshape(OWNERS, 1, 512), 'bins', 0, 0)]
    all_to_all x1 -> x0, waiting for transfers between devices: 32.9 us -> none  [on_device(): lax.all_to_all(sent.reshape(OWNERS, 1, OWN * 128), 'bins', 0, 0)]
    all_to_all x1 -> x0, starting transfers between devices: 19.9 us -> none  [on_device(): lax.all_to_all(sent.reshape(OWNERS, 1, OWN * 128), 'bins', 0, 0)]
    ppermute x2 -> x4, starting transfers between devices: 6.4 us -> 16.8 us  [the longest x1 7.48 us: on_device(): from_below = lax.ppermute(to_above, 'lat', up)]
    pallas_call x1 -> x2, Pallas kernels: 3.5 us -> 0.69 us  [the longest x1 0.37 us: on_device(): pl.pallas_call(edges_kernel, out_shape=shapes((288, 128), (288, 128), (OW...]
    pallas_call x1, Pallas kernels: 1.91 us -> 0.23 us  [on_device(): pl.pallas_call(unpack_kernel, out_shape=shapes((OWN * ROWS, NLON), (ROWS,...]
    unnamed x32 -> x22, local copies, waits for them, and re-layouts: 3.44 us -> 4.17 us
    ppermute x2 -> x4, waiting for transfers between devices: 4.83 us -> 4.46 us  [the longest x1 4.45 us: on_device(): from_above = lax.ppermute(to_below, 'lat', down)]
  transfers between devices with their start and end apart: 8 -> 9, of which waited for: 5 -> 4; matrix products, arithmetic and copies ran while one was open for 1% -> 0% of each run, Pallas kernels for 0% -> 0%
where the time goes in v2:
time: 114 us
  blocking collectives  40.6 us (36%)
  starting transfers between devices  35.8 us (31%)
  waiting for transfers between devices  22.6 us (20%)
  Pallas kernels  9.57 us (8%)
  local copies, waits for them, and re-layouts  4.27 us (4%)
    all_to_all x1, blocking collectives, on_device(): lax.all_to_all(sent.reshape(OWNERS, 1, 512), 'bins', 0, 0)  40.6 us
    all_to_all x1, waiting for transfers between devices, on_device(): lax.all_to_all(sent.reshape(OWNERS, 1, 512), 'bins', 0, 0)  13.2 us
    ppermute x1, starting transfers between devices, on_device(): from_below = lax.ppermute(to_above, 'lat', up)  7.48 us
    all_to_all x1, starting transfers between devices, on_device(): lax.all_to_all(sent.reshape(OWNERS, 1, 512), 'bins', 0, 0)  7.25 us
    pallas_call x1, Pallas kernels, on_device(): pl.pallas_call(points_kernel, out_shape=shapes((4 * OWNERS, 128), (48, 12...  6.48 us
    ppermute x1, starting transfers between devices, on_device(): from_east = lax.ppermute(to_west, 'bins', west)  4.99 us
    ppermute x1, waiting for transfers between devices, on_device(): from_above = lax.ppermute(to_below, 'lat', down)  4.45 us
    ppermute x1, waiting for transfers between devices, on_device(): from_above = lax.ppermute(low, 'lat', down)  4.35 us
  transfers between devices with their start and end apart: 9, of which 4 were waited for; matrix products, arithmetic and copies ran while one was open for 0% of the time, Pallas kernels for 0%

profile of v2, /device:TPU:9, one launch (start us, length us, event | category | flops | bytes accessed | tf_op | source)
XLA Modules:
  0.0 113.7 jit_solution(11760704864245777087)
XLA Ops:
  0.6 0.0 copy-start
  0.7 1.0 copy-done.2
  1.6 0.7 copy-done.3
  2.4 0.7 copy-done.7
  3.1 0.3 shard_map.113
  3.4 40.6 %all_to_all.10 = f32[128,1,512]{2,1,0:T(1,128)S(1)} all-to-all(f32[128,1,512]{2,1,0:T(1,128)S(1)} %bitcast.11), channel_id=1, replica_groups=mesh['bins'=128,'lat'=4] {'bins'}, dimensions={0} | all-to-all | bytes 524288 | tf_op jit(solution)/shard_map/all_to_all | solution.py:348
  44.0 0.4 shard_map.114
  44.4 0.0 copy-start.8
  44.4 2.4 %collective-permute-start = (f32[288,128]{1,0:T(8,128)S(1)}, f32[288,128]{1,0:T(8,128)S(1)}, u32[]{:S(2)}, u32[]{:S(2)}) collective-permute-start(f32[288,128]{1,0:T(8,128)S(1)} %get-tuple-element.17), channel_id=1, source_target_pairs={{0,4},{4,8},{8,12},{12,16},{16,20},{20,24},{24,28},{28,32},{32,36}... | collective-permute-start | bytes 442376 | tf_op jit(solution)/shard_map/ppermute | solution.py:354
  46.8 5.0 %collective-permute-start.1 = (f32[288,128]{1,0:T(8,128)S(1)}, f32[288,128]{1,0:T(8,128)S(1)}, u32[]{:S(2)}, u32[]{:S(2)}) collective-permute-start(f32[288,128]{1,0:T(8,128)S(1)} %get-tuple-element.18), channel_id=1, source_target_pairs={{4,0},{8,4},{12,8},{16,12},{20,16},{24,20},{28,24},{32,28},{36,32}... | collective-permute-start | bytes 442376 | tf_op jit(solution)/shard_map/ppermute | solution.py:355
  51.8 7.5 %collective-permute-start.2 = (f32[128,128]{1,0:T(8,128)S(1)}, f32[128,128]{1,0:T(8,128)S(1)}, u32[]{:S(2)}, u32[]{:S(2)}) collective-permute-start(f32[128,128]{1,0:T(8,128)S(1)} %get-tuple-element.19), channel_id=1, source_target_pairs={{0,1},{1,2},{2,3},{4,5},{5,6},{6,7},{8,9},{9,10},{10,11},{12,13},{... | collective-permute-start | bytes 196616 | tf_op jit(solution)/shard_map/ppermute | solution.py:356
  59.3 1.9 %collective-permute-start.3 = (f32[128,128]{1,0:T(8,128)S(1)}, f32[128,128]{1,0:T(8,128)S(1)}, u32[]{:S(2)}, u32[]{:S(2)}) collective-permute-start(f32[128,128]{1,0:T(8,128)S(1)} %get-tuple-element.20), channel_id=1, source_target_pairs={{1,0},{2,1},{3,2},{5,4},{6,5},{7,6},{9,8},{10,9},{11,10},{13,12},{... | collective-permute-start | bytes 196616 | tf_op jit(solution)/shard_map/ppermute | solution.py:357
  61.2 0.0 copy-start.9
  61.3 0.7 copy-done.9
  61.9 0.0 collective-permute-done.2.from_below
  61.9 4.4 %collective-permute-done.3.from_above = f32[128,128]{1,0:T(8,128)S(1)} collective-permute-done((f32[128,128]{1,0:T(8,128)S(1)}, f32[128,128]{1,0:T(8,128)S(1)}, u32[]{:S(2)}, u32[]{:S(2)}) %collective-permute-start.3) | collective-permute-done | bytes 65568 | tf_op jit(solution)/shard_map/ppermute | solution.py:357
  66.4 0.0 copy-start.1
  66.4 1.1 copy-done.1
  67.5 6.5 %shard_map.115 = (f32[512,128]{1,0:T(8,128)}, f32[48,128]{1,0:T(8,128)S(1)}) custom-call(s32[1]{0:T(128)} %bitcast.me, f32[512,128]{1,0:T(8,128)S(1)} %bitcast.9, f32[288,128]{1,0:T(8,128)S(1)} %collective-permute-done.from_west, f32[288,128]{1,0:T(8,128)S(1)} %collective-permute-done.1.from_east, f32[128,128]{1,0:T(8,128)S(1)} %collective-permute-done.2.from_below, ...), custom_call_target="tpu_custom_call" | custom-call | tf_op jit(solution)/shard_map/pallas_call | solution.py:360
  73.9 7.2 %all-to-all-start.1 = ((f32[128,1,512]{2,1,0:T(1,128)}), f32[128,1,512]{2,1,0:T(1,128)S(1)}, u32[]{:S(2)}, u32[]{:S(2)}) async-start(f32[128,1,512]{2,1,0:T(1,128)} %bitcast.3), calls=%async_computation.1 | async-start | bytes 524288 | tf_op jit(solution)/shard_map/all_to_all | solution.py:372
  81.2 0.0 copy-start.10
  81.2 3.1 %collective-permute-start.4 = (f32[16,128]{1,0:T(8,128)S(1)}, f32[16,128]{1,0:T(8,128)S(1)}, u32[]{:S(2)}, u32[]{:S(2)}) collective-permute-start(f32[16,128]{1,0:T(8,128)S(1)} %get-tuple-element.31), channel_id=1, source_target_pairs={{0,4},{4,8},{8,12},{12,16},{16,20},{20,24},{24,28},{28,32},{32,36}... | collective-permute-start | bytes 24584 | tf_op jit(solution)/shard_map/ppermute | solution.py:373
  84.3 4.3 %collective-permute-start.5 = (f32[16,128]{1,0:T(8,128)S(1)}, f32[16,128]{1,0:T(8,128)S(1)}, u32[]{:S(2)}, u32[]{:S(2)}) collective-permute-start(f32[16,128]{1,0:T(8,128)S(1)} %get-tuple-element.30), channel_id=1, source_target_pairs={{4,0},{8,4},{12,8},{16,12},{20,16},{24,20},{28,24},{32,28},{36,32}... | collective-permute-start | bytes 24584 | tf_op jit(solution)/shard_map/ppermute | solution.py:374
  88.7 0.1 select_select_fusion
  88.7 0.1 reshape.112
  88.8 0.6 collective-permute-done.5.drift_high
  89.4 13.2 %all-to-all-done.1 = f32[128,1,512]{2,1,0:T(1,128)S(1)} async-done(((f32[128,1,512]{2,1,0:T(1,128)}), f32[128,1,512]{2,1,0:T(1,128)S(1)}, u32[]{:S(2)}, u32[]{:S(2)}) %all-to-all-start.1) | async-done | bytes 262176 | tf_op jit(solution)/shard_map/all_to_all | solution.py:372
  102.6 0.2 shard_map.116
  102.8 1.9 %collective-permute-start.6 = (f32[24,384]{1,0:T(8,128)S(1)}, f32[24,384]{1,0:T(8,128)S(1)}, u32[]{:S(2)}, u32[]{:S(2)}) collective-permute-start(f32[24,384]{1,0:T(8,128)S(1)} %get-tuple-element.26), channel_id=1, source_target_pairs={{0,1},{1,2},{2,3},{4,5},{5,6},{6,7},{8,9},{9,10},{10,11},{12,13},{... | collective-permute-start | bytes 110600 | tf_op jit(solution)/shard_map/ppermute | solution.py:382
  104.8 2.4 %collective-permute-start.7 = (f32[24,384]{1,0:T(8,128)S(1)}, f32[24,384]{1,0:T(8,128)S(1)}, u32[]{:S(2)}, u32[]{:S(2)}) collective-permute-start(f32[24,384]{1,0:T(8,128)S(1)} %get-tuple-element.27), channel_id=1, source_target_pairs={{1,0},{2,1},{3,2},{5,4},{6,5},{7,6},{9,8},{10,9},{11,10},{13,12},{... | collective-permute-start | bytes 110600 | tf_op jit(solution)/shard_map/ppermute | solution.py:383
  107.2 4.3 %collective-permute-done.7.high = f32[24,384]{1,0:T(8,128)S(1)} collective-permute-done((f32[24,384]{1,0:T(8,128)S(1)}, f32[24,384]{1,0:T(8,128)S(1)}, u32[]{:S(2)}, u32[]{:S(2)}) %collective-permute-start.7) | collective-permute-done | bytes 36896 | tf_op jit(solution)/shard_map/ppermute | solution.py:383
  111.5 2.2 %shard_map.117 = (f32[9,16,384]{2,1,0:T(8,128)}, f32[2,192,64]{2,1,0:T(8,128)}) custom-call(s32[1]{0:T(128)} %bitcast.me, f32[2304]{0:T(1024)S(1)} %copy-done.6, f32[144,384]{1,0:T(8,128)S(1)} %get-tuple-element.24.middle, f32[16,384]{1,0:T(8,128)S(1)} %get-tuple-element.25.zonal, f32[24,384]{1,0:T(8,128)S(1)} %collective-permute-done.6.low, ...), custom_call_target="tpu_custom_call" | custom-call | tf_op jit(solution)/shard_map/pallas_call | solution.py:389
  (22 shorter events, 0.1 us)
Async XLA Ops:
  0.6 65.8 %copy-start = (f32[1152,128]{1,0:T(8,128)S(1)}, f32[1152,128]{1,0:T(8,128)}, u32[]{:S(2)}) copy-start(f32[1152,128]{1,0:T(8,128)} %constant.70.clone.speeds) | copy-start | bytes 1769476
  0.6 1.0 copy-start.2
  1.6 0.7 copy-start.3
  2.4 0.7 copy-start.7
  44.0 22.4 %copy-start.5 = (bf16[128,256]{1,0:T(8,128)(2,1)S(1)}, bf16[128,256]{1,0:T(8,128)(2,1)}, u32[]{:S(2)}) copy-start(bf16[128,256]{1,0:T(8,128)(2,1)} %constant.71.clone.stencil) | copy-start | bytes 196612
  44.4 16.9 %copy-start.8 = (s32[1152]{0:T(1024)S(1)}, s32[1152]{0:T(1024)}, u32[]{:S(2)}) copy-start(s32[1152]{0:T(1024)} %param.13) | copy-start | bytes 13828
  44.4 22.0 %collective-permute-start = (f32[288,128]{1,0:T(8,128)S(1)}, f32[288,128]{1,0:T(8,128)S(1)}, u32[]{:S(2)}, u32[]{:S(2)}) collective-permute-start(f32[288,128]{1,0:T(8,128)S(1)} %get-tuple-element.17), channel_id=1, source_target_pairs={{0,4},{4,8},{8,12},{12,16},{16,20},{20,24},{24,28},{28,32},{32,36}... | collective-permute-start | bytes 442376 | tf_op jit(solution)/shard_map/ppermute | solution.py:354
  46.8 19.6 %collective-permute-start.1 = (f32[288,128]{1,0:T(8,128)S(1)}, f32[288,128]{1,0:T(8,128)S(1)}, u32[]{:S(2)}, u32[]{:S(2)}) collective-permute-start(f32[288,128]{1,0:T(8,128)S(1)} %get-tuple-element.18), channel_id=1, source_target_pairs={{4,0},{8,4},{12,8},{16,12},{20,16},{24,20},{28,24},{32,28},{36,32}... | collective-permute-start | bytes 442376 | tf_op jit(solution)/shard_map/ppermute | solution.py:355
  51.8 10.1 %collective-permute-start.2 = (f32[128,128]{1,0:T(8,128)S(1)}, f32[128,128]{1,0:T(8,128)S(1)}, u32[]{:S(2)}, u32[]{:S(2)}) collective-permute-start(f32[128,128]{1,0:T(8,128)S(1)} %get-tuple-element.19), channel_id=1, source_target_pairs={{0,1},{1,2},{2,3},{4,5},{5,6},{6,7},{8,9},{9,10},{10,11},{12,13},{... | collective-permute-start | bytes 196616 | tf_op jit(solution)/shard_map/ppermute | solution.py:356
  59.3 7.1 %collective-permute-start.3 = (f32[128,128]{1,0:T(8,128)S(1)}, f32[128,128]{1,0:T(8,128)S(1)}, u32[]{:S(2)}, u32[]{:S(2)}) collective-permute-start(f32[128,128]{1,0:T(8,128)S(1)} %get-tuple-element.20), channel_id=1, source_target_pairs={{1,0},{2,1},{3,2},{5,4},{6,5},{7,6},{9,8},{10,9},{11,10},{13,12},{... | collective-permute-start | bytes 196616 | tf_op jit(solution)/shard_map/ppermute | solution.py:357
  61.2 0.7 copy-start.9
  66.4 1.1 copy-start.1
  73.9 28.7 %all-to-all-start.1 = ((f32[128,1,512]{2,1,0:T(1,128)}), f32[128,1,512]{2,1,0:T(1,128)S(1)}, u32[]{:S(2)}, u32[]{:S(2)}) async-start(f32[128,1,512]{2,1,0:T(1,128)} %bitcast.3), calls=%async_computation.1 | async-start | bytes 524288 | tf_op jit(solution)/shard_map/all_to_all | solution.py:372
  81.2 7.4 %copy-start.10 = (s32[6,32]{1,0:T(8,128)S(1)}, s32[6,32]{1,0:T(8,128)}, u32[]{:S(2)}) copy-start(s32[6,32]{1,0:T(8,128)} %param.15) | copy-start | bytes 2308
  81.2 7.6 %collective-permute-start.4 = (f32[16,128]{1,0:T(8,128)S(1)}, f32[16,128]{1,0:T(8,128)S(1)}, u32[]{:S(2)}, u32[]{:S(2)}) collective-permute-start(f32[16,128]{1,0:T(8,128)S(1)} %get-tuple-element.31), channel_id=1, source_target_pairs={{0,4},{4,8},{8,12},{12,16},{16,20},{20,24},{24,28},{28,32},{32,36}... | collective-permute-start | bytes 24584 | tf_op jit(solution)/shard_map/ppermute | solution.py:373
  84.3 5.1 %collective-permute-start.5 = (f32[16,128]{1,0:T(8,128)S(1)}, f32[16,128]{1,0:T(8,128)S(1)}, u32[]{:S(2)}, u32[]{:S(2)}) collective-permute-start(f32[16,128]{1,0:T(8,128)S(1)} %get-tuple-element.30), channel_id=1, source_target_pairs={{4,0},{8,4},{12,8},{16,12},{20,16},{24,20},{28,24},{32,28},{36,32}... | collective-permute-start | bytes 24584 | tf_op jit(solution)/shard_map/ppermute | solution.py:374
  102.6 8.9 %copy-start.4 = (s32[16,384]{1,0:T(8,128)S(1)}, s32[16,384]{1,0:T(8,128)}, u32[]{:S(2)}) copy-start(s32[16,384]{1,0:T(8,128)} %mask.3) | copy-start | bytes 73732
  102.6 8.9 %copy-start.6 = (f32[2304]{0:T(1024)S(1)}, f32[2304]{0:T(1024)}, u32[]{:S(2)}) copy-start(f32[2304]{0:T(1024)} %constant.73.clone.speeds) | copy-start | bytes 27652
  102.8 4.4 %collective-permute-start.6 = (f32[24,384]{1,0:T(8,128)S(1)}, f32[24,384]{1,0:T(8,128)S(1)}, u32[]{:S(2)}, u32[]{:S(2)}) collective-permute-start(f32[24,384]{1,0:T(8,128)S(1)} %get-tuple-element.26), channel_id=1, source_target_pairs={{0,1},{1,2},{2,3},{4,5},{5,6},{6,7},{8,9},{9,10},{10,11},{12,13},{... | collective-permute-start | bytes 110600 | tf_op jit(solution)/shard_map/ppermute | solution.py:382
  104.8 6.8 %collective-permute-start.7 = (f32[24,384]{1,0:T(8,128)S(1)}, f32[24,384]{1,0:T(8,128)S(1)}, u32[]{:S(2)}, u32[]{:S(2)}) collective-permute-start(f32[24,384]{1,0:T(8,128)S(1)} %get-tuple-element.27), channel_id=1, source_target_pairs={{1,0},{2,1},{3,2},{5,4},{6,5},{7,6},{9,8},{10,9},{11,10},{13,12},{... | collective-permute-start | bytes 110600 | tf_op jit(solution)/shard_map/ppermute | solution.py:383

commit v3 on v2

--- a/solution.py
+++ b/solution.py
@@ -71,7 +71,15 @@
     return (upper + pltpu.roll(x - upper, 64, 1)).astype(BF16)
 
 
-def pack_kernel(spec, mask, current, out, mask_out, stack, turned, turned2):
+def pack_kernel(spec_at, mask_at, current_at, out, mask_out, spec, mask, current, stack, turned, turned2, done):
+    copies = [
+        pltpu.make_async_copy(source, held, done.at[k])
+        for k, (source, held) in enumerate(((spec_at, spec), (mask_at, mask), (current_at, current)))
+    ]
+    for copy in copies:
+        copy.start()
+    for copy in copies:
+        copy.wait()
     sea = mask[...].astype(F32)
     masked = spec[...] * sea[None]
     stack[0:16, :] = masked[8]
@@ -127,9 +135,25 @@
         ref[...] = acc
 
 
+def partners_kernel(plus, minus, stencil_in, speeds_in, table_in, picks, hits, stencil, speeds, table):
+    stencil[...] = stencil_in[...]
+    speeds[...] = speeds_in[...]
+    table[...] = table_in[...]
+    numbers = lax.broadcasted_iota(jnp.int32, (128, BINS), 1).astype(F32)
+    for t in range(OWN):
+        rows = slice(128 * t, 128 * t + 128)
+        for k, row in enumerate((plus, minus)):
+            column = jnp.broadcast_to(row[:, rows].astype(F32), (128, 128)).T
+            wide = jnp.concatenate([column] * OWN, axis=1)
+            picks[BINS * k + 128 * t : BINS * k + 128 * t + 128, :] = jnp.where(wide == numbers, 1.0, 0.0).astype(BF16)
+        names = lax.broadcasted_iota(jnp.int32, (128, BINS), 0) + 128 * t
+        both = jnp.where(plus[...] == names, 1.0, 0.0) + jnp.where(minus[...] == names, 1.0, 0.0)
+        hits[rows, :] = both.astype(BF16)
+
+
 def points_kernel(
-    me, arrived, from_west, from_east, from_below, from_above, masks, plus, minus, speeds, stencil, table,
-    out, drift_out, first, source, middle, halves, plus_col, minus_col,
+    me, arrived, from_west, from_east, from_below, from_above, masks, picks, hits, stencil, speeds, table,
+    out, drift_out, first, source, middle, halves,
 ):
     device = me[0]
     lane = lanes(OWNERS)
@@ -189,30 +213,21 @@
         moved = jnp.where(lane < 48, moved, 0.0)
         first[chunk(t), :] = moved
         halves[chunk(t), :] = split_beside(moved)
-        for row, col in ((plus, plus_col), (minus, minus_col)):
-            part = jnp.broadcast_to(row[:, chunk(t)].astype(F32), (128, 128))
-            col[chunk(t), :] = part.T
-
-    numbers = lax.broadcasted_iota(jnp.int32, (128, BINS), 1).astype(F32)
-
-    def gathered(col, t):
-        wide = jnp.concatenate([col[chunk(t), :]] * OWN, axis=1)
-        chosen = jnp.where(wide == numbers, 1.0, 0.0).astype(BF16)
-        both = jnp.dot(chosen, halves[...], preferred_element_type=F32)
+
+    def gathered(at):
+        both = jnp.dot(picks[at : at + 128, :], halves[...], preferred_element_type=F32)
         return both + pltpu.roll(both, 64, 1)
 
     for t in range(OWN):
-        ahead = gathered(plus_col, t)
-        behind = gathered(minus_col, t)
+        ahead = gathered(128 * t)
+        behind = gathered(BINS + 128 * t)
         f = first[chunk(t), :]
         strength = jnp.broadcast_to(speeds[chunk(t), 127:128], (128, 128))
         source[chunk(t), :] = strength * (f * f * (ahead + behind) - 2.0 * f * ahead * behind)
     for t in range(OWN):
         halves[chunk(t), :] = split_beside(source[chunk(t), :])
     for t in range(OWN):
-        names = lax.broadcasted_iota(jnp.int32, (128, BINS), 0) + 128 * t
-        hits = jnp.where(plus[...] == names, 1.0, 0.0) + jnp.where(minus[...] == names, 1.0, 0.0)
-        both = jnp.dot(hits.astype(BF16), halves[...], preferred_element_type=F32)
+        both = jnp.dot(hits[chunk(t), :], halves[...], preferred_element_type=F32)
         back = both + pltpu.roll(both, 64, 1)
         m = first[chunk(t), :] + (source[chunk(t), :] - 0.5 * back)
         middle[chunk(t), :] = jnp.where(lane < 48, m, 0.0)
@@ -255,9 +270,7 @@
         ref[20:24, :] = jnp.zeros((4, NLON), F32)
 
 
-def final_kernel(
-    me, speeds, middle, zonal, low, high, mask, drift, drift_low, drift_high, place, out, stokes, rows, near
-):
+def inside_kernel(me, speeds, middle, zonal, mask, out, rows):
     first_bin = me[0] * OWN
     sea = mask[...].astype(F32)
     column = lax.broadcasted_iota(jnp.int32, (ROWS, NLON), 1)
@@ -269,11 +282,11 @@
     flow = zonal[...]
     lower_flow = 0.5 * (beside(flow, -1) + flow)
     upper_flow = 0.5 * (flow + beside(flow, 1))
+    rows[0:8, :] = jnp.zeros((8, NLON), F32)
+    rows[24:32, :] = jnp.zeros((8, NLON), F32)
     for i in range(OWN):
         f = middle[16 * i : 16 * i + 16, :]
         rows[8:24, :] = f
-        rows[6:8, :] = low[2 * i : 2 * i + 2, :]
-        rows[24:26, :] = high[2 * i : 2 * i + 2, :]
         along_x = speeds[first_bin + i]
         along_y = speeds[BINS + first_bin + i]
         r2, r1, u1, u2 = rows[6:22, :], rows[7:23, :], rows[9:25, :], rows[10:26, :]
@@ -293,6 +306,22 @@
         )
         out[i] = sea * (f - change)
 
+
+def final_kernel(me, speeds, inside, low, high, mask, drift, drift_low, drift_high, place, out, stokes, near):
+    first_bin = me[0] * OWN
+    sea = mask[...].astype(F32)
+    out[...] = inside[...]
+    for i in range(OWN):
+        along_y = speeds[BINS + first_bin + i]
+        forward = jnp.maximum(along_y, 0.0) * (1.0 / 6.0)
+        backward = jnp.minimum(along_y, 0.0) * (1.0 / 6.0)
+        r2, r1 = low[2 * i : 2 * i + 1, :], low[2 * i + 1 : 2 * i + 2, :]
+        u1, u2 = high[2 * i : 2 * i + 1, :], high[2 * i + 1 : 2 * i + 2, :]
+        lower = jnp.concatenate([forward * (r2 - 6.0 * r1) - backward * (2.0 * r1), forward * r1], axis=0)
+        upper = jnp.concatenate([-backward * u1, forward * (2.0 * u1) + backward * (6.0 * u1 - u2)], axis=0)
+        out[i, 0:2, :] = inside[i, 0:2, :] - sea[0:2] * lower
+        out[i, 14:16, :] = inside[i, 14:16, :] - sea[14:16] * upper
+
     near[...] = jnp.zeros_like(near)
     near[0:16, :] = drift_low[...]
     near[16:64, :] = drift[...]
@@ -337,15 +366,37 @@
 
     smem = pl.BlockSpec(memory_space=pltpu.SMEM)
     vmem = pl.BlockSpec(memory_space=pltpu.VMEM)
+    hbm = pl.BlockSpec(memory_space=pltpu.HBM)
     grant = pltpu.CompilerParams(vmem_limit_bytes=16 * 1024 * 1024)
     sent, masks = pl.pallas_call(
         pack_kernel,
         out_shape=shapes((4 * OWNERS, 128), (OWNERS, 128)),
-        scratch_shapes=[pltpu.VMEM((128, NLON), F32), pltpu.VMEM((NLON, 128), F32), pltpu.VMEM((NLON, 128), F32)],
+        in_specs=[hbm] * 3,
+        scratch_shapes=[
+            pltpu.VMEM(spectrum.shape, F32),
+            pltpu.VMEM(sea_mask.shape, jnp.int32),
+            pltpu.VMEM(current.shape, F32),
+            pltpu.VMEM((128, NLON), F32),
+            pltpu.VMEM((NLON, 128), F32),
+            pltpu.VMEM((NLON, 128), F32),
+            pltpu.SemaphoreType.DMA((3,)),
+        ],
+        compiler_params=pltpu.CompilerParams(vmem_limit_bytes=60 * 1024 * 1024),
+    )(spectrum, sea_mask, current)
+
+    plus, minus, sent = lax.optimization_barrier((partner_plus, partner_minus, sent))
+    arrived = lax.all_to_all(sent.reshape(OWNERS, 1, 512), "bins", 0, 0).reshape(4 * OWNERS, 128)
+    tables = (jnp.asarray(stencil), jnp.asarray(speeds), jnp.asarray(table))
+    tables = pl.pallas_call(
+        partners_kernel,
+        out_shape=[
+            jax.ShapeDtypeStruct((2 * BINS, BINS), BF16),
+            jax.ShapeDtypeStruct((BINS, BINS), BF16),
+            *(jax.ShapeDtypeStruct(t.shape, t.dtype) for t in tables),
+        ],
         compiler_params=grant,
-    )(spectrum, sea_mask, current)
-
-    arrived = lax.all_to_all(sent.reshape(OWNERS, 1, 512), "bins", 0, 0).reshape(4 * OWNERS, 128)
+        cost_estimate=pl.CostEstimate(flops=8 * BINS * BINS, bytes_accessed=6 * BINS * BINS, transcendentals=0),
+    )(plus.reshape(1, BINS), minus.reshape(1, BINS), *tables)
     to_east, to_west, to_above, to_below = pl.pallas_call(
         edges_kernel,
         out_shape=shapes((288, 128), (288, 128), (OWNERS, 128), (OWNERS, 128)),
@@ -361,13 +412,9 @@
         points_kernel,
         out_shape=shapes((4 * OWNERS, 128), (48, 128)),
         in_specs=[smem] + [vmem] * 11,
-        scratch_shapes=[big, big, big, pltpu.VMEM((BINS, 128), BF16), big, big],
-        compiler_params=pltpu.CompilerParams(vmem_limit_bytes=32 * 1024 * 1024),
-    )(
-        device, arrived, from_west, from_east, from_below, from_above, masks,
-        partner_plus.reshape(1, BINS), partner_minus.reshape(1, BINS),
-        jnp.asarray(speeds), jnp.asarray(stencil), jnp.asarray(table),
-    )
+        scratch_shapes=[big, big, big, pltpu.VMEM((BINS, 128), BF16)],
+        compiler_params=pltpu.CompilerParams(vmem_limit_bytes=24 * 1024 * 1024),
+    )(device, arrived, from_west, from_east, from_below, from_above, masks, *tables)
 
     arrived = lax.all_to_all(sent.reshape(OWNERS, 1, 512), "bins", 0, 0).reshape(4 * OWNERS, 128)
     drift_low = lax.ppermute(drift[32:48], "bins", east)
@@ -386,16 +433,22 @@
     col = jnp.arange(6, dtype=jnp.int32)[:, None] // 2 + source_map % 3
     place = jnp.where(row < 0, 80 + col, jnp.where(row > 15, 88 + col, 16 * col + row))
     place = jnp.pad(place.reshape(1, 192), ((0, 0), (0, 64))).astype(F32)
+    speed_refs = jnp.asarray(speed_list)
+    inside = pl.pallas_call(
+        inside_kernel,
+        out_shape=jax.ShapeDtypeStruct((OWN, ROWS, NLON), F32),
+        in_specs=[smem, smem] + [vmem] * 3,
+        scratch_shapes=[pltpu.VMEM((32, NLON), F32)],
+        compiler_params=grant,
+        cost_estimate=pl.CostEstimate(flops=60 * OWN * ROWS * NLON, bytes_accessed=8 * OWN * ROWS * NLON, transcendentals=0),
+    )(device, speed_refs, middle, zonal_all, sea_mask)
     second, stokes = pl.pallas_call(
         final_kernel,
         out_shape=shapes((OWN, ROWS, NLON), (2, 192, 64)),
-        in_specs=[smem, smem] + [vmem] * 9,
-        scratch_shapes=[pltpu.VMEM((32, NLON), F32), pltpu.VMEM((128, 128), F32)],
+        in_specs=[smem, smem] + [vmem] * 8,
+        scratch_shapes=[pltpu.VMEM((128, 128), F32)],
         compiler_params=grant,
-    )(
-        device, jnp.asarray(speed_list), middle, zonal_all, from_below, from_above, sea_mask,
-        drift, drift_low, drift_high, place,
-    )
+    )(device, speed_refs, inside, from_below, from_above, sea_mask, drift, drift_low, drift_high, place)
     return second, stokes.reshape(2, 6, 32, LEV).transpose(0, 3, 1, 2)
 
 

time: 114 us -> 117 us (1.026)
  the two profiles are of different devices: /device:TPU:9 before, /device:TPU:33 now
where the time goes in v3:
time: 117 us; the launch traced here: 116 us
  starting transfers between devices  40.2 us (34%)
  blocking collectives  40.1 us (34%)
  waiting for transfers between devices  15.2 us (13%)
  Pallas kernels  14.1 us (12%)
  local copies, waits for them, and re-layouts  5.3 us (5%)
    all_to_all x1, blocking collectives, on_device(): lax.all_to_all(sent.reshape(OWNERS, 1, 512), 'bins', 0, 0)  40.1 us
    all_to_all x1, waiting for transfers between devices, on_device(): lax.all_to_all(sent.reshape(OWNERS, 1, 512), 'bins', 0, 0)  8.56 us
    ppermute x1, starting transfers between devices, on_device(): from_below = lax.ppermute(to_above, 'lat', up)  8.36 us
    pallas_call x1, Pallas kernels, on_device(): pl.pallas_call(points_kernel, out_shape=shapes((4 * OWNERS, 128), (48, 12...  5.97 us
    all_to_all x1, starting transfers between devices, on_device(): lax.all_to_all(sent.reshape(OWNERS, 1, 512), 'bins', 0, 0)  5.83 us
    ppermute x1, starting transfers between devices, on_device(): from_below = lax.ppermute(high, 'lat', up)  5.62 us
    ppermute x1, starting transfers between devices, on_device(): from_east = lax.ppermute(to_west, 'bins', west)  5.31 us
    ppermute x1, starting transfers between devices, on_device(): drift_high = lax.ppermute(drift[0:16], 'bins', west)  5.2 us
  transfers between devices with their start and end apart: 9, of which 3 were waited for; matrix products, arithmetic and copies ran while one was open for 1% of the time, Pallas kernels for 3%

profile of v3, /device:TPU:33, one launch (start us, length us, event | category | flops | bytes accessed | tf_op | source)
XLA Modules:
  0.0 115.9 jit_solution(11435792603255489164)
XLA Ops:
  0.6 2.0 %shard_map.113 = (f32[512,128]{1,0:T(8,128)}, f32[128,128]{1,0:T(8,128)}) custom-call(f32[9,16,384]{2,1,0:T(8,128)} %spec_at.1, s32[16,384]{1,0:T(8,128)} %mask.3, f32[6,32]{1,0:T(8,128)} %current_at.1), custom_call_target="tpu_custom_call" | custom-call | tf_op jit(solution)/shard_map/pallas_call | solution.py:371
  2.6 40.1 %all_to_all.10 = f32[128,1,512]{2,1,0:T(1,128)S(1)} all-to-all(f32[128,1,512]{2,1,0:T(1,128)} %bitcast.11), channel_id=1, replica_groups=mesh['bins'=128,'lat'=4] {'bins'}, dimensions={0} | all-to-all | bytes 524288 | tf_op jit(solution)/shard_map/all_to_all | solution.py:388
  42.7 0.4 shard_map.114
  43.1 3.0 %collective-permute-start = (f32[288,128]{1,0:T(8,128)S(1)}, f32[288,128]{1,0:T(8,128)S(1)}, u32[]{:S(2)}, u32[]{:S(2)}) collective-permute-start(f32[288,128]{1,0:T(8,128)S(1)} %get-tuple-element.26), channel_id=1, source_target_pairs={{0,4},{4,8},{8,12},{12,16},{16,20},{20,24},{24,28},{28,32},{32,36}... | collective-permute-start | bytes 442376 | tf_op jit(solution)/shard_map/ppermute | solution.py:405
  46.1 5.3 %collective-permute-start.1 = (f32[288,128]{1,0:T(8,128)S(1)}, f32[288,128]{1,0:T(8,128)S(1)}, u32[]{:S(2)}, u32[]{:S(2)}) collective-permute-start(f32[288,128]{1,0:T(8,128)S(1)} %get-tuple-element.27), channel_id=1, source_target_pairs={{4,0},{8,4},{12,8},{16,12},{20,16},{24,20},{28,24},{32,28},{36,32}... | collective-permute-start | bytes 442376 | tf_op jit(solution)/shard_map/ppermute | solution.py:406
  51.4 8.4 %collective-permute-start.2 = (f32[128,128]{1,0:T(8,128)S(1)}, f32[128,128]{1,0:T(8,128)S(1)}, u32[]{:S(2)}, u32[]{:S(2)}) collective-permute-start(f32[128,128]{1,0:T(8,128)S(1)} %get-tuple-element.28), channel_id=1, source_target_pairs={{0,1},{1,2},{2,3},{4,5},{5,6},{6,7},{8,9},{9,10},{10,11},{12,13},{... | collective-permute-start | bytes 196616 | tf_op jit(solution)/shard_map/ppermute | solution.py:407
  59.8 1.9 %collective-permute-start.3 = (f32[128,128]{1,0:T(8,128)S(1)}, f32[128,128]{1,0:T(8,128)S(1)}, u32[]{:S(2)}, u32[]{:S(2)}) collective-permute-start(f32[128,128]{1,0:T(8,128)S(1)} %get-tuple-element.29), channel_id=1, source_target_pairs={{1,0},{2,1},{3,2},{5,4},{6,5},{7,6},{9,8},{10,9},{11,10},{13,12},{... | collective-permute-start | bytes 196616 | tf_op jit(solution)/shard_map/ppermute | solution.py:408
  61.7 0.7 reshape.108.plus
  62.4 0.7 reshape.109.minus
  63.1 1.1 copy-done
  64.2 1.1 copy-done.1
  65.3 0.8 copy-done.4
  66.1 2.4 %shard_map.115 = (bf16[2304,1152]{1,0:T(8,128)(2,1)S(1)}, bf16[1152,1152]{1,0:T(8,128)(2,1)S(1)}, bf16[128,256]{1,0:T(8,128)(2,1)S(1)}, f32[1152,128]{1,0:T(8,128)S(1)}, bf16[256,1152]{1,0:T(8,128)(2,1)S(1)}) custom-call(s32[1,1152]{1,0:T(1,128)S(1)} %reshape.108.plus, s32[1,1152]{1,0:T(1,128)S(1)} %reshape.109.minus, bf16[128,256]{1,0:T(8,128)(2,1)S(1)} %copy-done.4, ...), custom_call_target="tpu_custom_call" | custom-call | flops 10616832 | bytes 7962624 | tf_op jit(solution)/shard_map/pallas_call | solution.py:390
  68.5 0.0 copy-start.6
  68.5 0.0 collective-permute-done.2.from_below
  68.6 0.0 collective-permute-done.from_west
  68.6 0.0 copy-start.3
  68.6 0.8 copy-done.3
  69.4 6.0 %shard_map.116 = (f32[512,128]{1,0:T(8,128)}, f32[48,128]{1,0:T(8,128)S(1)}) custom-call(s32[1]{0:T(128)} %bitcast.me, f32[512,128]{1,0:T(8,128)S(1)} %bitcast.9, f32[288,128]{1,0:T(8,128)S(1)} %collective-permute-done.from_west, f32[288,128]{1,0:T(8,128)S(1)} %collective-permute-done.1.from_east, f32[128,128]{1,0:T(8,128)S(1)} %collective-permute-done.2.from_below, ...), custom_call_target="tpu_custom_call" | custom-call | tf_op jit(solution)/shard_map/pallas_call | solution.py:411
  75.4 5.8 %all-to-all-start.1 = ((f32[128,1,512]{2,1,0:T(1,128)}), f32[128,1,512]{2,1,0:T(1,128)S(1)}, u32[]{:S(2)}, u32[]{:S(2)}) async-start(f32[128,1,512]{2,1,0:T(1,128)} %bitcast.3), calls=%async_computation.1 | async-start | bytes 524288 | tf_op jit(solution)/shard_map/all_to_all | solution.py:419
  81.3 3.1 %collective-permute-start.4 = (f32[16,128]{1,0:T(8,128)S(1)}, f32[16,128]{1,0:T(8,128)S(1)}, u32[]{:S(2)}, u32[]{:S(2)}) collective-permute-start(f32[16,128]{1,0:T(8,128)S(1)} %get-tuple-element.47), channel_id=1, source_target_pairs={{0,4},{4,8},{8,12},{12,16},{16,20},{20,24},{24,28},{28,32},{32,36}... | collective-permute-start | bytes 24584 | tf_op jit(solution)/shard_map/ppermute | solution.py:420
  84.4 5.2 %collective-permute-start.5 = (f32[16,128]{1,0:T(8,128)S(1)}, f32[16,128]{1,0:T(8,128)S(1)}, u32[]{:S(2)}, u32[]{:S(2)}) collective-permute-start(f32[16,128]{1,0:T(8,128)S(1)} %get-tuple-element.46), channel_id=1, source_target_pairs={{4,0},{8,4},{12,8},{16,12},{20,16},{24,20},{28,24},{32,28},{36,32}... | collective-permute-start | bytes 24584 | tf_op jit(solution)/shard_map/ppermute | solution.py:421
  89.6 0.1 select_select_fusion
  89.7 0.1 reshape.112
  89.7 3.1 %collective-permute-done.4.drift_low = f32[16,128]{1,0:T(8,128)S(1)} collective-permute-done((f32[16,128]{1,0:T(8,128)S(1)}, f32[16,128]{1,0:T(8,128)S(1)}, u32[]{:S(2)}, u32[]{:S(2)}) %collective-permute-start.4) | collective-permute-done | bytes 8224 | tf_op jit(solution)/shard_map/ppermute | solution.py:420
  92.9 8.6 %all-to-all-done.1 = f32[128,1,512]{2,1,0:T(1,128)S(1)} async-done(((f32[128,1,512]{2,1,0:T(1,128)}), f32[128,1,512]{2,1,0:T(1,128)S(1)}, u32[]{:S(2)}, u32[]{:S(2)}) %all-to-all-start.1) | async-done | bytes 262176 | tf_op jit(solution)/shard_map/all_to_all | solution.py:419
  101.5 0.2 shard_map.117
  101.7 5.6 %collective-permute-start.6 = (f32[24,384]{1,0:T(8,128)S(1)}, f32[24,384]{1,0:T(8,128)S(1)}, u32[]{:S(2)}, u32[]{:S(2)}) collective-permute-start(f32[24,384]{1,0:T(8,128)S(1)} %get-tuple-element.42), channel_id=1, source_target_pairs={{0,1},{1,2},{2,3},{4,5},{5,6},{6,7},{8,9},{9,10},{10,11},{12,13},{... | collective-permute-start | bytes 110600 | tf_op jit(solution)/shard_map/ppermute | solution.py:429
  107.3 1.9 %collective-permute-start.7 = (f32[24,384]{1,0:T(8,128)S(1)}, f32[24,384]{1,0:T(8,128)S(1)}, u32[]{:S(2)}, u32[]{:S(2)}) collective-permute-start(f32[24,384]{1,0:T(8,128)S(1)} %get-tuple-element.43), channel_id=1, source_target_pairs={{1,0},{2,1},{3,2},{5,4},{6,5},{7,6},{9,8},{10,9},{11,10},{13,12},{... | collective-permute-start | bytes 110600 | tf_op jit(solution)/shard_map/ppermute | solution.py:430
  109.3 1.4 %shard_map.118.inside = f32[9,16,384]{2,1,0:T(8,128)S(1)} custom-call(s32[1]{0:T(128)} %bitcast.me, f32[2304]{0:T(1024)S(1)} %copy-done.5, f32[144,384]{1,0:T(8,128)S(1)} %get-tuple-element.40.middle, f32[16,384]{1,0:T(8,128)S(1)} %get-tuple-element.41.zonal, s32[16,384]{1,0:T(8,128)S(1)} %copy-done.2), custom_call_target="tpu_custom_call" | custom-call | flops 3317760 | bytes 442368 | tf_op jit(solution)/shard_map/pallas_call | solution.py:437
  110.6 3.5 %collective-permute-done.7.high = f32[24,384]{1,0:T(8,128)S(1)} collective-permute-done((f32[24,384]{1,0:T(8,128)S(1)}, f32[24,384]{1,0:T(8,128)S(1)}, u32[]{:S(2)}, u32[]{:S(2)}) %collective-permute-start.7) | collective-permute-done | bytes 36896 | tf_op jit(solution)/shard_map/ppermute | solution.py:430
  114.1 1.8 %shard_map.119 = (f32[9,16,384]{2,1,0:T(8,128)}, f32[2,192,64]{2,1,0:T(8,128)}) custom-call(s32[1]{0:T(128)} %bitcast.me, f32[2304]{0:T(1024)S(1)} %copy-done.5, f32[9,16,384]{2,1,0:T(8,128)S(1)} %shard_map.118.inside, f32[24,384]{1,0:T(8,128)S(1)} %collective-permute-done.6.low, f32[24,384]{1,0:T(8,128)S(1)} %collective-permute-done.7.high, ...), custom_call_target="tpu_custom_call" | custom-call | tf_op jit(solution)/shard_map/pallas_call | solution.py:445
  (16 shorter events, 0.0 us)
Async XLA Ops:
  43.1 25.4 %collective-permute-start = (f32[288,128]{1,0:T(8,128)S(1)}, f32[288,128]{1,0:T(8,128)S(1)}, u32[]{:S(2)}, u32[]{:S(2)}) collective-permute-start(f32[288,128]{1,0:T(8,128)S(1)} %get-tuple-element.26), channel_id=1, source_target_pairs={{0,4},{4,8},{8,12},{12,16},{16,20},{20,24},{24,28},{28,32},{32,36}... | collective-permute-start | bytes 442376 | tf_op jit(solution)/shard_map/ppermute | solution.py:405
  46.1 22.5 %collective-permute-start.1 = (f32[288,128]{1,0:T(8,128)S(1)}, f32[288,128]{1,0:T(8,128)S(1)}, u32[]{:S(2)}, u32[]{:S(2)}) collective-permute-start(f32[288,128]{1,0:T(8,128)S(1)} %get-tuple-element.27), channel_id=1, source_target_pairs={{4,0},{8,4},{12,8},{16,12},{20,16},{24,20},{28,24},{32,28},{36,32}... | collective-permute-start | bytes 442376 | tf_op jit(solution)/shard_map/ppermute | solution.py:406
  51.4 17.1 %collective-permute-start.2 = (f32[128,128]{1,0:T(8,128)S(1)}, f32[128,128]{1,0:T(8,128)S(1)}, u32[]{:S(2)}, u32[]{:S(2)}) collective-permute-start(f32[128,128]{1,0:T(8,128)S(1)} %get-tuple-element.28), channel_id=1, source_target_pairs={{0,1},{1,2},{2,3},{4,5},{5,6},{6,7},{8,9},{9,10},{10,11},{12,13},{... | collective-permute-start | bytes 196616 | tf_op jit(solution)/shard_map/ppermute | solution.py:407
  59.8 8.8 %collective-permute-start.3 = (f32[128,128]{1,0:T(8,128)S(1)}, f32[128,128]{1,0:T(8,128)S(1)}, u32[]{:S(2)}, u32[]{:S(2)}) collective-permute-start(f32[128,128]{1,0:T(8,128)S(1)} %get-tuple-element.29), channel_id=1, source_target_pairs={{1,0},{2,1},{3,2},{5,4},{6,5},{7,6},{9,8},{10,9},{11,10},{13,12},{... | collective-permute-start | bytes 196616 | tf_op jit(solution)/shard_map/ppermute | solution.py:408
  63.1 1.1 copy-start
  64.2 1.1 copy-start.1
  65.3 0.8 copy-start.4
  68.5 21.0 %copy-start.6 = (s32[6,32]{1,0:T(8,128)S(1)}, s32[6,32]{1,0:T(8,128)}, u32[]{:S(2)}) copy-start(s32[6,32]{1,0:T(8,128)} %param.15) | copy-start | bytes 2308
  68.6 0.8 copy-start.3
  69.4 39.8 %copy-start.2 = (s32[16,384]{1,0:T(8,128)S(1)}, s32[16,384]{1,0:T(8,128)}, u32[]{:S(2)}) copy-start(s32[16,384]{1,0:T(8,128)} %mask.3) | copy-start | bytes 73732
  69.4 39.8 %copy-start.5 = (f32[2304]{0:T(1024)S(1)}, f32[2304]{0:T(1024)}, u32[]{:S(2)}) copy-start(f32[2304]{0:T(1024)} %constant.73.clone.speeds) | copy-start | bytes 27652
  75.4 26.1 %all-to-all-start.1 = ((f32[128,1,512]{2,1,0:T(1,128)}), f32[128,1,512]{2,1,0:T(1,128)S(1)}, u32[]{:S(2)}, u32[]{:S(2)}) async-start(f32[128,1,512]{2,1,0:T(1,128)} %bitcast.3), calls=%async_computation.1 | async-start | bytes 524288 | tf_op jit(solution)/shard_map/all_to_all | solution.py:419
  81.3 11.6 %collective-permute-start.4 = (f32[16,128]{1,0:T(8,128)S(1)}, f32[16,128]{1,0:T(8,128)S(1)}, u32[]{:S(2)}, u32[]{:S(2)}) collective-permute-start(f32[16,128]{1,0:T(8,128)S(1)} %get-tuple-element.47), channel_id=1, source_target_pairs={{0,4},{4,8},{8,12},{12,16},{16,20},{20,24},{24,28},{28,32},{32,36}... | collective-permute-start | bytes 24584 | tf_op jit(solution)/shard_map/ppermute | solution.py:420
  84.4 8.5 %collective-permute-start.5 = (f32[16,128]{1,0:T(8,128)S(1)}, f32[16,128]{1,0:T(8,128)S(1)}, u32[]{:S(2)}, u32[]{:S(2)}) collective-permute-start(f32[16,128]{1,0:T(8,128)S(1)} %get-tuple-element.46), channel_id=1, source_target_pairs={{4,0},{8,4},{12,8},{16,12},{20,16},{24,20},{28,24},{32,28},{36,32}... | collective-permute-start | bytes 24584 | tf_op jit(solution)/shard_map/ppermute | solution.py:421
  101.7 9.0 %collective-permute-start.6 = (f32[24,384]{1,0:T(8,128)S(1)}, f32[24,384]{1,0:T(8,128)S(1)}, u32[]{:S(2)}, u32[]{:S(2)}) collective-permute-start(f32[24,384]{1,0:T(8,128)S(1)} %get-tuple-element.42), channel_id=1, source_target_pairs={{0,1},{1,2},{2,3},{4,5},{5,6},{6,7},{8,9},{9,10},{10,11},{12,13},{... | collective-permute-start | bytes 110600 | tf_op jit(solution)/shard_map/ppermute | solution.py:429
  107.3 6.8 %collective-permute-start.7 = (f32[24,384]{1,0:T(8,128)S(1)}, f32[24,384]{1,0:T(8,128)S(1)}, u32[]{:S(2)}, u32[]{:S(2)}) collective-permute-start(f32[24,384]{1,0:T(8,128)S(1)} %get-tuple-element.43), channel_id=1, source_target_pairs={{1,0},{2,1},{3,2},{5,4},{6,5},{7,6},{9,8},{10,9},{11,10},{13,12},{... | collective-permute-start | bytes 110600 | tf_op jit(solution)/shard_map/ppermute | solution.py:430

commit v4 on v3

--- a/solution.py
+++ b/solution.py
@@ -6,6 +6,7 @@
 from jax import lax
 from jax.experimental import pallas as pl
 from jax.experimental.pallas import tpu as pltpu
+from jax.sharding import Mesh
 from jax.sharding import PartitionSpec as P
 
 NDIR = 36
@@ -16,6 +17,9 @@
 ROWS = 16
 NLON = 384
 OWNERS = 128
+BANDS = 4
+ALONG_BINS = ("z", "y", "x")
+EXCHANGE = ("z", "x", "y")
 COLS = 3
 F32 = jnp.float32
 BF16 = jnp.bfloat16
@@ -30,10 +34,10 @@
     speeds = np.repeat(0.12 + 0.25 * (NFREQ - 1 - j) / (NFREQ - 1), NDIR)
     cosines, sines = np.tile(np.cos(angles), NFREQ), np.tile(np.sin(angles), NFREQ)
     strength = np.repeat(0.06 * (1.0 + j / (NFREQ - 1)), NDIR)
-    levels = np.arange(LEV) + 0.5
-    decay = np.repeat(np.exp(-levels[:, None] * (0.02 * 1.15**j)[None, :]), NDIR, axis=1)
-    drift = 2.0 / math.sqrt(BINS) * np.concatenate([decay * cosines, decay * sines], axis=0)
-    return speeds * cosines, speeds * sines, strength, drift
+    wavenumber = np.repeat(0.02 * 1.15**j, NDIR)
+    amplitude = 2.0 / math.sqrt(BINS)
+    rows = (speeds * cosines, speeds * sines, strength, -wavenumber, amplitude * cosines, amplitude * sines)
+    return np.stack(rows).astype(np.float32)
 
 
 def stencils():
@@ -66,20 +70,25 @@
     return lax.broadcasted_iota(jnp.int32, (rows, 128), 1)
 
 
+def exchange_place(device):
+    return (device & -8) | ((device & 3) << 1) | ((device >> 2) & 1)
+
+
+def device_at(place):
+    return (place & -8) | ((place & 1) << 2) | ((place >> 1) & 3)
+
+
+def bin_at(row):
+    place = (row * 7282) >> 16
+    return device_at(place) * OWN + row - place * OWN
+
+
 def split_beside(x):
     upper = x.astype(BF16).astype(F32)
     return (upper + pltpu.roll(x - upper, 64, 1)).astype(BF16)
 
 
-def pack_kernel(spec_at, mask_at, current_at, out, mask_out, spec, mask, current, stack, turned, turned2, done):
-    copies = [
-        pltpu.make_async_copy(source, held, done.at[k])
-        for k, (source, held) in enumerate(((spec_at, spec), (mask_at, mask), (current_at, current)))
-    ]
-    for copy in copies:
-        copy.start()
-    for copy in copies:
-        copy.wait()
+def pack_kernel(spec, mask, current, out, mask_out, stack, turned, turned2, held):
     sea = mask[...].astype(F32)
     masked = spec[...] * sea[None]
     stack[0:16, :] = masked[8]
@@ -95,17 +104,20 @@
     rest = jnp.zeros((OWNERS, 128), F32)
     sea_rows = jnp.zeros((OWNERS, 128), F32)
     for c in range(COLS):
-        out[pl.ds(c, OWNERS, stride=4), :] = turned[pl.ds(c, OWNERS, stride=COLS), :]
+        for j in range(8):
+            out[pl.ds(4 * exchange_place(j) + c, 16, stride=32), :] = turned[pl.ds(COLS * j + c, 16, stride=8 * COLS), :]
         column = turned2[pl.ds(c, OWNERS, stride=COLS), :]
         zonal = sums[2 * c : 2 * c + 1] + sums[2 * c + 1 : 2 * c + 2]
         rest = jnp.where(group == 2 * c, pltpu.roll(column, 32 * c, 1), rest)
         rest = jnp.where(group == 2 * c + 1, jnp.broadcast_to(zonal, rest.shape), rest)
         sea_rows = jnp.where(group == c, pltpu.roll(column, (16 * c - 16) % 128, 1), sea_rows)
-    out[pl.ds(3, OWNERS, stride=4), :] = rest
+    held[...] = rest
+    for j in range(8):
+        out[pl.ds(4 * exchange_place(j) + 3, 16, stride=32), :] = held[pl.ds(j, 16, stride=8), :]
     mask_out[...] = sea_rows
 
 
-def edges_kernel(arrived, to_east, to_west, to_above, to_below):
+def edges_kernel(band, arrived, to_east, to_west, to_bands):
     def part(c):
         return arrived[pl.ds(c, OWNERS, stride=4), :]
 
@@ -124,7 +136,9 @@
             moved = pltpu.roll(pair[32 * q : 32 * q + 32], 32 * q, 1)
             last = jnp.where(group[0:32] // 2 == q, moved, last)
         ref[256:288, :] = last
-    for ref, r in ((to_above, 14), (to_below, 0)):
+    here = band[0]
+    to_bands[...] = jnp.zeros_like(to_bands)
+    for target, r in ((jnp.minimum(here + 1, BANDS - 1), 14), (jnp.maximum(here - 1, 0), 0)):
         acc = jnp.zeros((OWNERS, 128), F32)
         for c in range(COLS):
             moved = pltpu.roll(part(c), (2 * c - r) % 128, 1)
@@ -132,36 +146,21 @@
         for c in range(COLS):
             moved = pltpu.roll(rest, (6 + 2 * c - 32 * c - r) % 128, 1)
             acc = jnp.where((lane >= 6 + 2 * c) & (lane < 8 + 2 * c), moved, acc)
-        ref[...] = acc
-
-
-def partners_kernel(plus, minus, stencil_in, speeds_in, table_in, picks, hits, stencil, speeds, table):
-    stencil[...] = stencil_in[...]
-    speeds[...] = speeds_in[...]
-    table[...] = table_in[...]
-    numbers = lax.broadcasted_iota(jnp.int32, (128, BINS), 1).astype(F32)
-    for t in range(OWN):
-        rows = slice(128 * t, 128 * t + 128)
-        for k, row in enumerate((plus, minus)):
-            column = jnp.broadcast_to(row[:, rows].astype(F32), (128, 128)).T
-            wide = jnp.concatenate([column] * OWN, axis=1)
-            picks[BINS * k + 128 * t : BINS * k + 128 * t + 128, :] = jnp.where(wide == numbers, 1.0, 0.0).astype(BF16)
-        names = lax.broadcasted_iota(jnp.int32, (128, BINS), 0) + 128 * t
-        both = jnp.where(plus[...] == names, 1.0, 0.0) + jnp.where(minus[...] == names, 1.0, 0.0)
-        hits[rows, :] = both.astype(BF16)
+        to_bands[pl.ds(pl.multiple_of(target * OWNERS, OWNERS), OWNERS), :] = acc
+    to_bands[pl.ds(pl.multiple_of(here * OWNERS, OWNERS), OWNERS), :] = jnp.zeros((OWNERS, 128), F32)
 
 
 def points_kernel(
-    me, arrived, from_west, from_east, from_below, from_above, masks, picks, hits, stencil, speeds, table,
-    out, drift_out, first, source, middle, halves,
+    me, arrived, from_west, from_east, from_bands, masks, plus, minus, stencil, values,
+    out, drift_out, first, source, middle, halves, speeds, plus_col, minus_col,
 ):
     device = me[0]
     lane = lanes(OWNERS)
     group = lane // 16
 
-    flow = arrived[pl.ds(4 * device + 3, 1), :]
-    below = arrived[pl.ds(4 * jnp.maximum(device - 1, 0) + 3, 1), :]
-    above = arrived[pl.ds(4 * jnp.minimum(device + 1, OWNERS - 1) + 3, 1), :]
+    flow = arrived[pl.ds(4 * exchange_place(device) + 3, 1), :]
+    below = arrived[pl.ds(4 * exchange_place(jnp.maximum(device - 1, 0)) + 3, 1), :]
+    above = arrived[pl.ds(4 * exchange_place(jnp.minimum(device + 1, OWNERS - 1)) + 3, 1), :]
     lower = jnp.where(device > 0, pltpu.roll(below, 48, 1), 0.0)
     upper = jnp.where(device < OWNERS - 1, pltpu.roll(above, 32, 1), 0.0)
     lane1 = lanes()
@@ -174,6 +173,9 @@
 
     def chunk(t):
         return slice(128 * t, 128 * t + 128)
+
+    def band_rows(band):
+        return from_bands[pl.ds(pl.multiple_of(band * OWNERS, OWNERS), OWNERS), :]
 
     for i in range(OWN):
         acc = jnp.zeros((OWNERS, 128), F32)
@@ -195,10 +197,12 @@
                 part = pltpu.roll(part, (16 * g - 16 * i) % 128, 1)
             acc = jnp.where(group == g, part, acc)
         held = 16 * i if i < 8 else 6
-        for ref, at in ((from_below, 112), (from_above, 118)):
-            acc = jnp.where((lane >= at) & (lane < at + 6), pltpu.roll(ref[...], (at - held) % 128, 1), acc)
+        for band, at in ((jnp.maximum(me[1] - 1, 0), 112), (jnp.minimum(me[1] + 1, BANDS - 1), 118)):
+            beyond = pltpu.roll(band_rows(band), (at - held) % 128, 1)
+            acc = jnp.where((lane >= at) & (lane < at + 6), beyond, acc)
         middle[pl.ds(i, OWNERS, stride=OWN), :] = acc
 
+    inner = lax.broadcasted_iota(jnp.int32, (128, 128), 0)
     for t in range(OWN):
         value = middle[chunk(t), :]
         upper_half = value.astype(BF16)
@@ -206,6 +210,10 @@
         sums = jnp.dot(upper_half, stencil[...], preferred_element_type=F32) + jnp.dot(
             lower_half, stencil[...], preferred_element_type=F32
         )
+        part = jnp.where(inner < 64, values[0:1, chunk(t)], values[1:2, chunk(t)])
+        speeds[chunk(t), :] = jnp.where(inner == 127, values[2:3, chunk(t)], part).T
+        for row, col in ((plus, plus_col), (minus, minus_col)):
+            col[chunk(t), :] = jnp.broadcast_to(row[:, chunk(t)].astype(F32), (128, 128)).T
         speed = (speeds[chunk(t), :] + faces) * (1.0 / 6.0)
         flux = jnp.maximum(speed, 0.0) * sums[:, 0:128] + jnp.minimum(speed, 0.0) * sums[:, 128:256]
         change = (pltpu.roll(flux, 112, 1) - flux) + pltpu.roll(flux, 64, 1)
@@ -214,27 +222,39 @@
         first[chunk(t), :] = moved
         halves[chunk(t), :] = split_beside(moved)
 
-    def gathered(at):
-        both = jnp.dot(picks[at : at + 128, :], halves[...], preferred_element_type=F32)
+    numbers = bin_at(lax.broadcasted_iota(jnp.int32, (128, BINS), 1)).astype(F32)
+
+    def gathered(col, t):
+        wide = jnp.concatenate([col[chunk(t), :]] * OWN, axis=1)
+        chosen = jnp.where(wide == numbers, 1.0, 0.0).astype(BF16)
+        both = jnp.dot(chosen, halves[...], preferred_element_type=F32)
         return both + pltpu.roll(both, 64, 1)
 
     for t in range(OWN):
-        ahead = gathered(128 * t)
-        behind = gathered(BINS + 128 * t)
+        ahead = gathered(plus_col, t)
+        behind = gathered(minus_col, t)
         f = first[chunk(t), :]
         strength = jnp.broadcast_to(speeds[chunk(t), 127:128], (128, 128))
         source[chunk(t), :] = strength * (f * f * (ahead + behind) - 2.0 * f * ahead * behind)
     for t in range(OWN):
         halves[chunk(t), :] = split_beside(source[chunk(t), :])
     for t in range(OWN):
-        both = jnp.dot(hits[chunk(t), :], halves[...], preferred_element_type=F32)
+        names = bin_at(inner + 128 * t)
+        names = jnp.concatenate([names] * OWN, axis=1)
+        hits = jnp.where(plus[...] == names, 1.0, 0.0) + jnp.where(minus[...] == names, 1.0, 0.0)
+        both = jnp.dot(hits.astype(BF16), halves[...], preferred_element_type=F32)
         back = both + pltpu.roll(both, 64, 1)
         m = first[chunk(t), :] + (source[chunk(t), :] - 0.5 * back)
         middle[chunk(t), :] = jnp.where(lane < 48, m, 0.0)
     for t in range(OWN):
         halves[chunk(t), :] = split_beside(middle[chunk(t), :])
-    sums = jnp.dot(table[...], halves[...], preferred_element_type=F32)
-    drift = sums[0:128] + pltpu.roll(sums[0:128], 64, 1) + sums[128:256]
+    level = lax.broadcasted_iota(jnp.int32, (LEV, BINS), 0).astype(F32) + 0.5
+    decay = jnp.exp(level * values[3:4, :])
+    table = jnp.concatenate([decay * values[4:5, :], decay * values[5:6, :]], axis=0)
+    table_upper = table.astype(BF16)
+    table_lower = (table - table_upper.astype(F32)).astype(BF16)
+    sums = jnp.dot(table_upper, halves[...], preferred_element_type=F32)
+    drift = sums + pltpu.roll(sums, 64, 1) + jnp.dot(table_lower, halves[...], preferred_element_type=F32)
     drift_out[...] = drift.T[0:48]
 
     for c in range(COLS):
@@ -251,10 +271,12 @@
 
 
 def unpack_kernel(arrived, drift, drift_low, drift_high, middle, zonal, low, high, turned, turned2):
-    for c in range(COLS):
-        turned[pl.ds(c, OWNERS, stride=COLS), :] = arrived[pl.ds(c, OWNERS, stride=4), :]
-        rest = arrived[pl.ds(3, OWNERS, stride=4), :]
-        turned2[pl.ds(c, OWNERS, stride=COLS), :] = pltpu.roll(rest, (128 - 32 * c) % 128, 1)
+    for j in range(8):
+        place = 4 * exchange_place(j)
+        rest = arrived[pl.ds(place + 3, 16, stride=32), :]
+        for c in range(COLS):
+            turned[pl.ds(COLS * j + c, 16, stride=8 * COLS), :] = arrived[pl.ds(place + c, 16, stride=32), :]
+            turned2[pl.ds(COLS * j + c, 16, stride=8 * COLS), :] = pltpu.roll(rest, (128 - 32 * c) % 128, 1)
     middle[0:128, :] = turned[...].T
     rest = turned2[...].T
     middle[128:144, :] = rest[0:16]
@@ -341,84 +363,69 @@
     stokes[1] = total[:, 64:128]
 
 
+def in_exchange_order(partner):
+    return partner.reshape(16, 2, 4, OWN).transpose(0, 2, 1, 3).reshape(1, BINS)
+
+
 def shapes(*sizes):
     return [jax.ShapeDtypeStruct(size, F32) for size in sizes]
 
 
 def on_device(spectrum, sea_mask, current, partner_plus, partner_minus, source_map):
-    along_x, along_y, strength, drift_table = bin_values()
-    speeds = np.zeros((BINS, 128), np.float32)
-    speeds[:, 0:64] = along_x[:, None]
-    speeds[:, 64:112] = along_y[:, None]
-    speeds[:, 127] = strength
-    speed_list = np.concatenate([along_x, along_y]).astype(np.float32)
-    drift_upper = drift_table.astype(np.float32).astype(BF16)
-    drift_lower = (drift_table.astype(np.float32) - drift_upper.astype(np.float32)).astype(BF16)
-    table = np.concatenate([drift_upper, drift_lower], axis=0)
+    values = bin_values()
+    speed_list = values[0:2].reshape(-1)
+    held_values = np.concatenate([values[:, bin_at(np.arange(BINS))], np.zeros((2, BINS), np.float32)])
     stencil = stencils().astype(BF16)
 
-    device = lax.axis_index("bins").reshape(1)
-    bands = lax.axis_size("lat")
-    up = [(i, i + 1) for i in range(bands - 1)]
-    down = [(i + 1, i) for i in range(bands - 1)]
+    device = lax.axis_index(ALONG_BINS).reshape(1)
+    band = lax.axis_index("lat").reshape(1)
+    me = jnp.concatenate([device, band])
+    up = [(i, i + 1) for i in range(BANDS - 1)]
+    down = [(i + 1, i) for i in range(BANDS - 1)]
     east = [(i, i + 1) for i in range(OWNERS - 1)]
     west = [(i + 1, i) for i in range(OWNERS - 1)]
 
     smem = pl.BlockSpec(memory_space=pltpu.SMEM)
     vmem = pl.BlockSpec(memory_space=pltpu.VMEM)
-    hbm = pl.BlockSpec(memory_space=pltpu.HBM)
     grant = pltpu.CompilerParams(vmem_limit_bytes=16 * 1024 * 1024)
     sent, masks = pl.pallas_call(
         pack_kernel,
         out_shape=shapes((4 * OWNERS, 128), (OWNERS, 128)),
-        in_specs=[hbm] * 3,
         scratch_shapes=[
-            pltpu.VMEM(spectrum.shape, F32),
-            pltpu.VMEM(sea_mask.shape, jnp.int32),
-            pltpu.VMEM(current.shape, F32),
             pltpu.VMEM((128, NLON), F32),
             pltpu.VMEM((NLON, 128), F32),
             pltpu.VMEM((NLON, 128), F32),
-            pltpu.SemaphoreType.DMA((3,)),
-        ],
-        compiler_params=pltpu.CompilerParams(vmem_limit_bytes=60 * 1024 * 1024),
-    )(spectrum, sea_mask, current)
-
-    plus, minus, sent = lax.optimization_barrier((partner_plus, partner_minus, sent))
-    arrived = lax.all_to_all(sent.reshape(OWNERS, 1, 512), "bins", 0, 0).reshape(4 * OWNERS, 128)
-    tables = (jnp.asarray(stencil), jnp.asarray(speeds), jnp.asarray(table))
-    tables = pl.pallas_call(
-        partners_kernel,
-        out_shape=[
-            jax.ShapeDtypeStruct((2 * BINS, BINS), BF16),
-            jax.ShapeDtypeStruct((BINS, BINS), BF16),
-            *(jax.ShapeDtypeStruct(t.shape, t.dtype) for t in tables),
+            pltpu.VMEM((OWNERS, 128), F32),
         ],
         compiler_params=grant,
-        cost_estimate=pl.CostEstimate(flops=8 * BINS * BINS, bytes_accessed=6 * BINS * BINS, transcendentals=0),
-    )(plus.reshape(1, BINS), minus.reshape(1, BINS), *tables)
-    to_east, to_west, to_above, to_below = pl.pallas_call(
+    )(spectrum, sea_mask, current)
+
+    plus, minus, sent = lax.optimization_barrier((partner_plus, partner_minus, sent))
+    arrived = lax.all_to_all(sent.reshape(OWNERS, 1, 512), EXCHANGE, 0, 0).reshape(4 * OWNERS, 128)
+    plus, minus = in_exchange_order(plus), in_exchange_order(minus)
+    arrived, plus, minus = lax.optimization_barrier((arrived, plus, minus))
+    to_east, to_west, to_bands = pl.pallas_call(
         edges_kernel,
-        out_shape=shapes((288, 128), (288, 128), (OWNERS, 128), (OWNERS, 128)),
+        out_shape=shapes((288, 128), (288, 128), (BANDS * OWNERS, 128)),
+        in_specs=[smem, vmem],
         compiler_params=grant,
-    )(arrived)
-    from_west = lax.ppermute(to_east, "bins", east)
-    from_east = lax.ppermute(to_west, "bins", west)
-    from_below = lax.ppermute(to_above, "lat", up)
-    from_above = lax.ppermute(to_below, "lat", down)
+    )(band, arrived)
+    from_west = lax.ppermute(to_east, ALONG_BINS, east)
+    from_east = lax.ppermute(to_west, ALONG_BINS, west)
+    from_bands = lax.all_to_all(to_bands.reshape(BANDS, OWNERS, 128), "lat", 0, 0).reshape(BANDS * OWNERS, 128)
 
     big = pltpu.VMEM((BINS, 128), F32)
     sent, drift = pl.pallas_call(
         points_kernel,
         out_shape=shapes((4 * OWNERS, 128), (48, 128)),
-        in_specs=[smem] + [vmem] * 11,
-        scratch_shapes=[big, big, big, pltpu.VMEM((BINS, 128), BF16)],
+        in_specs=[smem] + [vmem] * 9,
+        scratch_shapes=[big, big, big, pltpu.VMEM((BINS, 128), BF16), big, big, big],
         compiler_params=pltpu.CompilerParams(vmem_limit_bytes=24 * 1024 * 1024),
-    )(device, arrived, from_west, from_east, from_below, from_above, masks, *tables)
-
-    arrived = lax.all_to_all(sent.reshape(OWNERS, 1, 512), "bins", 0, 0).reshape(4 * OWNERS, 128)
-    drift_low = lax.ppermute(drift[32:48], "bins", east)
-    drift_high = lax.ppermute(drift[0:16], "bins", west)
+    )(me, arrived, from_west, from_east, from_bands, masks, plus, minus, jnp.asarray(stencil), jnp.asarray(held_values))
+
+    arrived = lax.all_to_all(sent.reshape(OWNERS, 1, 512), EXCHANGE, 0, 0).reshape(4 * OWNERS, 128)
+    drift_low = lax.ppermute(drift[32:48], ALONG_BINS, east)
+    drift_high = lax.ppermute(drift[0:16], ALONG_BINS, west)
 
     middle, zonal_all, low, high = pl.pallas_call(
         unpack_kernel,
@@ -453,6 +460,8 @@
 
 
 def solution(mesh):
-    in_specs = (P("bins", "lat", None), P("lat", None), P("bins", "lat"), P(), P(), P("bins", "lat"))
-    out_specs = (P("bins", "lat", None), P(None, None, "bins", "lat"))
-    return jax.shard_map(on_device, mesh=mesh, in_specs=in_specs, out_specs=out_specs, check_vma=False)
+    finer = Mesh(mesh.devices.reshape(16, 2, 4, BANDS), ALONG_BINS + ("lat",))
+    bins = ALONG_BINS
+    in_specs = (P(bins, "lat", None), P("lat", None), P(bins, "lat"), P(), P(), P(bins, "lat"))
+    out_specs = (P(bins, "lat", None), P(None, None, bins, "lat"))
+    return jax.shard_map(on_device, mesh=finer, in_specs=in_specs, out_specs=out_specs, check_vma=False)

time: 117 us -> 122 us (1.043)
  blocking collectives: 40.1 us -> 0 us
  waiting for transfers between devices: 15.2 us -> 39.8 us
  starting transfers between devices: 40.2 us -> 63.2 us
  local copies, waits for them, and re-layouts: 5.3 us -> 3.92 us
    all_to_all x1 -> x0, blocking collectives: 40.1 us -> none  [on_device(): lax.all_to_all(sent.reshape(OWNERS, 1, 512), 'bins', 0, 0)]
    all_to_all x1 -> x3, starting transfers between devices: 5.83 us -> 37.3 us  [the longest x2 30.8 us: on_device(): lax.all_to_all(sent.reshape(OWNERS, 1, 512), EXCHANGE, 0, 0)]
    all_to_all x1 -> x3, waiting for transfers between devices: 8.56 us -> 32.6 us  [the longest x2 32.6 us: on_device(): lax.all_to_all(sent.reshape(OWNERS, 1, 512), EXCHANGE, 0, 0)]
    ppermute x6 -> x4, starting transfers between devices: 26.9 us -> 16.6 us  [the longest x1 6.12 us: on_device(): from_east = lax.ppermute(to_west, ALONG_BINS, west)]
    ppermute x1, starting transfers between devices: 5.62 us -> 7.37 us  [on_device(): from_below = lax.ppermute(high, 'lat', up)]
    pallas_call x2 -> x1, Pallas kernels: 2.79 us -> 1.08 us  [on_device(): pl.pallas_call(edges_kernel, out_shape=shapes((288, 128), (288, 128), (BA...]
    pallas_call x1, Pallas kernels: 5.97 us -> 7.6 us  [on_device(): pl.pallas_call(points_kernel, out_shape=shapes((4 * OWNERS, 128), (48, 12...]
    unnamed x14 -> x20, local copies, waits for them, and re-layouts: 3.81 us -> 2.86 us
  transfers between devices with their start and end apart: 9 -> 9, of which waited for: 3 -> 7; matrix products, arithmetic and copies ran while one was open for 1% -> 1% of each run, Pallas kernels for 3% -> 1%
where the time goes in v4:
time: 122 us; the launch traced here: 121 us
  starting transfers between devices  63.2 us (52%)
  waiting for transfers between devices  39.8 us (33%)
  Pallas kernels  13.3 us (11%)
  local copies, waits for them, and re-layouts  3.92 us (3%)
    all_to_all x2, waiting for transfers between devices, on_device(): lax.all_to_all(sent.reshape(OWNERS, 1, 512), EXCHANGE, 0, 0)  32.6 us
    all_to_all x2, starting transfers between devices, on_device(): lax.all_to_all(sent.reshape(OWNERS, 1, 512), EXCHANGE, 0, 0)  30.8 us
    pallas_call x1, Pallas kernels, on_device(): pl.pallas_call(points_kernel, out_shape=shapes((4 * OWNERS, 128), (48, 12...  7.6 us
    ppermute x1, starting transfers between devices, on_device(): from_below = lax.ppermute(high, 'lat', up)  7.37 us
    all_to_all x1, starting transfers between devices, on_device(): lax.all_to_all(to_bands.reshape(BANDS, OWNERS, 128), 'lat', 0, 0)  6.53 us
    ppermute x1, starting transfers between devices, on_device(): from_east = lax.ppermute(to_west, ALONG_BINS, west)  6.12 us
    ppermute x1, starting transfers between devices, on_device(): drift_high = lax.ppermute(drift[0:16], ALONG_BINS, west)  5.2 us
    ppermute x1, waiting for transfers between devices, on_device(): from_above = lax.ppermute(low, 'lat', down)  3.45 us
  transfers between devices with their start and end apart: 9, of which 7 were waited for; matrix products, arithmetic and copies ran while one was open for 1% of the time, Pallas kernels for 1%

profile of v4, /device:TPU:33, one launch (start us, length us, event | category | flops | bytes accessed | tf_op | source)
XLA Modules:
  0.0 121.1 jit_solution(12220569389454630581)
XLA Ops:
  0.6 0.7 copy-done
  1.4 0.9 copy-done.2
  2.3 0.7 copy-done.6
  3.0 1.1 shard_map.104
  4.1 19.6 %all-to-all-start = ((f32[128,1,512]{2,1,0:T(1,128)}), f32[128,1,512]{2,1,0:T(1,128)S(1)}, u32[]{:S(2)}, u32[]{:S(2)}) async-start(f32[128,1,512]{2,1,0:T(1,128)} %bitcast.2), calls=%async_computation | async-start | bytes 524288 | tf_op jit(solution)/shard_map/all_to_all | solution.py:404
  23.7 0.2 reshape.124
  24.0 0.2 reshape.125.plus
  24.2 0.5 copy-done.8
  24.7 0.2 reshape.126
  25.0 0.2 reshape.127.minus
  25.2 20.7 %all-to-all-done = f32[128,1,512]{2,1,0:T(1,128)S(1)} async-done(((f32[128,1,512]{2,1,0:T(1,128)}), f32[128,1,512]{2,1,0:T(1,128)S(1)}, u32[]{:S(2)}, u32[]{:S(2)}) %all-to-all-start) | async-done | bytes 262176 | tf_op jit(solution)/shard_map/all_to_all | solution.py:404
  45.9 1.1 shard_map.105
  46.9 6.5 %all-to-all-start.1 = ((f32[4,128,128]{2,1,0:T(8,128)}), f32[4,128,128]{2,1,0:T(8,128)S(1)}, u32[]{:S(2)}, u32[]{:S(2)}) async-start(f32[4,128,128]{2,1,0:T(8,128)} %bitcast.6), calls=%async_computation.1 | async-start | bytes 524288 | tf_op jit(solution)/shard_map/all_to_all | solution.py:415
  53.5 2.2 %collective-permute-start = (f32[288,128]{1,0:T(8,128)S(1)}, f32[288,128]{1,0:T(8,128)S(1)}, u32[]{:S(2)}, u32[]{:S(2)}) collective-permute-start(f32[288,128]{1,0:T(8,128)S(1)} %get-tuple-element.26), channel_id=1, source_target_pairs={{0,4},{4,8},{8,12},{12,16},{16,20},{20,24},{24,28},{28,32},{32,36}... | collective-permute-start | bytes 442376 | tf_op jit(solution)/shard_map/ppermute | solution.py:413
  55.7 6.1 %collective-permute-start.1 = (f32[288,128]{1,0:T(8,128)S(1)}, f32[288,128]{1,0:T(8,128)S(1)}, u32[]{:S(2)}, u32[]{:S(2)}) collective-permute-start(f32[288,128]{1,0:T(8,128)S(1)} %get-tuple-element.27), channel_id=1, source_target_pairs={{4,0},{8,4},{12,8},{16,12},{20,16},{24,20},{28,24},{32,28},{36,32}... | collective-permute-start | bytes 442376 | tf_op jit(solution)/shard_map/ppermute | solution.py:414
  61.8 0.1 pad_add_fusion.me
  61.9 2.0 %collective-permute-done.from_west = f32[288,128]{1,0:T(8,128)S(1)} collective-permute-done((f32[288,128]{1,0:T(8,128)S(1)}, f32[288,128]{1,0:T(8,128)S(1)}, u32[]{:S(2)}, u32[]{:S(2)}) %collective-permute-start) | collective-permute-done | bytes 147488 | tf_op jit(solution)/shard_map/ppermute | solution.py:413
  63.9 0.9 collective-permute-done.1.from_east
  64.7 7.6 %shard_map.106 = (f32[512,128]{1,0:T(8,128)}, f32[48,128]{1,0:T(8,128)S(1)}) custom-call(s32[2]{0:T(128)S(1)} %pad_add_fusion.me, f32[512,128]{1,0:T(8,128)S(1)} %bitcast.14, f32[288,128]{1,0:T(8,128)S(1)} %collective-permute-done.from_west, f32[288,128]{1,0:T(8,128)S(1)} %collective-permute-done.1.from_east, f32[512,128]{1,0:T(8,128)S(1)} %bitcast.16, ...), custom_call_target="tpu_custom_call" | custom-call | tf_op jit(solution)/shard_map/pallas_call | solution.py:418
  72.3 11.2 %all-to-all-start.2 = ((f32[128,1,512]{2,1,0:T(1,128)}), f32[128,1,512]{2,1,0:T(1,128)S(1)}, u32[]{:S(2)}, u32[]{:S(2)}) async-start(f32[128,1,512]{2,1,0:T(1,128)} %bitcast.8), calls=%async_computation.2 | async-start | bytes 524288 | tf_op jit(solution)/shard_map/all_to_all | solution.py:426
  83.6 3.1 %collective-permute-start.2 = (f32[16,128]{1,0:T(8,128)S(1)}, f32[16,128]{1,0:T(8,128)S(1)}, u32[]{:S(2)}, u32[]{:S(2)}) collective-permute-start(f32[16,128]{1,0:T(8,128)S(1)} %get-tuple-element.41), channel_id=1, source_target_pairs={{0,4},{4,8},{8,12},{12,16},{16,20},{20,24},{24,28},{28,32},{32,36}... | collective-permute-start | bytes 24584 | tf_op jit(solution)/shard_map/ppermute | solution.py:427
  86.7 5.2 %collective-permute-start.3 = (f32[16,128]{1,0:T(8,128)S(1)}, f32[16,128]{1,0:T(8,128)S(1)}, u32[]{:S(2)}, u32[]{:S(2)}) collective-permute-start(f32[16,128]{1,0:T(8,128)S(1)} %get-tuple-element.40), channel_id=1, source_target_pairs={{4,0},{8,4},{12,8},{16,12},{20,16},{24,20},{28,24},{32,28},{36,32}... | collective-permute-start | bytes 24584 | tf_op jit(solution)/shard_map/ppermute | solution.py:428
  92.0 0.1 reshape.132
  92.1 0.5 collective-permute-done.2.drift_low
  92.6 0.4 collective-permute-done.3.drift_high
  92.9 11.9 %all-to-all-done.2 = f32[128,1,512]{2,1,0:T(1,128)S(1)} async-done(((f32[128,1,512]{2,1,0:T(1,128)}), f32[128,1,512]{2,1,0:T(1,128)S(1)}, u32[]{:S(2)}, u32[]{:S(2)}) %all-to-all-start.2) | async-done | bytes 262176 | tf_op jit(solution)/shard_map/all_to_all | solution.py:426
  104.9 0.3 shard_map.107
  105.2 7.4 %collective-permute-start.4 = (f32[24,384]{1,0:T(8,128)S(1)}, f32[24,384]{1,0:T(8,128)S(1)}, u32[]{:S(2)}, u32[]{:S(2)}) collective-permute-start(f32[24,384]{1,0:T(8,128)S(1)} %get-tuple-element.36), channel_id=1, source_target_pairs={{0,1},{1,2},{2,3},{4,5},{5,6},{6,7},{8,9},{9,10},{10,11},{12,13},{... | collective-permute-start | bytes 110600 | tf_op jit(solution)/shard_map/ppermute | solution.py:436
  112.6 1.9 %collective-permute-start.5 = (f32[24,384]{1,0:T(8,128)S(1)}, f32[24,384]{1,0:T(8,128)S(1)}, u32[]{:S(2)}, u32[]{:S(2)}) collective-permute-start(f32[24,384]{1,0:T(8,128)S(1)} %get-tuple-element.37), channel_id=1, source_target_pairs={{1,0},{2,1},{3,2},{5,4},{6,5},{7,6},{9,8},{10,9},{11,10},{13,12},{... | collective-permute-start | bytes 110600 | tf_op jit(solution)/shard_map/ppermute | solution.py:437
  114.6 1.4 %shard_map.108.inside = f32[9,16,384]{2,1,0:T(8,128)S(1)} custom-call(s32[1]{0:T(128)} %bitcast.me, f32[2304]{0:T(1024)S(1)} %copy-done.4, f32[144,384]{1,0:T(8,128)S(1)} %get-tuple-element.34.middle, f32[16,384]{1,0:T(8,128)S(1)} %get-tuple-element.35.zonal, s32[16,384]{1,0:T(8,128)S(1)} %copy-done.1), custom_call_target="tpu_custom_call" | custom-call | flops 3317760 | bytes 442368 | tf_op jit(solution)/shard_map/pallas_call | solution.py:444
  115.9 3.5 %collective-permute-done.5.high = f32[24,384]{1,0:T(8,128)S(1)} collective-permute-done((f32[24,384]{1,0:T(8,128)S(1)}, f32[24,384]{1,0:T(8,128)S(1)}, u32[]{:S(2)}, u32[]{:S(2)}) %collective-permute-start.5) | collective-permute-done | bytes 36896 | tf_op jit(solution)/shard_map/ppermute | solution.py:437
  119.4 1.8 %shard_map.109 = (f32[9,16,384]{2,1,0:T(8,128)}, f32[2,192,64]{2,1,0:T(8,128)}) custom-call(s32[1]{0:T(128)} %bitcast.me, f32[2304]{0:T(1024)S(1)} %copy-done.4, f32[9,16,384]{2,1,0:T(8,128)S(1)} %shard_map.108.inside, f32[24,384]{1,0:T(8,128)S(1)} %collective-permute-done.4.low, f32[24,384]{1,0:T(8,128)S(1)} %collective-permute-done.5.high, ...), custom_call_target="tpu_custom_call" | custom-call | tf_op jit(solution)/shard_map/pallas_call | solution.py:452
  (25 shorter events, 0.2 us)
Async XLA Ops:
  0.6 0.7 copy-start
  1.4 0.9 copy-start.2
  2.3 0.7 copy-start.6
  4.1 19.6 %copy-start.7 = (s32[1152]{0:T(1024)S(1)}, s32[1152]{0:T(1024)}, u32[]{:S(2)}) copy-start(s32[1152]{0:T(1024)} %param.12) | copy-start | bytes 13828
  4.1 41.7 %all-to-all-start = ((f32[128,1,512]{2,1,0:T(1,128)}), f32[128,1,512]{2,1,0:T(1,128)S(1)}, u32[]{:S(2)}, u32[]{:S(2)}) async-start(f32[128,1,512]{2,1,0:T(1,128)} %bitcast.2), calls=%async_computation | async-start | bytes 524288 | tf_op jit(solution)/shard_map/all_to_all | solution.py:404
  24.0 0.7 copy-start.8
  46.9 17.8 %copy-start.3 = (bf16[128,256]{1,0:T(8,128)(2,1)S(1)}, bf16[128,256]{1,0:T(8,128)(2,1)}, u32[]{:S(2)}) copy-start(bf16[128,256]{1,0:T(8,128)(2,1)} %constant.84.clone.stencil) | copy-start | bytes 196612
  46.9 17.8 %copy-start.5 = (f32[8,1152]{1,0:T(8,128)S(1)}, f32[8,1152]{1,0:T(8,128)}, u32[]{:S(2)}) copy-start(f32[8,1152]{1,0:T(8,128)} %constant.85.clone.values) | copy-start | bytes 110596
  46.9 17.8 %all-to-all-start.1 = ((f32[4,128,128]{2,1,0:T(8,128)}), f32[4,128,128]{2,1,0:T(8,128)S(1)}, u32[]{:S(2)}, u32[]{:S(2)}) async-start(f32[4,128,128]{2,1,0:T(8,128)} %bitcast.6), calls=%async_computation.1 | async-start | bytes 524288 | tf_op jit(solution)/shard_map/all_to_all | solution.py:415
  53.5 10.4 %collective-permute-start = (f32[288,128]{1,0:T(8,128)S(1)}, f32[288,128]{1,0:T(8,128)S(1)}, u32[]{:S(2)}, u32[]{:S(2)}) collective-permute-start(f32[288,128]{1,0:T(8,128)S(1)} %get-tuple-element.26), channel_id=1, source_target_pairs={{0,4},{4,8},{8,12},{12,16},{16,20},{20,24},{24,28},{28,32},{32,36}... | collective-permute-start | bytes 442376 | tf_op jit(solution)/shard_map/ppermute | solution.py:413
  55.7 9.1 %collective-permute-start.1 = (f32[288,128]{1,0:T(8,128)S(1)}, f32[288,128]{1,0:T(8,128)S(1)}, u32[]{:S(2)}, u32[]{:S(2)}) collective-permute-start(f32[288,128]{1,0:T(8,128)S(1)} %get-tuple-element.27), channel_id=1, source_target_pairs={{4,0},{8,4},{12,8},{16,12},{20,16},{24,20},{28,24},{32,28},{36,32}... | collective-permute-start | bytes 442376 | tf_op jit(solution)/shard_map/ppermute | solution.py:414
  72.3 32.5 %all-to-all-start.2 = ((f32[128,1,512]{2,1,0:T(1,128)}), f32[128,1,512]{2,1,0:T(1,128)S(1)}, u32[]{:S(2)}, u32[]{:S(2)}) async-start(f32[128,1,512]{2,1,0:T(1,128)} %bitcast.8), calls=%async_computation.2 | async-start | bytes 524288 | tf_op jit(solution)/shard_map/all_to_all | solution.py:426
  83.6 8.3 %copy-start.9 = (s32[6,32]{1,0:T(8,128)S(1)}, s32[6,32]{1,0:T(8,128)}, u32[]{:S(2)}) copy-start(s32[6,32]{1,0:T(8,128)} %param.14) | copy-start | bytes 2308
  83.6 9.0 %collective-permute-start.2 = (f32[16,128]{1,0:T(8,128)S(1)}, f32[16,128]{1,0:T(8,128)S(1)}, u32[]{:S(2)}, u32[]{:S(2)}) collective-permute-start(f32[16,128]{1,0:T(8,128)S(1)} %get-tuple-element.41), channel_id=1, source_target_pairs={{0,4},{4,8},{8,12},{12,16},{16,20},{20,24},{24,28},{28,32},{32,36}... | collective-permute-start | bytes 24584 | tf_op jit(solution)/shard_map/ppermute | solution.py:427
  86.7 6.2 %collective-permute-start.3 = (f32[16,128]{1,0:T(8,128)S(1)}, f32[16,128]{1,0:T(8,128)S(1)}, u32[]{:S(2)}, u32[]{:S(2)}) collective-permute-start(f32[16,128]{1,0:T(8,128)S(1)} %get-tuple-element.40), channel_id=1, source_target_pairs={{4,0},{8,4},{12,8},{16,12},{20,16},{24,20},{28,24},{32,28},{36,32}... | collective-permute-start | bytes 24584 | tf_op jit(solution)/shard_map/ppermute | solution.py:428
  104.9 9.7 %copy-start.1 = (s32[16,384]{1,0:T(8,128)S(1)}, s32[16,384]{1,0:T(8,128)}, u32[]{:S(2)}) copy-start(s32[16,384]{1,0:T(8,128)} %mask.5) | copy-start | bytes 73732
  104.9 9.7 %copy-start.4 = (f32[2304]{0:T(1024)S(1)}, f32[2304]{0:T(1024)}, u32[]{:S(2)}) copy-start(f32[2304]{0:T(1024)} %constant.86.clone.speeds) | copy-start | bytes 27652
  105.2 10.7 %collective-permute-start.4 = (f32[24,384]{1,0:T(8,128)S(1)}, f32[24,384]{1,0:T(8,128)S(1)}, u32[]{:S(2)}, u32[]{:S(2)}) collective-permute-start(f32[24,384]{1,0:T(8,128)S(1)} %get-tuple-element.36), channel_id=1, source_target_pairs={{0,1},{1,2},{2,3},{4,5},{5,6},{6,7},{8,9},{9,10},{10,11},{12,13},{... | collective-permute-start | bytes 110600 | tf_op jit(solution)/shard_map/ppermute | solution.py:436
  112.6 6.8 %collective-permute-start.5 = (f32[24,384]{1,0:T(8,128)S(1)}, f32[24,384]{1,0:T(8,128)S(1)}, u32[]{:S(2)}, u32[]{:S(2)}) collective-permute-start(f32[24,384]{1,0:T(8,128)S(1)} %get-tuple-element.37), channel_id=1, source_target_pairs={{1,0},{2,1},{3,2},{5,4},{6,5},{7,6},{9,8},{10,9},{11,10},{13,12},{... | collective-permute-start | bytes 110600 | tf_op jit(solution)/shard_map/ppermute | solution.py:437

commit v5 on v4

--- a/solution.py
+++ b/solution.py
@@ -6,7 +6,6 @@
 from jax import lax
 from jax.experimental import pallas as pl
 from jax.experimental.pallas import tpu as pltpu
-from jax.sharding import Mesh
 from jax.sharding import PartitionSpec as P
 
 NDIR = 36
@@ -18,8 +17,6 @@
 NLON = 384
 OWNERS = 128
 BANDS = 4
-ALONG_BINS = ("z", "y", "x")
-EXCHANGE = ("z", "x", "y")
 COLS = 3
 F32 = jnp.float32
 BF16 = jnp.bfloat16
@@ -70,136 +67,99 @@
     return lax.broadcasted_iota(jnp.int32, (rows, 128), 1)
 
 
-def exchange_place(device):
-    return (device & -8) | ((device & 3) << 1) | ((device >> 2) & 1)
-
-
-def device_at(place):
-    return (place & -8) | ((place & 1) << 2) | ((place >> 1) & 3)
-
-
-def bin_at(row):
-    place = (row * 7282) >> 16
-    return device_at(place) * OWN + row - place * OWN
-
-
 def split_beside(x):
     upper = x.astype(BF16).astype(F32)
     return (upper + pltpu.roll(x - upper, 64, 1)).astype(BF16)
 
 
-def pack_kernel(spec, mask, current, out, mask_out, stack, turned, turned2, held):
+def pack_kernel(me, spec, mask, current, out, mask_out, zonal_out, stack, turned, turned2):
     sea = mask[...].astype(F32)
     masked = spec[...] * sea[None]
     stack[0:16, :] = masked[8]
     stack[16:32, :] = sea
     stack[32:128, :] = jnp.zeros((96, NLON), F32)
-    turned[...] = masked[0:8].reshape(128, NLON).T
-    turned2[...] = stack[...].T
+    for ref in (turned, turned2):
+        ref[0:8, :] = jnp.zeros((8, 128), F32)
+        ref[392:400, :] = jnp.zeros((8, 128), F32)
+    turned[8:392, :] = masked[0:8].reshape(128, NLON).T
+    turned2[8:392, :] = stack[...].T
 
     pair = lax.broadcasted_iota(jnp.int32, (32, 128), 0) // 2
     means = jnp.where(pair == lax.broadcasted_iota(jnp.int32, (32, 128), 1) % 16, 0.25, 0.0)
     sums = jnp.dot(current[...], means, precision=HIGHEST, preferred_element_type=F32)
+    zonal = [sums[2 * c : 2 * c + 1] + sums[2 * c + 1 : 2 * c + 2] for c in range(COLS)]
+    zonal_out[...] = jnp.concatenate(zonal + [jnp.zeros((5, 128), F32)], axis=0)
+
+    def column(ref, offset):
+        return ref[pl.ds(8 + offset, OWNERS, stride=COLS), :]
+
     group = lanes(OWNERS) // 16
-    rest = jnp.zeros((OWNERS, 128), F32)
+    east = lax.broadcasted_iota(jnp.int32, (OWNERS, 128), 0) == me[0] + 1
+    rest = jnp.where(east, zonal[2], zonal[0])
     sea_rows = jnp.zeros((OWNERS, 128), F32)
-    for c in range(COLS):
-        for j in range(8):
-            out[pl.ds(4 * exchange_place(j) + c, 16, stride=32), :] = turned[pl.ds(COLS * j + c, 16, stride=8 * COLS), :]
-        column = turned2[pl.ds(c, OWNERS, stride=COLS), :]
-        zonal = sums[2 * c : 2 * c + 1] + sums[2 * c + 1 : 2 * c + 2]
-        rest = jnp.where(group == 2 * c, pltpu.roll(column, 32 * c, 1), rest)
-        rest = jnp.where(group == 2 * c + 1, jnp.broadcast_to(zonal, rest.shape), rest)
-        sea_rows = jnp.where(group == c, pltpu.roll(column, (16 * c - 16) % 128, 1), sea_rows)
-    held[...] = rest
-    for j in range(8):
-        out[pl.ds(4 * exchange_place(j) + 3, 16, stride=32), :] = held[pl.ds(j, 16, stride=8), :]
+    for g, offset in enumerate(GROUP_COLUMNS):
+        out[pl.ds(g, OWNERS, stride=8), :] = column(turned, offset)
+        last = column(turned2, offset)
+        rest = jnp.where(group == g, pltpu.roll(last, 16 * g, 1), rest)
+        if g < COLS:
+            sea_rows = jnp.where(group == g, pltpu.roll(last, (16 * g - 16) % 128, 1), sea_rows)
+    out[pl.ds(7, OWNERS, stride=8), :] = rest
     mask_out[...] = sea_rows
 
 
-def edges_kernel(band, arrived, to_east, to_west, to_bands):
-    def part(c):
-        return arrived[pl.ds(c, OWNERS, stride=4), :]
+def edges_kernel(arrived, to_above, to_below):
+    def part(g):
+        return arrived[pl.ds(g, OWNERS, stride=8), :]
 
     lane = lanes(OWNERS)
-    group = lane // 16
     inside = lane % 16
-    rest = part(3)
-    for ref, c in ((to_east, 1), (to_west, 0)):
-        ref[0:128, :] = part(c)
-        ref[128:256, :] = part(c + 1)
-        pair = jnp.where(
-            group == 0, pltpu.roll(rest, (-32 * c) % 128, 1), pltpu.roll(rest, (16 - 32 * (c + 1)) % 128, 1)
-        )
-        last = jnp.zeros((32, 128), F32)
-        for q in range(4):
-            moved = pltpu.roll(pair[32 * q : 32 * q + 32], 32 * q, 1)
-            last = jnp.where(group[0:32] // 2 == q, moved, last)
-        ref[256:288, :] = last
-    here = band[0]
-    to_bands[...] = jnp.zeros_like(to_bands)
-    for target, r in ((jnp.minimum(here + 1, BANDS - 1), 14), (jnp.maximum(here - 1, 0), 0)):
+    rest = part(7)
+    for ref, r in ((to_above, 14), (to_below, 0)):
         acc = jnp.zeros((OWNERS, 128), F32)
         for c in range(COLS):
             moved = pltpu.roll(part(c), (2 * c - r) % 128, 1)
             acc = jnp.where((inside >= 2 * c) & (inside < 2 * c + 2), moved, acc)
         for c in range(COLS):
-            moved = pltpu.roll(rest, (6 + 2 * c - 32 * c - r) % 128, 1)
+            moved = pltpu.roll(rest, (6 + 2 * c - 16 * c - r) % 128, 1)
             acc = jnp.where((lane >= 6 + 2 * c) & (lane < 8 + 2 * c), moved, acc)
-        to_bands[pl.ds(pl.multiple_of(target * OWNERS, OWNERS), OWNERS), :] = acc
-    to_bands[pl.ds(pl.multiple_of(here * OWNERS, OWNERS), OWNERS), :] = jnp.zeros((OWNERS, 128), F32)
+        ref[...] = acc
 
 
 def points_kernel(
-    me, arrived, from_west, from_east, from_bands, masks, plus, minus, stencil, values,
+    me, arrived, from_below, from_above, masks, zonal, plus, minus, stencil, values,
     out, drift_out, first, source, middle, halves, speeds, plus_col, minus_col,
 ):
     device = me[0]
     lane = lanes(OWNERS)
     group = lane // 16
 
-    flow = arrived[pl.ds(4 * exchange_place(device) + 3, 1), :]
-    below = arrived[pl.ds(4 * exchange_place(jnp.maximum(device - 1, 0)) + 3, 1), :]
-    above = arrived[pl.ds(4 * exchange_place(jnp.minimum(device + 1, OWNERS - 1)) + 3, 1), :]
-    lower = jnp.where(device > 0, pltpu.roll(below, 48, 1), 0.0)
-    upper = jnp.where(device < OWNERS - 1, pltpu.roll(above, 32, 1), 0.0)
+    below = arrived[pl.ds(8 * jnp.maximum(device - 1, 0) + 7, 1), :]
+    above = arrived[pl.ds(8 * jnp.minimum(device + 1, OWNERS - 1) + 7, 1), :]
+    lower = jnp.where(device > 0, pltpu.roll(below, 16, 1), 0.0)
+    upper = jnp.where(device < OWNERS - 1, pltpu.roll(above, 64, 1), 0.0)
     lane1 = lanes()
     group1 = lane1 // 16
+    columns = [zonal[c : c + 1, :] for c in range(COLS)]
     for c in range(COLS):
-        lower = jnp.where(group1 == c + 1, pltpu.roll(flow, (-16 * c) % 128, 1), lower)
-        upper = jnp.where(group1 == c, pltpu.roll(flow, (-16 * (c + 1)) % 128, 1), upper)
+        lower = jnp.where(group1 == c + 1, columns[c], lower)
+        upper = jnp.where(group1 == c, columns[c], upper)
     faces = jnp.where(lane1 < 64, 0.5 * (lower + upper), 0.0)
     sea = masks[pl.ds(device, 1), :]
 
     def chunk(t):
         return slice(128 * t, 128 * t + 128)
 
-    def band_rows(band):
-        return from_bands[pl.ds(pl.multiple_of(band * OWNERS, OWNERS), OWNERS), :]
-
     for i in range(OWN):
-        acc = jnp.zeros((OWNERS, 128), F32)
-        for g in range(7):
-            if i == 8:
-                if g < 3:
-                    part = pltpu.roll(arrived[pl.ds(3, OWNERS, stride=4), :], (-16 * g) % 128, 1)
-                else:
-                    ref, at = (from_west, 48) if g < 5 else (from_east, 80)
-                    piece = ref[256:288, :]
-                    part = jnp.concatenate([pltpu.roll(piece, (at - 32 * q) % 128, 1) for q in range(4)], axis=0)
-            else:
-                if g < 3:
-                    part = arrived[pl.ds(g, OWNERS, stride=4), :]
-                elif g < 5:
-                    part = from_west[chunk(g - 3), :]
-                else:
-                    part = from_east[chunk(g - 5), :]
-                part = pltpu.roll(part, (16 * g - 16 * i) % 128, 1)
-            acc = jnp.where(group == g, part, acc)
+        if i < 8:
+            acc = jnp.zeros((OWNERS, 128), F32)
+            for g in range(7):
+                part = pltpu.roll(arrived[pl.ds(g, OWNERS, stride=8), :], (16 * g - 16 * i) % 128, 1)
+                acc = jnp.where(group == g, part, acc)
+        else:
+            acc = arrived[pl.ds(7, OWNERS, stride=8), :]
         held = 16 * i if i < 8 else 6
-        for band, at in ((jnp.maximum(me[1] - 1, 0), 112), (jnp.minimum(me[1] + 1, BANDS - 1), 118)):
-            beyond = pltpu.roll(band_rows(band), (at - held) % 128, 1)
-            acc = jnp.where((lane >= at) & (lane < at + 6), beyond, acc)
+        for ref, at in ((from_below, 112), (from_above, 118)):
+            acc = jnp.where((lane >= at) & (lane < at + 6), pltpu.roll(ref[...], (at - held) % 128, 1), acc)
         middle[pl.ds(i, OWNERS, stride=OWN), :] = acc
 
     inner = lax.broadcasted_iota(jnp.int32, (128, 128), 0)
@@ -222,7 +182,7 @@
         first[chunk(t), :] = moved
         halves[chunk(t), :] = split_beside(moved)
 
-    numbers = bin_at(lax.broadcasted_iota(jnp.int32, (128, BINS), 1)).astype(F32)
+    numbers = lax.broadcasted_iota(jnp.int32, (128, BINS), 1).astype(F32)
 
     def gathered(col, t):
         wide = jnp.concatenate([col[chunk(t), :]] * OWN, axis=1)
@@ -239,8 +199,7 @@
     for t in range(OWN):
         halves[chunk(t), :] = split_beside(source[chunk(t), :])
     for t in range(OWN):
-        names = bin_at(inner + 128 * t)
-        names = jnp.concatenate([names] * OWN, axis=1)
+        names = lax.broadcasted_iota(jnp.int32, (128, BINS), 0) + 128 * t
         hits = jnp.where(plus[...] == names, 1.0, 0.0) + jnp.where(minus[...] == names, 1.0, 0.0)
         both = jnp.dot(hits.astype(BF16), halves[...], preferred_element_type=F32)
         back = both + pltpu.roll(both, 64, 1)
@@ -263,20 +222,19 @@
             part = pltpu.roll(middle[pl.ds(i, OWNERS, stride=OWN), :], (16 * (i - c)) % 128, 1)
             acc = jnp.where(group == i, part, acc)
         out[pl.ds(c, OWNERS, stride=4), :] = acc
-    acc = jnp.broadcast_to(flow, (OWNERS, 128))
+    acc = jnp.zeros((OWNERS, 128), F32)
     last = middle[pl.ds(8, OWNERS, stride=OWN), :]
     for c in range(COLS):
         acc = jnp.where(group == 2 * c, pltpu.roll(last, 16 * c, 1), acc)
+        acc = jnp.where(group == 2 * c + 1, jnp.broadcast_to(columns[c], acc.shape), acc)
     out[pl.ds(3, OWNERS, stride=4), :] = acc
 
 
 def unpack_kernel(arrived, drift, drift_low, drift_high, middle, zonal, low, high, turned, turned2):
-    for j in range(8):
-        place = 4 * exchange_place(j)
-        rest = arrived[pl.ds(place + 3, 16, stride=32), :]
-        for c in range(COLS):
-            turned[pl.ds(COLS * j + c, 16, stride=8 * COLS), :] = arrived[pl.ds(place + c, 16, stride=32), :]
-            turned2[pl.ds(COLS * j + c, 16, stride=8 * COLS), :] = pltpu.roll(rest, (128 - 32 * c) % 128, 1)
+    rest = arrived[pl.ds(3, OWNERS, stride=4), :]
+    for c in range(COLS):
+        turned[pl.ds(c, OWNERS, stride=COLS), :] = arrived[pl.ds(c, OWNERS, stride=4), :]
+        turned2[pl.ds(c, OWNERS, stride=COLS), :] = pltpu.roll(rest, (128 - 32 * c) % 128, 1)
     middle[0:128, :] = turned[...].T
     rest = turned2[...].T
     middle[128:144, :] = rest[0:16]
@@ -363,10 +321,6 @@
     stokes[1] = total[:, 64:128]
 
 
-def in_exchange_order(partner):
-    return partner.reshape(16, 2, 4, OWN).transpose(0, 2, 1, 3).reshape(1, BINS)
-
-
 def shapes(*sizes):
     return [jax.ShapeDtypeStruct(size, F32) for size in sizes]
 
@@ -374,12 +328,10 @@
 def on_device(spectrum, sea_mask, current, partner_plus, partner_minus, source_map):
     values = bin_values()
     speed_list = values[0:2].reshape(-1)
-    held_values = np.concatenate([values[:, bin_at(np.arange(BINS))], np.zeros((2, BINS), np.float32)])
+    held_values = np.concatenate([values, np.zeros((2, BINS), np.float32)])
     stencil = stencils().astype(BF16)
 
-    device = lax.axis_index(ALONG_BINS).reshape(1)
-    band = lax.axis_index("lat").reshape(1)
-    me = jnp.concatenate([device, band])
+    device = lax.axis_index("bins").reshape(1)
     up = [(i, i + 1) for i in range(BANDS - 1)]
     down = [(i + 1, i) for i in range(BANDS - 1)]
     east = [(i, i + 1) for i in range(OWNERS - 1)]
@@ -388,31 +340,25 @@
     smem = pl.BlockSpec(memory_space=pltpu.SMEM)
     vmem = pl.BlockSpec(memory_space=pltpu.VMEM)
     grant = pltpu.CompilerParams(vmem_limit_bytes=16 * 1024 * 1024)
-    sent, masks = pl.pallas_call(
+    sent, masks, zonal = pl.pallas_call(
         pack_kernel,
-        out_shape=shapes((4 * OWNERS, 128), (OWNERS, 128)),
-        scratch_shapes=[
-            pltpu.VMEM((128, NLON), F32),
-            pltpu.VMEM((NLON, 128), F32),
-            pltpu.VMEM((NLON, 128), F32),
-            pltpu.VMEM((OWNERS, 128), F32),
-        ],
+        out_shape=shapes((8 * OWNERS, 128), (OWNERS, 128), (8, 128)),
+        in_specs=[smem] + [vmem] * 3,
+        scratch_shapes=[pltpu.VMEM((128, NLON), F32), pltpu.VMEM((400, 128), F32), pltpu.VMEM((400, 128), F32)],
         compiler_params=grant,
-    )(spectrum, sea_mask, current)
+    )(device, spectrum, sea_mask, current)
 
     plus, minus, sent = lax.optimization_barrier((partner_plus, partner_minus, sent))
-    arrived = lax.all_to_all(sent.reshape(OWNERS, 1, 512), EXCHANGE, 0, 0).reshape(4 * OWNERS, 128)
-    plus, minus = in_exchange_order(plus), in_exchange_order(minus)
+    arrived = lax.all_to_all(sent.reshape(OWNERS, 1, 1024), "bins", 0, 0).reshape(8 * OWNERS, 128)
+    plus, minus = plus.reshape(1, BINS), minus.reshape(1, BINS)
     arrived, plus, minus = lax.optimization_barrier((arrived, plus, minus))
-    to_east, to_west, to_bands = pl.pallas_call(
+    to_above, to_below = pl.pallas_call(
         edges_kernel,
-        out_shape=shapes((288, 128), (288, 128), (BANDS * OWNERS, 128)),
-        in_specs=[smem, vmem],
+        out_shape=shapes((OWNERS, 128), (OWNERS, 128)),
         compiler_params=grant,
-    )(band, arrived)
-    from_west = lax.ppermute(to_east, ALONG_BINS, east)
-    from_east = lax.ppermute(to_west, ALONG_BINS, west)
-    from_bands = lax.all_to_all(to_bands.reshape(BANDS, OWNERS, 128), "lat", 0, 0).reshape(BANDS * OWNERS, 128)
+    )(arrived)
+    from_below = lax.ppermute(to_above, "lat", up)
+    from_above = lax.ppermute(to_below, "lat", down)
 
     big = pltpu.VMEM((BINS, 128), F32)
     sent, drift = pl.pallas_call(
@@ -421,11 +367,11 @@
         in_specs=[smem] + [vmem] * 9,
         scratch_shapes=[big, big, big, pltpu.VMEM((BINS, 128), BF16), big, big, big],
         compiler_params=pltpu.CompilerParams(vmem_limit_bytes=24 * 1024 * 1024),
-    )(me, arrived, from_west, from_east, from_bands, masks, plus, minus, jnp.asarray(stencil), jnp.asarray(held_values))
-
-    arrived = lax.all_to_all(sent.reshape(OWNERS, 1, 512), EXCHANGE, 0, 0).reshape(4 * OWNERS, 128)
-    drift_low = lax.ppermute(drift[32:48], ALONG_BINS, east)
-    drift_high = lax.ppermute(drift[0:16], ALONG_BINS, west)
+    )(device, arrived, from_below, from_above, masks, zonal, plus, minus, jnp.asarray(stencil), jnp.asarray(held_values))
+
+    arrived = lax.all_to_all(sent.reshape(OWNERS, 1, 512), "bins", 0, 0).reshape(4 * OWNERS, 128)
+    drift_low = lax.ppermute(drift[32:48], "bins", east)
+    drift_high = lax.ppermute(drift[0:16], "bins", west)
 
     middle, zonal_all, low, high = pl.pallas_call(
         unpack_kernel,
@@ -460,8 +406,6 @@
 
 
 def solution(mesh):
-    finer = Mesh(mesh.devices.reshape(16, 2, 4, BANDS), ALONG_BINS + ("lat",))
-    bins = ALONG_BINS
-    in_specs = (P(bins, "lat", None), P("lat", None), P(bins, "lat"), P(), P(), P(bins, "lat"))
-    out_specs = (P(bins, "lat", None), P(None, None, bins, "lat"))
-    return jax.shard_map(on_device, mesh=finer, in_specs=in_specs, out_specs=out_specs, check_vma=False)
+    in_specs = (P("bins", "lat", None), P("lat", None), P("bins", "lat"), P(), P(), P("bins", "lat"))
+    out_specs = (P("bins", "lat", None), P(None, None, "bins", "lat"))
+    return jax.shard_map(on_device, mesh=mesh, in_specs=in_specs, out_specs=out_specs, check_vma=False)

time: 122 us -> 115 us (0.943)
  the two profiles are of different devices: /device:TPU:33 before, /device:TPU:9 now
where the time goes in v5:
time: 115 us; the launch traced here: 114 us
  waiting for transfers between devices  51.3 us (45%)
  starting transfers between devices  47.4 us (41%)
  Pallas kernels  11.5 us (10%)
  local copies, waits for them, and re-layouts  3.15 us (3%)
    all_to_all x1, waiting for transfers between devices, on_device(): lax.all_to_all(sent.reshape(OWNERS, 1, 1024), 'bins', 0, 0)  30.6 us
    all_to_all x1, starting transfers between devices, on_device(): lax.all_to_all(sent.reshape(OWNERS, 1, 1024), 'bins', 0, 0)  19.9 us
    all_to_all x1, waiting for transfers between devices, on_device(): lax.all_to_all(sent.reshape(OWNERS, 1, 512), 'bins', 0, 0)  11.9 us
    ppermute x1, starting transfers between devices, on_device(): from_below = lax.ppermute(to_above, 'lat', up)  7.29 us
    pallas_call x1, Pallas kernels, on_device(): pl.pallas_call(points_kernel, out_shape=shapes((4 * OWNERS, 128), (48, 12...  6.77 us
    all_to_all x1, starting transfers between devices, on_device(): lax.all_to_all(sent.reshape(OWNERS, 1, 512), 'bins', 0, 0)  6.5 us
    ppermute x1, waiting for transfers between devices, on_device(): from_above = lax.ppermute(to_below, 'lat', down)  5.15 us
    ppermute x1, starting transfers between devices, on_device(): drift_high = lax.ppermute(drift[0:16], 'bins', west)  4.3 us
  transfers between devices with their start and end apart: 8, of which 5 were waited for; matrix products, arithmetic and copies ran while one was open for 0% of the time, Pallas kernels for 1%

profile of v5, /device:TPU:9, one launch (start us, length us, event | category | flops | bytes accessed | tf_op | source)
XLA Modules:
  0.0 114.3 jit_solution(16692232004107285662)
XLA Ops:
  0.6 0.0 copy-start.6
  0.6 0.7 copy-done.6
  1.3 0.7 copy-done
  2.1 0.9 copy-done.2
  3.0 1.2 %shard_map.104 = (f32[1024,128]{1,0:T(8,128)}, f32[128,128]{1,0:T(8,128)S(1)}, f32[8,128]{1,0:T(8,128)S(1)}) custom-call(s32[1]{0:T(128)} %bitcast.me, f32[9,16,384]{2,1,0:T(8,128)S(1)} %copy-done.2, s32[16,384]{1,0:T(8,128)S(1)} %copy-done, f32[6,32]{1,0:T(8,128)S(1)} %copy-done.6), custom_call_target="tpu_custom_call" | custom-call | tf_op jit(solution)/shard_map/pallas_call | solution.py:343
  4.2 19.9 %all-to-all-start = ((f32[128,1,1024]{2,1,0:T(1,128)}), f32[128,1,1024]{2,1,0:T(1,128)S(1)}, u32[]{:S(2)}, u32[]{:S(2)}) async-start(f32[128,1,1024]{2,1,0:T(1,128)} %bitcast.1), calls=%async_computation | async-start | bytes 1048576 | tf_op jit(solution)/shard_map/all_to_all | solution.py:352
  24.2 0.0 copy-start.8
  24.2 0.7 copy-done.8
  24.9 30.6 %all-to-all-done = f32[128,1,1024]{2,1,0:T(1,128)S(1)} async-done(((f32[128,1,1024]{2,1,0:T(1,128)}), f32[128,1,1024]{2,1,0:T(1,128)S(1)}, u32[]{:S(2)}, u32[]{:S(2)}) %all-to-all-start) | async-done | bytes 524320 | tf_op jit(solution)/shard_map/all_to_all | solution.py:352
  55.5 0.2 shard_map.105
  55.7 7.3 %collective-permute-start = (f32[128,128]{1,0:T(8,128)S(1)}, f32[128,128]{1,0:T(8,128)S(1)}, u32[]{:S(2)}, u32[]{:S(2)}) collective-permute-start(f32[128,128]{1,0:T(8,128)S(1)} %get-tuple-element.26), channel_id=1, source_target_pairs={{0,1},{1,2},{2,3},{4,5},{5,6},{6,7},{8,9},{9,10},{10,11},{12,13},{... | collective-permute-start | bytes 196616 | tf_op jit(solution)/shard_map/ppermute | solution.py:360
  63.0 1.9 %collective-permute-start.1 = (f32[128,128]{1,0:T(8,128)S(1)}, f32[128,128]{1,0:T(8,128)S(1)}, u32[]{:S(2)}, u32[]{:S(2)}) collective-permute-start(f32[128,128]{1,0:T(8,128)S(1)} %get-tuple-element.27), channel_id=1, source_target_pairs={{1,0},{2,1},{3,2},{5,4},{6,5},{7,6},{9,8},{10,9},{11,10},{13,12},{... | collective-permute-start | bytes 196616 | tf_op jit(solution)/shard_map/ppermute | solution.py:361
  65.0 0.0 collective-permute-done.from_below
  65.0 5.2 %collective-permute-done.1.from_above = f32[128,128]{1,0:T(8,128)S(1)} collective-permute-done((f32[128,128]{1,0:T(8,128)S(1)}, f32[128,128]{1,0:T(8,128)S(1)}, u32[]{:S(2)}, u32[]{:S(2)}) %collective-permute-start.1) | collective-permute-done | bytes 65568 | tf_op jit(solution)/shard_map/ppermute | solution.py:361
  70.1 0.0 copy-done.3
  70.1 6.8 %shard_map.106 = (f32[512,128]{1,0:T(8,128)}, f32[48,128]{1,0:T(8,128)S(1)}) custom-call(s32[1]{0:T(128)} %bitcast.me, f32[1024,128]{1,0:T(8,128)S(1)} %bitcast.9, f32[128,128]{1,0:T(8,128)S(1)} %collective-permute-done.from_below, f32[128,128]{1,0:T(8,128)S(1)} %collective-permute-done.1.from_above, f32[128,128]{1,0:T(8,128)S(1)} %get-tuple-element.28.masks, ...), custom_call_target="tpu_custom_call" | custom-call | tf_op jit(solution)/shard_map/pallas_call | solution.py:364
  76.9 6.5 %all-to-all-start.1 = ((f32[128,1,512]{2,1,0:T(1,128)}), f32[128,1,512]{2,1,0:T(1,128)S(1)}, u32[]{:S(2)}, u32[]{:S(2)}) async-start(f32[128,1,512]{2,1,0:T(1,128)} %bitcast.3), calls=%async_computation.1 | async-start | bytes 524288 | tf_op jit(solution)/shard_map/all_to_all | solution.py:372
  83.4 0.0 copy-start.9
  83.5 3.1 %collective-permute-start.2 = (f32[16,128]{1,0:T(8,128)S(1)}, f32[16,128]{1,0:T(8,128)S(1)}, u32[]{:S(2)}, u32[]{:S(2)}) collective-permute-start(f32[16,128]{1,0:T(8,128)S(1)} %get-tuple-element.41), channel_id=1, source_target_pairs={{0,4},{4,8},{8,12},{12,16},{16,20},{20,24},{24,28},{28,32},{32,36}... | collective-permute-start | bytes 24584 | tf_op jit(solution)/shard_map/ppermute | solution.py:373
  86.6 4.3 %collective-permute-start.3 = (f32[16,128]{1,0:T(8,128)S(1)}, f32[16,128]{1,0:T(8,128)S(1)}, u32[]{:S(2)}, u32[]{:S(2)}) collective-permute-start(f32[16,128]{1,0:T(8,128)S(1)} %get-tuple-element.40), channel_id=1, source_target_pairs={{4,0},{8,4},{12,8},{16,12},{20,16},{24,20},{28,24},{32,28},{36,32}... | collective-permute-start | bytes 24584 | tf_op jit(solution)/shard_map/ppermute | solution.py:374
  90.9 0.1 select_select_fusion
  91.0 0.1 reshape.112
  91.0 0.0 collective-permute-done.2.drift_low
  91.0 0.6 collective-permute-done.3.drift_high
  91.6 11.9 %all-to-all-done.1 = f32[128,1,512]{2,1,0:T(1,128)S(1)} async-done(((f32[128,1,512]{2,1,0:T(1,128)}), f32[128,1,512]{2,1,0:T(1,128)S(1)}, u32[]{:S(2)}, u32[]{:S(2)}) %all-to-all-start.1) | async-done | bytes 262176 | tf_op jit(solution)/shard_map/all_to_all | solution.py:372
  103.6 0.2 shard_map.107
  103.8 1.9 %collective-permute-start.4 = (f32[24,384]{1,0:T(8,128)S(1)}, f32[24,384]{1,0:T(8,128)S(1)}, u32[]{:S(2)}, u32[]{:S(2)}) collective-permute-start(f32[24,384]{1,0:T(8,128)S(1)} %get-tuple-element.36), channel_id=1, source_target_pairs={{0,1},{1,2},{2,3},{4,5},{5,6},{6,7},{8,9},{9,10},{10,11},{12,13},{... | collective-permute-start | bytes 110600 | tf_op jit(solution)/shard_map/ppermute | solution.py:382
  105.7 2.4 %collective-permute-start.5 = (f32[24,384]{1,0:T(8,128)S(1)}, f32[24,384]{1,0:T(8,128)S(1)}, u32[]{:S(2)}, u32[]{:S(2)}) collective-permute-start(f32[24,384]{1,0:T(8,128)S(1)} %get-tuple-element.37), channel_id=1, source_target_pairs={{1,0},{2,1},{3,2},{5,4},{6,5},{7,6},{9,8},{10,9},{11,10},{13,12},{... | collective-permute-start | bytes 110600 | tf_op jit(solution)/shard_map/ppermute | solution.py:383
  108.2 1.4 %shard_map.108.inside = f32[9,16,384]{2,1,0:T(8,128)S(1)} custom-call(s32[1]{0:T(128)} %bitcast.me, f32[2304]{0:T(1024)S(1)} %copy-done.4, f32[144,384]{1,0:T(8,128)S(1)} %get-tuple-element.34.middle, f32[16,384]{1,0:T(8,128)S(1)} %get-tuple-element.35.zonal, s32[16,384]{1,0:T(8,128)S(1)} %copy-done.1), custom_call_target="tpu_custom_call" | custom-call | flops 3317760 | bytes 442368 | tf_op jit(solution)/shard_map/pallas_call | solution.py:390
  109.5 0.0 collective-permute-done.4.low
  109.5 3.0 %collective-permute-done.5.high = f32[24,384]{1,0:T(8,128)S(1)} collective-permute-done((f32[24,384]{1,0:T(8,128)S(1)}, f32[24,384]{1,0:T(8,128)S(1)}, u32[]{:S(2)}, u32[]{:S(2)}) %collective-permute-start.5) | collective-permute-done | bytes 36896 | tf_op jit(solution)/shard_map/ppermute | solution.py:383
  112.5 1.8 %shard_map.109 = (f32[9,16,384]{2,1,0:T(8,128)}, f32[2,192,64]{2,1,0:T(8,128)}) custom-call(s32[1]{0:T(128)} %bitcast.me, f32[2304]{0:T(1024)S(1)} %copy-done.4, f32[9,16,384]{2,1,0:T(8,128)S(1)} %shard_map.108.inside, f32[24,384]{1,0:T(8,128)S(1)} %collective-permute-done.4.low, f32[24,384]{1,0:T(8,128)S(1)} %collective-permute-done.5.high, ...), custom_call_target="tpu_custom_call" | custom-call | tf_op jit(solution)/shard_map/pallas_call | solution.py:398
  (18 shorter events, 0.0 us)
Async XLA Ops:
  0.6 0.7 copy-start.6
  1.3 0.7 copy-start
  2.1 0.9 copy-start.2
  4.2 19.9 %copy-start.7 = (s32[1152]{0:T(1024)S(1)}, s32[1152]{0:T(1024)}, u32[]{:S(2)}) copy-start(s32[1152]{0:T(1024)} %param.12) | copy-start | bytes 13828
  4.2 51.3 %all-to-all-start = ((f32[128,1,1024]{2,1,0:T(1,128)}), f32[128,1,1024]{2,1,0:T(1,128)S(1)}, u32[]{:S(2)}, u32[]{:S(2)}) async-start(f32[128,1,1024]{2,1,0:T(1,128)} %bitcast.1), calls=%async_computation | async-start | bytes 1048576 | tf_op jit(solution)/shard_map/all_to_all | solution.py:352
  24.2 0.7 copy-start.8
  55.5 14.6 %copy-start.3 = (bf16[128,256]{1,0:T(8,128)(2,1)S(1)}, bf16[128,256]{1,0:T(8,128)(2,1)}, u32[]{:S(2)}) copy-start(bf16[128,256]{1,0:T(8,128)(2,1)} %constant.68.clone.stencil) | copy-start | bytes 196612
  55.5 14.6 %copy-start.5 = (f32[8,1152]{1,0:T(8,128)S(1)}, f32[8,1152]{1,0:T(8,128)}, u32[]{:S(2)}) copy-start(f32[8,1152]{1,0:T(8,128)} %constant.69.clone.values) | copy-start | bytes 110596
  55.7 9.2 %collective-permute-start = (f32[128,128]{1,0:T(8,128)S(1)}, f32[128,128]{1,0:T(8,128)S(1)}, u32[]{:S(2)}, u32[]{:S(2)}) collective-permute-start(f32[128,128]{1,0:T(8,128)S(1)} %get-tuple-element.26), channel_id=1, source_target_pairs={{0,1},{1,2},{2,3},{4,5},{5,6},{6,7},{8,9},{9,10},{10,11},{12,13},{... | collective-permute-start | bytes 196616 | tf_op jit(solution)/shard_map/ppermute | solution.py:360
  63.0 7.1 %collective-permute-start.1 = (f32[128,128]{1,0:T(8,128)S(1)}, f32[128,128]{1,0:T(8,128)S(1)}, u32[]{:S(2)}, u32[]{:S(2)}) collective-permute-start(f32[128,128]{1,0:T(8,128)S(1)} %get-tuple-element.27), channel_id=1, source_target_pairs={{1,0},{2,1},{3,2},{5,4},{6,5},{7,6},{9,8},{10,9},{11,10},{13,12},{... | collective-permute-start | bytes 196616 | tf_op jit(solution)/shard_map/ppermute | solution.py:361
  76.9 26.7 %all-to-all-start.1 = ((f32[128,1,512]{2,1,0:T(1,128)}), f32[128,1,512]{2,1,0:T(1,128)S(1)}, u32[]{:S(2)}, u32[]{:S(2)}) async-start(f32[128,1,512]{2,1,0:T(1,128)} %bitcast.3), calls=%async_computation.1 | async-start | bytes 524288 | tf_op jit(solution)/shard_map/all_to_all | solution.py:372
  83.4 7.4 %copy-start.9 = (s32[6,32]{1,0:T(8,128)S(1)}, s32[6,32]{1,0:T(8,128)}, u32[]{:S(2)}) copy-start(s32[6,32]{1,0:T(8,128)} %param.14) | copy-start | bytes 2308
  83.5 7.6 %collective-permute-start.2 = (f32[16,128]{1,0:T(8,128)S(1)}, f32[16,128]{1,0:T(8,128)S(1)}, u32[]{:S(2)}, u32[]{:S(2)}) collective-permute-start(f32[16,128]{1,0:T(8,128)S(1)} %get-tuple-element.41), channel_id=1, source_target_pairs={{0,4},{4,8},{8,12},{12,16},{16,20},{20,24},{24,28},{28,32},{32,36}... | collective-permute-start | bytes 24584 | tf_op jit(solution)/shard_map/ppermute | solution.py:373
  86.6 5.1 %collective-permute-start.3 = (f32[16,128]{1,0:T(8,128)S(1)}, f32[16,128]{1,0:T(8,128)S(1)}, u32[]{:S(2)}, u32[]{:S(2)}) collective-permute-start(f32[16,128]{1,0:T(8,128)S(1)} %get-tuple-element.40), channel_id=1, source_target_pairs={{4,0},{8,4},{12,8},{16,12},{20,16},{24,20},{28,24},{32,28},{36,32}... | collective-permute-start | bytes 24584 | tf_op jit(solution)/shard_map/ppermute | solution.py:374
  103.6 4.6 %copy-start.1 = (s32[16,384]{1,0:T(8,128)S(1)}, s32[16,384]{1,0:T(8,128)}, u32[]{:S(2)}) copy-start(s32[16,384]{1,0:T(8,128)} %mask.5) | copy-start | bytes 73732
  103.6 4.6 %copy-start.4 = (f32[2304]{0:T(1024)S(1)}, f32[2304]{0:T(1024)}, u32[]{:S(2)}) copy-start(f32[2304]{0:T(1024)} %constant.70.clone.speeds) | copy-start | bytes 27652
  103.8 5.7 %collective-permute-start.4 = (f32[24,384]{1,0:T(8,128)S(1)}, f32[24,384]{1,0:T(8,128)S(1)}, u32[]{:S(2)}, u32[]{:S(2)}) collective-permute-start(f32[24,384]{1,0:T(8,128)S(1)} %get-tuple-element.36), channel_id=1, source_target_pairs={{0,1},{1,2},{2,3},{4,5},{5,6},{6,7},{8,9},{9,10},{10,11},{12,13},{... | collective-permute-start | bytes 110600 | tf_op jit(solution)/shard_map/ppermute | solution.py:382
  105.7 6.8 %collective-permute-start.5 = (f32[24,384]{1,0:T(8,128)S(1)}, f32[24,384]{1,0:T(8,128)S(1)}, u32[]{:S(2)}, u32[]{:S(2)}) collective-permute-start(f32[24,384]{1,0:T(8,128)S(1)} %get-tuple-element.37), channel_id=1, source_target_pairs={{1,0},{2,1},{3,2},{5,4},{6,5},{7,6},{9,8},{10,9},{11,10},{13,12},{... | collective-permute-start | bytes 110600 | tf_op jit(solution)/shard_map/ppermute | solution.py:383

commit v6 on v4

--- a/solution.py
+++ b/solution.py
@@ -6,7 +6,6 @@
 from jax import lax
 from jax.experimental import pallas as pl
 from jax.experimental.pallas import tpu as pltpu
-from jax.sharding import Mesh
 from jax.sharding import PartitionSpec as P
 
 NDIR = 36
@@ -18,8 +17,6 @@
 NLON = 384
 OWNERS = 128
 BANDS = 4
-ALONG_BINS = ("z", "y", "x")
-EXCHANGE = ("z", "x", "y")
 COLS = 3
 F32 = jnp.float32
 BF16 = jnp.bfloat16
@@ -70,25 +67,12 @@
     return lax.broadcasted_iota(jnp.int32, (rows, 128), 1)
 
 
-def exchange_place(device):
-    return (device & -8) | ((device & 3) << 1) | ((device >> 2) & 1)
-
-
-def device_at(place):
-    return (place & -8) | ((place & 1) << 2) | ((place >> 1) & 3)
-
-
-def bin_at(row):
-    place = (row * 7282) >> 16
-    return device_at(place) * OWN + row - place * OWN
-
-
 def split_beside(x):
     upper = x.astype(BF16).astype(F32)
     return (upper + pltpu.roll(x - upper, 64, 1)).astype(BF16)
 
 
-def pack_kernel(spec, mask, current, out, mask_out, stack, turned, turned2, held):
+def pack_kernel(spec, mask, current, out, mask_out, stack, turned, turned2):
     sea = mask[...].astype(F32)
     masked = spec[...] * sea[None]
     stack[0:16, :] = masked[8]
@@ -104,20 +88,21 @@
     rest = jnp.zeros((OWNERS, 128), F32)
     sea_rows = jnp.zeros((OWNERS, 128), F32)
     for c in range(COLS):
-        for j in range(8):
-            out[pl.ds(4 * exchange_place(j) + c, 16, stride=32), :] = turned[pl.ds(COLS * j + c, 16, stride=8 * COLS), :]
+        out[pl.ds(c, OWNERS, stride=4), :] = turned[pl.ds(c, OWNERS, stride=COLS), :]
         column = turned2[pl.ds(c, OWNERS, stride=COLS), :]
         zonal = sums[2 * c : 2 * c + 1] + sums[2 * c + 1 : 2 * c + 2]
         rest = jnp.where(group == 2 * c, pltpu.roll(column, 32 * c, 1), rest)
         rest = jnp.where(group == 2 * c + 1, jnp.broadcast_to(zonal, rest.shape), rest)
         sea_rows = jnp.where(group == c, pltpu.roll(column, (16 * c - 16) % 128, 1), sea_rows)
-    held[...] = rest
-    for j in range(8):
-        out[pl.ds(4 * exchange_place(j) + 3, 16, stride=32), :] = held[pl.ds(j, 16, stride=8), :]
+    out[pl.ds(3, OWNERS, stride=4), :] = rest
     mask_out[...] = sea_rows
 
 
-def edges_kernel(band, arrived, to_east, to_west, to_bands):
+def swapped(odd, first, second):
+    return jnp.where(odd, second, first), jnp.where(odd, first, second)
+
+
+def edges_kernel(device, band, arrived, columns_a, columns_b, rows_a, rows_b):
     def part(c):
         return arrived[pl.ds(c, OWNERS, stride=4), :]
 
@@ -125,9 +110,12 @@
     group = lane // 16
     inside = lane % 16
     rest = part(3)
-    for ref, c in ((to_east, 1), (to_west, 0)):
-        ref[0:128, :] = part(c)
-        ref[128:256, :] = part(c + 1)
+
+    odd = (device[0] & 1) == 1
+    columns_a[0:128, :], columns_b[0:128, :] = swapped(odd, part(1), part(0))
+    columns_a[128:256, :], columns_b[128:256, :] = swapped(odd, part(2), part(1))
+    lasts = []
+    for c in (1, 0):
         pair = jnp.where(
             group == 0, pltpu.roll(rest, (-32 * c) % 128, 1), pltpu.roll(rest, (16 - 32 * (c + 1)) % 128, 1)
         )
@@ -135,10 +123,11 @@
         for q in range(4):
             moved = pltpu.roll(pair[32 * q : 32 * q + 32], 32 * q, 1)
             last = jnp.where(group[0:32] // 2 == q, moved, last)
-        ref[256:288, :] = last
-    here = band[0]
-    to_bands[...] = jnp.zeros_like(to_bands)
-    for target, r in ((jnp.minimum(here + 1, BANDS - 1), 14), (jnp.maximum(here - 1, 0), 0)):
+        lasts.append(last)
+    columns_a[256:288, :], columns_b[256:288, :] = swapped(odd, *lasts)
+
+    edges = []
+    for r in (14, 0):
         acc = jnp.zeros((OWNERS, 128), F32)
         for c in range(COLS):
             moved = pltpu.roll(part(c), (2 * c - r) % 128, 1)
@@ -146,21 +135,30 @@
         for c in range(COLS):
             moved = pltpu.roll(rest, (6 + 2 * c - 32 * c - r) % 128, 1)
             acc = jnp.where((lane >= 6 + 2 * c) & (lane < 8 + 2 * c), moved, acc)
-        to_bands[pl.ds(pl.multiple_of(target * OWNERS, OWNERS), OWNERS), :] = acc
-    to_bands[pl.ds(pl.multiple_of(here * OWNERS, OWNERS), OWNERS), :] = jnp.zeros((OWNERS, 128), F32)
+        edges.append(acc)
+    rows_a[...], rows_b[...] = swapped((band[0] & 1) == 1, *edges)
 
 
 def points_kernel(
-    me, arrived, from_west, from_east, from_bands, masks, plus, minus, stencil, values,
-    out, drift_out, first, source, middle, halves, speeds, plus_col, minus_col,
+    me, band, arrived, columns_a, columns_b, rows_a, rows_b, masks, plus, minus, stencil, values,
+    out, drift_out, drift_a, drift_b, first, source, middle, halves, speeds, plus_col, minus_col,
 ):
     device = me[0]
+    odd = (device & 1) == 1
+    rows_below, rows_above = swapped((band[0] & 1) == 1, rows_b[...], rows_a[...])
+
+    def from_west(rows):
+        return jnp.where(odd, columns_a[rows, :], columns_b[rows, :])
+
+    def from_east(rows):
+        return jnp.where(odd, columns_b[rows, :], columns_a[rows, :])
+
     lane = lanes(OWNERS)
     group = lane // 16
 
-    flow = arrived[pl.ds(4 * exchange_place(device) + 3, 1), :]
-    below = arrived[pl.ds(4 * exchange_place(jnp.maximum(device - 1, 0)) + 3, 1), :]
-    above = arrived[pl.ds(4 * exchange_place(jnp.minimum(device + 1, OWNERS - 1)) + 3, 1), :]
+    flow = arrived[pl.ds(4 * device + 3, 1), :]
+    below = arrived[pl.ds(4 * jnp.maximum(device - 1, 0) + 3, 1), :]
+    above = arrived[pl.ds(4 * jnp.minimum(device + 1, OWNERS - 1) + 3, 1), :]
     lower = jnp.where(device > 0, pltpu.roll(below, 48, 1), 0.0)
     upper = jnp.where(device < OWNERS - 1, pltpu.roll(above, 32, 1), 0.0)
     lane1 = lanes()
@@ -174,9 +172,6 @@
     def chunk(t):
         return slice(128 * t, 128 * t + 128)
 
-    def band_rows(band):
-        return from_bands[pl.ds(pl.multiple_of(band * OWNERS, OWNERS), OWNERS), :]
-
     for i in range(OWN):
         acc = jnp.zeros((OWNERS, 128), F32)
         for g in range(7):
@@ -184,22 +179,21 @@
                 if g < 3:
                     part = pltpu.roll(arrived[pl.ds(3, OWNERS, stride=4), :], (-16 * g) % 128, 1)
                 else:
-                    ref, at = (from_west, 48) if g < 5 else (from_east, 80)
-                    piece = ref[256:288, :]
+                    side, at = (from_west, 48) if g < 5 else (from_east, 80)
+                    piece = side(slice(256, 288))
                     part = jnp.concatenate([pltpu.roll(piece, (at - 32 * q) % 128, 1) for q in range(4)], axis=0)
             else:
                 if g < 3:
                     part = arrived[pl.ds(g, OWNERS, stride=4), :]
                 elif g < 5:
-                    part = from_west[chunk(g - 3), :]
+                    part = from_west(chunk(g - 3))
                 else:
-                    part = from_east[chunk(g - 5), :]
+                    part = from_east(chunk(g - 5))
                 part = pltpu.roll(part, (16 * g - 16 * i) % 128, 1)
             acc = jnp.where(group == g, part, acc)
         held = 16 * i if i < 8 else 6
-        for band, at in ((jnp.maximum(me[1] - 1, 0), 112), (jnp.minimum(me[1] + 1, BANDS - 1), 118)):
-            beyond = pltpu.roll(band_rows(band), (at - held) % 128, 1)
-            acc = jnp.where((lane >= at) & (lane < at + 6), beyond, acc)
+        for beyond, at in ((rows_below, 112), (rows_above, 118)):
+            acc = jnp.where((lane >= at) & (lane < at + 6), pltpu.roll(beyond, (at - held) % 128, 1), acc)
         middle[pl.ds(i, OWNERS, stride=OWN), :] = acc
 
     inner = lax.broadcasted_iota(jnp.int32, (128, 128), 0)
@@ -222,7 +216,7 @@
         first[chunk(t), :] = moved
         halves[chunk(t), :] = split_beside(moved)
 
-    numbers = bin_at(lax.broadcasted_iota(jnp.int32, (128, BINS), 1)).astype(F32)
+    numbers = lax.broadcasted_iota(jnp.int32, (128, BINS), 1).astype(F32)
 
     def gathered(col, t):
         wide = jnp.concatenate([col[chunk(t), :]] * OWN, axis=1)
@@ -239,8 +233,7 @@
     for t in range(OWN):
         halves[chunk(t), :] = split_beside(source[chunk(t), :])
     for t in range(OWN):
-        names = bin_at(inner + 128 * t)
-        names = jnp.concatenate([names] * OWN, axis=1)
+        names = lax.broadcasted_iota(jnp.int32, (128, BINS), 0) + 128 * t
         hits = jnp.where(plus[...] == names, 1.0, 0.0) + jnp.where(minus[...] == names, 1.0, 0.0)
         both = jnp.dot(hits.astype(BF16), halves[...], preferred_element_type=F32)
         back = both + pltpu.roll(both, 64, 1)
@@ -255,7 +248,9 @@
     table_lower = (table - table_upper.astype(F32)).astype(BF16)
     sums = jnp.dot(table_upper, halves[...], preferred_element_type=F32)
     drift = sums + pltpu.roll(sums, 64, 1) + jnp.dot(table_lower, halves[...], preferred_element_type=F32)
-    drift_out[...] = drift.T[0:48]
+    turned = drift.T[0:48]
+    drift_out[...] = turned
+    drift_a[...], drift_b[...] = swapped(odd, turned[32:48], turned[0:16])
 
     for c in range(COLS):
         acc = jnp.zeros((OWNERS, 128), F32)
@@ -270,13 +265,13 @@
     out[pl.ds(3, OWNERS, stride=4), :] = acc
 
 
-def unpack_kernel(arrived, drift, drift_low, drift_high, middle, zonal, low, high, turned, turned2):
-    for j in range(8):
-        place = 4 * exchange_place(j)
-        rest = arrived[pl.ds(place + 3, 16, stride=32), :]
-        for c in range(COLS):
-            turned[pl.ds(COLS * j + c, 16, stride=8 * COLS), :] = arrived[pl.ds(place + c, 16, stride=32), :]
-            turned2[pl.ds(COLS * j + c, 16, stride=8 * COLS), :] = pltpu.roll(rest, (128 - 32 * c) % 128, 1)
+def unpack_kernel(
+    device, band, arrived, drift, drift_a, drift_b, middle, zonal, near, rows_a, rows_b, low, high, turned, turned2
+):
+    rest = arrived[pl.ds(3, OWNERS, stride=4), :]
+    for c in range(COLS):
+        turned[pl.ds(c, OWNERS, stride=COLS), :] = arrived[pl.ds(c, OWNERS, stride=4), :]
+        turned2[pl.ds(c, OWNERS, stride=COLS), :] = pltpu.roll(rest, (128 - 32 * c) % 128, 1)
     middle[0:128, :] = turned[...].T
     rest = turned2[...].T
     middle[128:144, :] = rest[0:16]
@@ -284,12 +279,14 @@
     for i in range(OWN):
         low[2 * i : 2 * i + 2, :] = middle[16 * i : 16 * i + 2, :]
         high[2 * i : 2 * i + 2, :] = middle[16 * i + 14 : 16 * i + 16, :]
+    near[0:16, :], near[64:80, :] = swapped((device[0] & 1) == 1, drift_b[...], drift_a[...])
+    near[16:64, :] = drift[...]
     for ref, r in ((low, 0), (high, 15)):
-        pieces = [drift_low[r : r + 1, :]] + [drift[16 * c + r : 16 * c + r + 1, :] for c in range(COLS)]
-        pieces += [drift_high[r : r + 1, :], jnp.zeros((1, 128), F32)]
+        pieces = [near[16 * k + r : 16 * k + r + 1, :] for k in range(5)] + [jnp.zeros((1, 128), F32)]
         ref[18:19, :] = jnp.concatenate(pieces[0:3], axis=1)
         ref[19:20, :] = jnp.concatenate(pieces[3:6], axis=1)
         ref[20:24, :] = jnp.zeros((4, NLON), F32)
+    rows_a[...], rows_b[...] = swapped((band[0] & 1) == 1, high[...], low[...])
 
 
 def inside_kernel(me, speeds, middle, zonal, mask, out, rows):
@@ -329,9 +326,10 @@
         out[i] = sea * (f - change)
 
 
-def final_kernel(me, speeds, inside, low, high, mask, drift, drift_low, drift_high, place, out, stokes, near):
+def final_kernel(me, band, speeds, inside, rows_a, rows_b, mask, drift, place, out, stokes, near, low, high):
     first_bin = me[0] * OWN
     sea = mask[...].astype(F32)
+    low[...], high[...] = swapped((band[0] & 1) == 1, rows_b[...], rows_a[...])
     out[...] = inside[...]
     for i in range(OWN):
         along_y = speeds[BINS + first_bin + i]
@@ -344,10 +342,8 @@
         out[i, 0:2, :] = inside[i, 0:2, :] - sea[0:2] * lower
         out[i, 14:16, :] = inside[i, 14:16, :] - sea[14:16] * upper
 
-    near[...] = jnp.zeros_like(near)
-    near[0:16, :] = drift_low[...]
-    near[16:64, :] = drift[...]
-    near[64:80, :] = drift_high[...]
+    near[0:80, :] = drift[...]
+    near[80:128, :] = jnp.zeros((48, 128), F32)
     for ref, at in ((low, 80), (high, 88)):
         for k in range(5):
             near[at + k : at + k + 1, :] = ref[18 + k // 3 : 19 + k // 3, 128 * (k % 3) : 128 * (k % 3) + 128]
@@ -363,10 +359,6 @@
     stokes[1] = total[:, 64:128]
 
 
-def in_exchange_order(partner):
-    return partner.reshape(16, 2, 4, OWN).transpose(0, 2, 1, 3).reshape(1, BINS)
-
-
 def shapes(*sizes):
     return [jax.ShapeDtypeStruct(size, F32) for size in sizes]
 
@@ -374,16 +366,15 @@
 def on_device(spectrum, sea_mask, current, partner_plus, partner_minus, source_map):
     values = bin_values()
     speed_list = values[0:2].reshape(-1)
-    held_values = np.concatenate([values[:, bin_at(np.arange(BINS))], np.zeros((2, BINS), np.float32)])
+    held_values = np.concatenate([values, np.zeros((2, BINS), np.float32)])
     stencil = stencils().astype(BF16)
 
-    device = lax.axis_index(ALONG_BINS).reshape(1)
+    device = lax.axis_index("bins").reshape(1)
     band = lax.axis_index("lat").reshape(1)
-    me = jnp.concatenate([device, band])
-    up = [(i, i + 1) for i in range(BANDS - 1)]
-    down = [(i + 1, i) for i in range(BANDS - 1)]
-    east = [(i, i + 1) for i in range(OWNERS - 1)]
-    west = [(i + 1, i) for i in range(OWNERS - 1)]
+
+    def swap(x, axis, second):
+        pairs = [(k, k + 1) for k in range(second, lax.axis_size(axis) - 1, 2)]
+        return lax.ppermute(x, axis, pairs + [(j, i) for i, j in pairs])
 
     smem = pl.BlockSpec(memory_space=pltpu.SMEM)
     vmem = pl.BlockSpec(memory_space=pltpu.VMEM)
@@ -391,50 +382,55 @@
     sent, masks = pl.pallas_call(
         pack_kernel,
         out_shape=shapes((4 * OWNERS, 128), (OWNERS, 128)),
+        scratch_shapes=[pltpu.VMEM((128, NLON), F32), pltpu.VMEM((NLON, 128), F32), pltpu.VMEM((NLON, 128), F32)],
+        compiler_params=grant,
+    )(spectrum, sea_mask, current)
+
+    plus, minus, sent = lax.optimization_barrier((partner_plus, partner_minus, sent))
+    arrived = lax.all_to_all(sent.reshape(OWNERS, 1, 512), "bins", 0, 0).reshape(4 * OWNERS, 128)
+    plus, minus = plus.reshape(1, BINS), minus.reshape(1, BINS)
+    arrived, plus, minus = lax.optimization_barrier((arrived, plus, minus))
+    columns_a, columns_b, rows_a, rows_b = pl.pallas_call(
+        edges_kernel,
+        out_shape=shapes((288, 128), (288, 128), (OWNERS, 128), (OWNERS, 128)),
+        in_specs=[smem, smem, vmem],
+        compiler_params=grant,
+    )(device, band, arrived)
+    rows_b = swap(rows_b, "lat", 1)
+    columns_b = swap(columns_b, "bins", 1)
+    columns_a = swap(columns_a, "bins", 0)
+    rows_a = swap(rows_a, "lat", 0)
+
+    big = pltpu.VMEM((BINS, 128), F32)
+    sent, drift, drift_a, drift_b = pl.pallas_call(
+        points_kernel,
+        out_shape=shapes((4 * OWNERS, 128), (48, 128), (16, 128), (16, 128)),
+        in_specs=[smem, smem] + [vmem] * 10,
+        scratch_shapes=[big, big, big, pltpu.VMEM((BINS, 128), BF16), big, big, big],
+        compiler_params=pltpu.CompilerParams(vmem_limit_bytes=24 * 1024 * 1024),
+    )(
+        device, band, arrived, columns_a, columns_b, rows_a, rows_b, masks, plus, minus,
+        jnp.asarray(stencil), jnp.asarray(held_values),
+    )
+
+    arrived = lax.all_to_all(sent.reshape(OWNERS, 1, 512), "bins", 0, 0).reshape(4 * OWNERS, 128)
+    drift_b = swap(drift_b, "bins", 1)
+    drift_a = swap(drift_a, "bins", 0)
+
+    middle, zonal_all, near, rows_a, rows_b = pl.pallas_call(
+        unpack_kernel,
+        out_shape=shapes((OWN * ROWS, NLON), (ROWS, NLON), (80, 128), (24, NLON), (24, NLON)),
+        in_specs=[smem, smem] + [vmem] * 4,
         scratch_shapes=[
-            pltpu.VMEM((128, NLON), F32),
+            pltpu.VMEM((24, NLON), F32),
+            pltpu.VMEM((24, NLON), F32),
             pltpu.VMEM((NLON, 128), F32),
             pltpu.VMEM((NLON, 128), F32),
-            pltpu.VMEM((OWNERS, 128), F32),
         ],
         compiler_params=grant,
-    )(spectrum, sea_mask, current)
-
-    plus, minus, sent = lax.optimization_barrier((partner_plus, partner_minus, sent))
-    arrived = lax.all_to_all(sent.reshape(OWNERS, 1, 512), EXCHANGE, 0, 0).reshape(4 * OWNERS, 128)
-    plus, minus = in_exchange_order(plus), in_exchange_order(minus)
-    arrived, plus, minus = lax.optimization_barrier((arrived, plus, minus))
-    to_east, to_west, to_bands = pl.pallas_call(
-        edges_kernel,
-        out_shape=shapes((288, 128), (288, 128), (BANDS * OWNERS, 128)),
-        in_specs=[smem, vmem],
-        compiler_params=grant,
-    )(band, arrived)
-    from_west = lax.ppermute(to_east, ALONG_BINS, east)
-    from_east = lax.ppermute(to_west, ALONG_BINS, west)
-    from_bands = lax.all_to_all(to_bands.reshape(BANDS, OWNERS, 128), "lat", 0, 0).reshape(BANDS * OWNERS, 128)
-
-    big = pltpu.VMEM((BINS, 128), F32)
-    sent, drift = pl.pallas_call(
-        points_kernel,
-        out_shape=shapes((4 * OWNERS, 128), (48, 128)),
-        in_specs=[smem] + [vmem] * 9,
-        scratch_shapes=[big, big, big, pltpu.VMEM((BINS, 128), BF16), big, big, big],
-        compiler_params=pltpu.CompilerParams(vmem_limit_bytes=24 * 1024 * 1024),
-    )(me, arrived, from_west, from_east, from_bands, masks, plus, minus, jnp.asarray(stencil), jnp.asarray(held_values))
-
-    arrived = lax.all_to_all(sent.reshape(OWNERS, 1, 512), EXCHANGE, 0, 0).reshape(4 * OWNERS, 128)
-    drift_low = lax.ppermute(drift[32:48], ALONG_BINS, east)
-    drift_high = lax.ppermute(drift[0:16], ALONG_BINS, west)
-
-    middle, zonal_all, low, high = pl.pallas_call(
-        unpack_kernel,
-        out_shape=shapes((OWN * ROWS, NLON), (ROWS, NLON), (24, NLON), (24, NLON)),
-        scratch_shapes=[pltpu.VMEM((NLON, 128), F32), pltpu.VMEM((NLON, 128), F32)],
-        compiler_params=grant,
-    )(arrived, drift, drift_low, drift_high)
-    from_below = lax.ppermute(high, "lat", up)
-    from_above = lax.ppermute(low, "lat", down)
+    )(device, band, arrived, drift, drift_a, drift_b)
+    rows_b = swap(rows_b, "lat", 1)
+    rows_a = swap(rows_a, "lat", 0)
 
     row = jnp.arange(32, dtype=jnp.int32)[None, :] // 2 + source_map // 3 - 1
     col = jnp.arange(6, dtype=jnp.int32)[:, None] // 2 + source_map % 3
@@ -452,16 +448,14 @@
     second, stokes = pl.pallas_call(
         final_kernel,
         out_shape=shapes((OWN, ROWS, NLON), (2, 192, 64)),
-        in_specs=[smem, smem] + [vmem] * 8,
-        scratch_shapes=[pltpu.VMEM((128, 128), F32)],
+        in_specs=[smem, smem, smem] + [vmem] * 6,
+        scratch_shapes=[pltpu.VMEM((128, 128), F32), pltpu.VMEM((24, NLON), F32), pltpu.VMEM((24, NLON), F32)],
         compiler_params=grant,
-    )(device, speed_refs, inside, from_below, from_above, sea_mask, drift, drift_low, drift_high, place)
+    )(device, band, speed_refs, inside, rows_a, rows_b, sea_mask, near, place)
     return second, stokes.reshape(2, 6, 32, LEV).transpose(0, 3, 1, 2)
 
 
 def solution(mesh):
-    finer = Mesh(mesh.devices.reshape(16, 2, 4, BANDS), ALONG_BINS + ("lat",))
-    bins = ALONG_BINS
-    in_specs = (P(bins, "lat", None), P("lat", None), P(bins, "lat"), P(), P(), P(bins, "lat"))
-    out_specs = (P(bins, "lat", None), P(None, None, bins, "lat"))
-    return jax.shard_map(on_device, mesh=finer, in_specs=in_specs, out_specs=out_specs, check_vma=False)
+    in_specs = (P("bins", "lat", None), P("lat", None), P("bins", "lat"), P(), P(), P("bins", "lat"))
+    out_specs = (P("bins", "lat", None), P(None, None, "bins", "lat"))
+    return jax.shard_map(on_device, mesh=mesh, in_specs=in_specs, out_specs=out_specs, check_vma=False)

time: 122 us -> 110 us (0.902)
  the two profiles are of different devices: /device:TPU:33 before, /device:TPU:9 now
where the time goes in v6:
time: 110 us; the launch traced here: 109 us
  starting transfers between devices  55.4 us (50%)
  waiting for transfers between devices  38.1 us (35%)
  Pallas kernels  11.6 us (11%)
  local copies, waits for them, and re-layouts  3.13 us (3%)
    all_to_all x2, waiting for transfers between devices, on_device(): lax.all_to_all(sent.reshape(OWNERS, 1, 512), 'bins', 0, 0)  29.8 us
    all_to_all x2, starting transfers between devices, on_device(): lax.all_to_all(sent.reshape(OWNERS, 1, 512), 'bins', 0, 0)  29.3 us
    ppermute x8, starting transfers between devices, swap(): return lax.ppermute(x, axis, pairs + [(j, i) for i, j in pairs])  26 us
    ppermute x8, waiting for transfers between devices, swap(): return lax.ppermute(x, axis, pairs + [(j, i) for i, j in pairs])  8.28 us
    pallas_call x1, Pallas kernels, on_device(): pl.pallas_call(points_kernel, out_shape=shapes((4 * OWNERS, 128), (48, 12...  6.9 us
    unnamed x20, local copies, waits for them, and re-layouts  3.04 us
  transfers between devices with their start and end apart: 10, of which 5 were waited for; matrix products, arithmetic and copies ran while one was open for 0% of the time, Pallas kernels for 1%

profile of v6, /device:TPU:9, one launch (start us, length us, event | category | flops | bytes accessed | tf_op | source)
XLA Modules:
  0.0 109.1 jit_solution(1394681420275614264)
XLA Ops:
  0.6 0.0 copy-start
  0.6 0.7 copy-done
  1.4 0.9 copy-done.2
  2.3 0.7 copy-done.6
  3.0 1.0 shard_map.104
  4.0 19.9 %all-to-all-start = ((f32[128,1,512]{2,1,0:T(1,128)}), f32[128,1,512]{2,1,0:T(1,128)S(1)}, u32[]{:S(2)}, u32[]{:S(2)}) async-start(f32[128,1,512]{2,1,0:T(1,128)} %bitcast.2), calls=%async_computation | async-start | bytes 524288 | tf_op jit(solution)/shard_map/all_to_all | solution.py:390
  23.9 0.0 copy-start.8
  24.0 0.7 copy-done.8
  24.7 20.3 %all-to-all-done = f32[128,1,512]{2,1,0:T(1,128)S(1)} async-done(((f32[128,1,512]{2,1,0:T(1,128)}), f32[128,1,512]{2,1,0:T(1,128)S(1)}, u32[]{:S(2)}, u32[]{:S(2)}) %all-to-all-start) | async-done | bytes 262176 | tf_op jit(solution)/shard_map/all_to_all | solution.py:390
  45.0 0.4 shard_map.105
  45.3 2.4 %collective-permute-start = (f32[288,128]{1,0:T(8,128)S(1)}, f32[288,128]{1,0:T(8,128)S(1)}, u32[]{:S(2)}, u32[]{:S(2)}) collective-permute-start(f32[288,128]{1,0:T(8,128)S(1)} %get-tuple-element.30), channel_id=1, source_target_pairs={{0,4},{8,12},{16,20},{24,28},{32,36},{40,44},{48,52},{56,60},{64,6... | collective-permute-start | bytes 442376 | tf_op jit(solution)/shard_map/ppermute | solution.py:377
  47.7 2.9 %collective-permute-start.1 = (f32[288,128]{1,0:T(8,128)S(1)}, f32[288,128]{1,0:T(8,128)S(1)}, u32[]{:S(2)}, u32[]{:S(2)}) collective-permute-start(f32[288,128]{1,0:T(8,128)S(1)} %get-tuple-element.31), channel_id=1, source_target_pairs={{4,8},{12,16},{20,24},{28,32},{36,40},{44,48},{52,56},{60,64},{68,... | collective-permute-start | bytes 442376 | tf_op jit(solution)/shard_map/ppermute | solution.py:377
  50.6 4.9 %collective-permute-start.2 = (f32[128,128]{1,0:T(8,128)S(1)}, f32[128,128]{1,0:T(8,128)S(1)}, u32[]{:S(2)}, u32[]{:S(2)}) collective-permute-start(f32[128,128]{1,0:T(8,128)S(1)} %get-tuple-element.32), channel_id=1, source_target_pairs={{0,1},{2,3},{1,0},{3,2},{4,5},{6,7},{5,4},{7,6},{8,9},{10,11},{9,8... | collective-permute-start | bytes 196616 | tf_op jit(solution)/shard_map/ppermute | solution.py:377
  55.6 3.8 %collective-permute-start.3 = (f32[128,128]{1,0:T(8,128)S(1)}, f32[128,128]{1,0:T(8,128)S(1)}, u32[]{:S(2)}, u32[]{:S(2)}) collective-permute-start(f32[128,128]{1,0:T(8,128)S(1)} %get-tuple-element.33), channel_id=1, source_target_pairs={{1,2},{2,1},{5,6},{6,5},{9,10},{10,9},{13,14},{14,13},{17,18},{18,... | collective-permute-start | bytes 196616 | tf_op jit(solution)/shard_map/ppermute | solution.py:377
  59.4 0.0 collective-permute-done.2.rows_a
  59.4 3.2 %collective-permute-done.3.rows_b = f32[128,128]{1,0:T(8,128)S(1)} collective-permute-done((f32[128,128]{1,0:T(8,128)S(1)}, f32[128,128]{1,0:T(8,128)S(1)}, u32[]{:S(2)}, u32[]{:S(2)}) %collective-permute-start.3) | collective-permute-done | bytes 65568 | tf_op jit(solution)/shard_map/ppermute | solution.py:377
  62.7 6.9 %shard_map.106 = (f32[512,128]{1,0:T(8,128)}, f32[48,128]{1,0:T(8,128)S(1)}, f32[16,128]{1,0:T(8,128)S(1)}, f32[16,128]{1,0:T(8,128)S(1)}) custom-call(s32[1]{0:T(128)} %bitcast.device.me, s32[1]{0:T(128)} %bitcast.1.band, f32[512,128]{1,0:T(8,128)S(1)} %bitcast.10, f32[288,128]{1,0:T(8,128)S(1)} %collective-permute-done.columns_a, ...), custom_call_target="tpu_custom_call" | custom-call | tf_op jit(solution)/shard_map/pallas_call | solution.py:405
  69.6 9.4 %all-to-all-start.1 = ((f32[128,1,512]{2,1,0:T(1,128)}), f32[128,1,512]{2,1,0:T(1,128)S(1)}, u32[]{:S(2)}, u32[]{:S(2)}) async-start(f32[128,1,512]{2,1,0:T(1,128)} %bitcast.4), calls=%async_computation.1 | async-start | bytes 524288 | tf_op jit(solution)/shard_map/all_to_all | solution.py:416
  79.0 0.0 copy-start.9
  79.0 3.1 %collective-permute-start.4 = (f32[16,128]{1,0:T(8,128)S(1)}, f32[16,128]{1,0:T(8,128)S(1)}, u32[]{:S(2)}, u32[]{:S(2)}) collective-permute-start(f32[16,128]{1,0:T(8,128)S(1)} %get-tuple-element.39), channel_id=1, source_target_pairs={{0,4},{8,12},{16,20},{24,28},{32,36},{40,44},{48,52},{56,60},{64,6... | collective-permute-start | bytes 24584 | tf_op jit(solution)/shard_map/ppermute | solution.py:377
  82.1 3.7 %collective-permute-start.5 = (f32[16,128]{1,0:T(8,128)S(1)}, f32[16,128]{1,0:T(8,128)S(1)}, u32[]{:S(2)}, u32[]{:S(2)}) collective-permute-start(f32[16,128]{1,0:T(8,128)S(1)} %get-tuple-element.40), channel_id=1, source_target_pairs={{4,8},{12,16},{20,24},{28,32},{36,40},{44,48},{52,56},{60,64},{68,... | collective-permute-start | bytes 24584 | tf_op jit(solution)/shard_map/ppermute | solution.py:377
  85.8 0.1 select_select_fusion
  85.9 0.1 reshape.116
  86.0 0.0 collective-permute-done.4.drift_a
  86.0 2.9 %collective-permute-done.5.drift_b = f32[16,128]{1,0:T(8,128)S(1)} collective-permute-done((f32[16,128]{1,0:T(8,128)S(1)}, f32[16,128]{1,0:T(8,128)S(1)}, u32[]{:S(2)}, u32[]{:S(2)}) %collective-permute-start.5) | collective-permute-done | bytes 8224 | tf_op jit(solution)/shard_map/ppermute | solution.py:377
  88.9 9.5 %all-to-all-done.1 = f32[128,1,512]{2,1,0:T(1,128)S(1)} async-done(((f32[128,1,512]{2,1,0:T(1,128)}), f32[128,1,512]{2,1,0:T(1,128)S(1)}, u32[]{:S(2)}, u32[]{:S(2)}) %all-to-all-start.1) | async-done | bytes 262176 | tf_op jit(solution)/shard_map/all_to_all | solution.py:416
  98.5 0.2 shard_map.107
  98.7 1.9 %collective-permute-start.6 = (f32[24,384]{1,0:T(8,128)S(1)}, f32[24,384]{1,0:T(8,128)S(1)}, u32[]{:S(2)}, u32[]{:S(2)}) collective-permute-start(f32[24,384]{1,0:T(8,128)S(1)} %get-tuple-element.43), channel_id=1, source_target_pairs={{0,1},{2,3},{1,0},{3,2},{4,5},{6,7},{5,4},{7,6},{8,9},{10,11},{9,8... | collective-permute-start | bytes 110600 | tf_op jit(solution)/shard_map/ppermute | solution.py:377
  100.6 3.3 %collective-permute-start.7 = (f32[24,384]{1,0:T(8,128)S(1)}, f32[24,384]{1,0:T(8,128)S(1)}, u32[]{:S(2)}, u32[]{:S(2)}) collective-permute-start(f32[24,384]{1,0:T(8,128)S(1)} %get-tuple-element.44), channel_id=1, source_target_pairs={{1,2},{2,1},{5,6},{6,5},{9,10},{10,9},{13,14},{14,13},{17,18},{18,... | collective-permute-start | bytes 110600 | tf_op jit(solution)/shard_map/ppermute | solution.py:377
  103.9 1.4 %shard_map.108.inside = f32[9,16,384]{2,1,0:T(8,128)S(1)} custom-call(s32[1]{0:T(128)} %bitcast.device.me, f32[2304]{0:T(1024)S(1)} %copy-done.4, f32[144,384]{1,0:T(8,128)S(1)} %get-tuple-element.41.middle, f32[16,384]{1,0:T(8,128)S(1)} %get-tuple-element.42.zonal, s32[16,384]{1,0:T(8,128)S(1)} %copy-done.1), custom_call_target="tpu_custom_call" | custom-call | flops 3317760 | bytes 442368 | tf_op jit(solution)/shard_map/pallas_call | solution.py:440
  105.3 2.1 %collective-permute-done.7.rows_b = f32[24,384]{1,0:T(8,128)S(1)} collective-permute-done((f32[24,384]{1,0:T(8,128)S(1)}, f32[24,384]{1,0:T(8,128)S(1)}, u32[]{:S(2)}, u32[]{:S(2)}) %collective-permute-start.7) | collective-permute-done | bytes 36896 | tf_op jit(solution)/shard_map/ppermute | solution.py:377
  107.4 1.7 %shard_map.109 = (f32[9,16,384]{2,1,0:T(8,128)}, f32[2,192,64]{2,1,0:T(8,128)}) custom-call(s32[1]{0:T(128)} %bitcast.device.me, s32[1]{0:T(128)} %bitcast.1.band, f32[2304]{0:T(1024)S(1)} %copy-done.4, f32[9,16,384]{2,1,0:T(8,128)S(1)} %shard_map.108.inside, f32[24,384]{1,0:T(8,128)S(1)} %collective-permute-done.6.rows_a, ...), custom_call_target="tpu_custom_call" | custom-call | tf_op jit(solution)/shard_map/pallas_call | solution.py:448
  (21 shorter events, 0.1 us)
Async XLA Ops:
  0.6 0.7 copy-start
  1.4 0.9 copy-start.2
  2.3 0.7 copy-start.6
  4.0 20.0 %copy-start.7 = (s32[1152]{0:T(1024)S(1)}, s32[1152]{0:T(1024)}, u32[]{:S(2)}) copy-start(s32[1152]{0:T(1024)} %param.12) | copy-start | bytes 13828
  4.0 40.9 %all-to-all-start = ((f32[128,1,512]{2,1,0:T(1,128)}), f32[128,1,512]{2,1,0:T(1,128)S(1)}, u32[]{:S(2)}, u32[]{:S(2)}) async-start(f32[128,1,512]{2,1,0:T(1,128)} %bitcast.2), calls=%async_computation | async-start | bytes 524288 | tf_op jit(solution)/shard_map/all_to_all | solution.py:390
  23.9 0.7 copy-start.8
  45.0 17.7 %copy-start.3 = (bf16[128,256]{1,0:T(8,128)(2,1)S(1)}, bf16[128,256]{1,0:T(8,128)(2,1)}, u32[]{:S(2)}) copy-start(bf16[128,256]{1,0:T(8,128)(2,1)} %constant.71.clone.stencil) | copy-start | bytes 196612
  45.0 17.7 %copy-start.5 = (f32[8,1152]{1,0:T(8,128)S(1)}, f32[8,1152]{1,0:T(8,128)}, u32[]{:S(2)}) copy-start(f32[8,1152]{1,0:T(8,128)} %constant.72.clone.values) | copy-start | bytes 110596
  45.3 17.3 %collective-permute-start = (f32[288,128]{1,0:T(8,128)S(1)}, f32[288,128]{1,0:T(8,128)S(1)}, u32[]{:S(2)}, u32[]{:S(2)}) collective-permute-start(f32[288,128]{1,0:T(8,128)S(1)} %get-tuple-element.30), channel_id=1, source_target_pairs={{0,4},{8,12},{16,20},{24,28},{32,36},{40,44},{48,52},{56,60},{64,6... | collective-permute-start | bytes 442376 | tf_op jit(solution)/shard_map/ppermute | solution.py:377
  47.7 14.9 %collective-permute-start.1 = (f32[288,128]{1,0:T(8,128)S(1)}, f32[288,128]{1,0:T(8,128)S(1)}, u32[]{:S(2)}, u32[]{:S(2)}) collective-permute-start(f32[288,128]{1,0:T(8,128)S(1)} %get-tuple-element.31), channel_id=1, source_target_pairs={{4,8},{12,16},{20,24},{28,32},{36,40},{44,48},{52,56},{60,64},{68,... | collective-permute-start | bytes 442376 | tf_op jit(solution)/shard_map/ppermute | solution.py:377
  50.6 8.8 %collective-permute-start.2 = (f32[128,128]{1,0:T(8,128)S(1)}, f32[128,128]{1,0:T(8,128)S(1)}, u32[]{:S(2)}, u32[]{:S(2)}) collective-permute-start(f32[128,128]{1,0:T(8,128)S(1)} %get-tuple-element.32), channel_id=1, source_target_pairs={{0,1},{2,3},{1,0},{3,2},{4,5},{6,7},{5,4},{7,6},{8,9},{10,11},{9,8... | collective-permute-start | bytes 196616 | tf_op jit(solution)/shard_map/ppermute | solution.py:377
  55.6 7.1 %collective-permute-start.3 = (f32[128,128]{1,0:T(8,128)S(1)}, f32[128,128]{1,0:T(8,128)S(1)}, u32[]{:S(2)}, u32[]{:S(2)}) collective-permute-start(f32[128,128]{1,0:T(8,128)S(1)} %get-tuple-element.33), channel_id=1, source_target_pairs={{1,2},{2,1},{5,6},{6,5},{9,10},{10,9},{13,14},{14,13},{17,18},{18,... | collective-permute-start | bytes 196616 | tf_op jit(solution)/shard_map/ppermute | solution.py:377
  69.6 28.9 %all-to-all-start.1 = ((f32[128,1,512]{2,1,0:T(1,128)}), f32[128,1,512]{2,1,0:T(1,128)S(1)}, u32[]{:S(2)}, u32[]{:S(2)}) async-start(f32[128,1,512]{2,1,0:T(1,128)} %bitcast.4), calls=%async_computation.1 | async-start | bytes 524288 | tf_op jit(solution)/shard_map/all_to_all | solution.py:416
  79.0 6.8 %copy-start.9 = (s32[6,32]{1,0:T(8,128)S(1)}, s32[6,32]{1,0:T(8,128)}, u32[]{:S(2)}) copy-start(s32[6,32]{1,0:T(8,128)} %param.14) | copy-start | bytes 2308
  79.0 7.0 %collective-permute-start.4 = (f32[16,128]{1,0:T(8,128)S(1)}, f32[16,128]{1,0:T(8,128)S(1)}, u32[]{:S(2)}, u32[]{:S(2)}) collective-permute-start(f32[16,128]{1,0:T(8,128)S(1)} %get-tuple-element.39), channel_id=1, source_target_pairs={{0,4},{8,12},{16,20},{24,28},{32,36},{40,44},{48,52},{56,60},{64,6... | collective-permute-start | bytes 24584 | tf_op jit(solution)/shard_map/ppermute | solution.py:377
  82.1 6.8 %collective-permute-start.5 = (f32[16,128]{1,0:T(8,128)S(1)}, f32[16,128]{1,0:T(8,128)S(1)}, u32[]{:S(2)}, u32[]{:S(2)}) collective-permute-start(f32[16,128]{1,0:T(8,128)S(1)} %get-tuple-element.40), channel_id=1, source_target_pairs={{4,8},{12,16},{20,24},{28,32},{36,40},{44,48},{52,56},{60,64},{68,... | collective-permute-start | bytes 24584 | tf_op jit(solution)/shard_map/ppermute | solution.py:377
  98.5 5.5 %copy-start.1 = (s32[16,384]{1,0:T(8,128)S(1)}, s32[16,384]{1,0:T(8,128)}, u32[]{:S(2)}) copy-start(s32[16,384]{1,0:T(8,128)} %mask.5) | copy-start | bytes 73732
  98.5 5.5 %copy-start.4 = (f32[2304]{0:T(1024)S(1)}, f32[2304]{0:T(1024)}, u32[]{:S(2)}) copy-start(f32[2304]{0:T(1024)} %constant.73.clone.speeds) | copy-start | bytes 27652
  98.7 6.6 %collective-permute-start.6 = (f32[24,384]{1,0:T(8,128)S(1)}, f32[24,384]{1,0:T(8,128)S(1)}, u32[]{:S(2)}, u32[]{:S(2)}) collective-permute-start(f32[24,384]{1,0:T(8,128)S(1)} %get-tuple-element.43), channel_id=1, source_target_pairs={{0,1},{2,3},{1,0},{3,2},{4,5},{6,7},{5,4},{7,6},{8,9},{10,11},{9,8... | collective-permute-start | bytes 110600 | tf_op jit(solution)/shard_map/ppermute | solution.py:377
  100.6 6.8 %collective-permute-start.7 = (f32[24,384]{1,0:T(8,128)S(1)}, f32[24,384]{1,0:T(8,128)S(1)}, u32[]{:S(2)}, u32[]{:S(2)}) collective-permute-start(f32[24,384]{1,0:T(8,128)S(1)} %get-tuple-element.44), channel_id=1, source_target_pairs={{1,2},{2,1},{5,6},{6,5},{9,10},{10,9},{13,14},{14,13},{17,18},{18,... | collective-permute-start | bytes 110600 | tf_op jit(solution)/shard_map/ppermute | solution.py:377

commit v7 on v6

--- a/solution.py
+++ b/solution.py
@@ -102,7 +102,7 @@
     return jnp.where(odd, second, first), jnp.where(odd, first, second)
 
 
-def edges_kernel(device, band, arrived, columns_a, columns_b, rows_a, rows_b):
+def edges_kernel(device, band, arrived, rows_b, columns_b, columns_a, rows_a):
     def part(c):
         return arrived[pl.ds(c, OWNERS, stride=4), :]
 
@@ -140,8 +140,8 @@
 
 
 def points_kernel(
-    me, band, arrived, columns_a, columns_b, rows_a, rows_b, masks, plus, minus, stencil, values,
-    out, drift_out, drift_a, drift_b, first, source, middle, halves, speeds, plus_col, minus_col,
+    me, band, arrived, rows_b, columns_b, columns_a, rows_a, sea_row, plus, minus, stencil, values,
+    out, drift_out, drift_b, drift_a, first, source, middle, halves, speeds, plus_col, minus_col,
 ):
     device = me[0]
     odd = (device & 1) == 1
@@ -167,7 +167,7 @@
         lower = jnp.where(group1 == c + 1, pltpu.roll(flow, (-16 * c) % 128, 1), lower)
         upper = jnp.where(group1 == c, pltpu.roll(flow, (-16 * (c + 1)) % 128, 1), upper)
     faces = jnp.where(lane1 < 64, 0.5 * (lower + upper), 0.0)
-    sea = masks[pl.ds(device, 1), :]
+    sea = sea_row[...]
 
     def chunk(t):
         return slice(128 * t, 128 * t + 128)
@@ -266,7 +266,7 @@
 
 
 def unpack_kernel(
-    device, band, arrived, drift, drift_a, drift_b, middle, zonal, near, rows_a, rows_b, low, high, turned, turned2
+    device, band, arrived, drift, drift_b, drift_a, middle, zonal, near, rows_b, rows_a, low, high, turned, turned2
 ):
     rest = arrived[pl.ds(3, OWNERS, stride=4), :]
     for c in range(COLS):
@@ -326,7 +326,7 @@
         out[i] = sea * (f - change)
 
 
-def final_kernel(me, band, speeds, inside, rows_a, rows_b, mask, drift, place, out, stokes, near, low, high):
+def final_kernel(me, band, speeds, inside, rows_b, rows_a, mask, drift, place, out, stokes, near, low, high):
     first_bin = me[0] * OWN
     sea = mask[...].astype(F32)
     low[...], high[...] = swapped((band[0] & 1) == 1, rows_b[...], rows_a[...])
@@ -383,16 +383,17 @@
         pack_kernel,
         out_shape=shapes((4 * OWNERS, 128), (OWNERS, 128)),
         scratch_shapes=[pltpu.VMEM((128, NLON), F32), pltpu.VMEM((NLON, 128), F32), pltpu.VMEM((NLON, 128), F32)],
-        compiler_params=grant,
+        compiler_params=pltpu.CompilerParams(vmem_limit_bytes=60 * 1024 * 1024),
     )(spectrum, sea_mask, current)
 
-    plus, minus, sent = lax.optimization_barrier((partner_plus, partner_minus, sent))
+    plus, minus, sent, masks = lax.optimization_barrier((partner_plus, partner_minus, sent, masks))
     arrived = lax.all_to_all(sent.reshape(OWNERS, 1, 512), "bins", 0, 0).reshape(4 * OWNERS, 128)
     plus, minus = plus.reshape(1, BINS), minus.reshape(1, BINS)
-    arrived, plus, minus = lax.optimization_barrier((arrived, plus, minus))
-    columns_a, columns_b, rows_a, rows_b = pl.pallas_call(
+    sea = lax.dynamic_slice(masks, (device[0], 0), (1, 128))
+    arrived, plus, minus, sea = lax.optimization_barrier((arrived, plus, minus, sea))
+    rows_b, columns_b, columns_a, rows_a = pl.pallas_call(
         edges_kernel,
-        out_shape=shapes((288, 128), (288, 128), (OWNERS, 128), (OWNERS, 128)),
+        out_shape=shapes((OWNERS, 128), (288, 128), (288, 128), (OWNERS, 128)),
         in_specs=[smem, smem, vmem],
         compiler_params=grant,
     )(device, band, arrived)
@@ -402,14 +403,14 @@
     rows_a = swap(rows_a, "lat", 0)
 
     big = pltpu.VMEM((BINS, 128), F32)
-    sent, drift, drift_a, drift_b = pl.pallas_call(
+    sent, drift, drift_b, drift_a = pl.pallas_call(
         points_kernel,
         out_shape=shapes((4 * OWNERS, 128), (48, 128), (16, 128), (16, 128)),
         in_specs=[smem, smem] + [vmem] * 10,
         scratch_shapes=[big, big, big, pltpu.VMEM((BINS, 128), BF16), big, big, big],
         compiler_params=pltpu.CompilerParams(vmem_limit_bytes=24 * 1024 * 1024),
     )(
-        device, band, arrived, columns_a, columns_b, rows_a, rows_b, masks, plus, minus,
+        device, band, arrived, rows_b, columns_b, columns_a, rows_a, sea, plus, minus,
         jnp.asarray(stencil), jnp.asarray(held_values),
     )
 
@@ -417,7 +418,7 @@
     drift_b = swap(drift_b, "bins", 1)
     drift_a = swap(drift_a, "bins", 0)
 
-    middle, zonal_all, near, rows_a, rows_b = pl.pallas_call(
+    middle, zonal_all, near, rows_b, rows_a = pl.pallas_call(
         unpack_kernel,
         out_shape=shapes((OWN * ROWS, NLON), (ROWS, NLON), (80, 128), (24, NLON), (24, NLON)),
         in_specs=[smem, smem] + [vmem] * 4,
@@ -428,7 +429,7 @@
             pltpu.VMEM((NLON, 128), F32),
         ],
         compiler_params=grant,
-    )(device, band, arrived, drift, drift_a, drift_b)
+    )(device, band, arrived, drift, drift_b, drift_a)
     rows_b = swap(rows_b, "lat", 1)
     rows_a = swap(rows_a, "lat", 0)
 
@@ -451,7 +452,7 @@
         in_specs=[smem, smem, smem] + [vmem] * 6,
         scratch_shapes=[pltpu.VMEM((128, 128), F32), pltpu.VMEM((24, NLON), F32), pltpu.VMEM((24, NLON), F32)],
         compiler_params=grant,
-    )(device, band, speed_refs, inside, rows_a, rows_b, sea_mask, near, place)
+    )(device, band, speed_refs, inside, rows_b, rows_a, sea_mask, near, place)
     return second, stokes.reshape(2, 6, 32, LEV).transpose(0, 3, 1, 2)
 
 

time: 110 us -> 108 us (0.982)
  the two profiles are of different devices: /device:TPU:9 before, /device:TPU:33 now
where the time goes in v7:
time: 108 us; the launch traced here: 107 us
  starting transfers between devices  57.4 us (53%)
  waiting for transfers between devices  35.1 us (32%)
  Pallas kernels  12.5 us (12%)
  local copies, waits for them, and re-layouts  1.5 us (1%)
    all_to_all x2, waiting for transfers between devices, on_device(): lax.all_to_all(sent.reshape(OWNERS, 1, 512), 'bins', 0, 0)  31.3 us
    ppermute x8, starting transfers between devices, swap(): return lax.ppermute(x, axis, pairs + [(j, i) for i, j in pairs])  28.8 us
    all_to_all x2, starting transfers between devices, on_device(): lax.all_to_all(sent.reshape(OWNERS, 1, 512), 'bins', 0, 0)  28.6 us
    pallas_call x1, Pallas kernels, on_device(): pl.pallas_call(points_kernel, out_shape=shapes((4 * OWNERS, 128), (48, 12...  6.87 us
    ppermute x8, waiting for transfers between devices, swap(): return lax.ppermute(x, axis, pairs + [(j, i) for i, j in pairs])  3.83 us
  transfers between devices with their start and end apart: 10, of which 5 were waited for; matrix products, arithmetic and copies ran while one was open for 1% of the time, Pallas kernels for 1%

profile of v7, /device:TPU:33, one launch (start us, length us, event | category | flops | bytes accessed | tf_op | source)
XLA Modules:
  0.0 107.4 jit_solution(12201920574686556334)
XLA Ops:
  0.6 2.0 %shard_map.104 = (f32[512,128]{1,0:T(8,128)}, f32[128,128]{1,0:T(8,128)}) custom-call(f32[9,16,384]{2,1,0:T(8,128)} %spec.1, s32[16,384]{1,0:T(8,128)} %mask.5, f32[6,32]{1,0:T(8,128)} %current.1), custom_call_target="tpu_custom_call" | custom-call | tf_op jit(solution)/shard_map/pallas_call | solution.py:382
  2.6 19.5 %all-to-all-start = ((f32[128,1,512]{2,1,0:T(1,128)}), f32[128,1,512]{2,1,0:T(1,128)S(1)}, u32[]{:S(2)}, u32[]{:S(2)}) async-start(f32[128,1,512]{2,1,0:T(1,128)} %bitcast.12), calls=%async_computation | async-start | bytes 524288 | tf_op jit(solution)/shard_map/all_to_all | solution.py:390
  22.1 0.0 copy-start.4
  22.1 0.0 copy-start.5
  22.1 0.7 copy-done.4
  22.8 0.0 copy-done.5
  22.8 0.7 constant_dynamic-slice_fusion.sea_row
  23.5 19.2 %all-to-all-done = f32[128,1,512]{2,1,0:T(1,128)S(1)} async-done(((f32[128,1,512]{2,1,0:T(1,128)}), f32[128,1,512]{2,1,0:T(1,128)S(1)}, u32[]{:S(2)}, u32[]{:S(2)}) %all-to-all-start) | async-done | bytes 262176 | tf_op jit(solution)/shard_map/all_to_all | solution.py:390
  42.7 0.4 shard_map.105
  43.1 3.3 %collective-permute-start.1 = (f32[288,128]{1,0:T(8,128)S(1)}, f32[288,128]{1,0:T(8,128)S(1)}, u32[]{:S(2)}, u32[]{:S(2)}) collective-permute-start(f32[288,128]{1,0:T(8,128)S(1)} %get-tuple-element.35), channel_id=1, source_target_pairs={{4,8},{12,16},{20,24},{28,32},{36,40},{44,48},{52,56},{60,64},{68,... | collective-permute-start | bytes 442376 | tf_op jit(solution)/shard_map/ppermute | solution.py:377
  46.4 2.5 %collective-permute-start.2 = (f32[288,128]{1,0:T(8,128)S(1)}, f32[288,128]{1,0:T(8,128)S(1)}, u32[]{:S(2)}, u32[]{:S(2)}) collective-permute-start(f32[288,128]{1,0:T(8,128)S(1)} %get-tuple-element.36), channel_id=1, source_target_pairs={{0,4},{8,12},{16,20},{24,28},{32,36},{40,44},{48,52},{56,60},{64,6... | collective-permute-start | bytes 442376 | tf_op jit(solution)/shard_map/ppermute | solution.py:377
  48.9 7.9 %collective-permute-start = (f32[128,128]{1,0:T(8,128)S(1)}, f32[128,128]{1,0:T(8,128)S(1)}, u32[]{:S(2)}, u32[]{:S(2)}) collective-permute-start(f32[128,128]{1,0:T(8,128)S(1)} %get-tuple-element.34), channel_id=1, source_target_pairs={{1,2},{2,1},{5,6},{6,5},{9,10},{10,9},{13,14},{14,13},{17,18},{18,... | collective-permute-start | bytes 196616 | tf_op jit(solution)/shard_map/ppermute | solution.py:377
  56.8 1.9 %collective-permute-start.3 = (f32[128,128]{1,0:T(8,128)S(1)}, f32[128,128]{1,0:T(8,128)S(1)}, u32[]{:S(2)}, u32[]{:S(2)}) collective-permute-start(f32[128,128]{1,0:T(8,128)S(1)} %get-tuple-element.37), channel_id=1, source_target_pairs={{0,1},{2,3},{1,0},{3,2},{4,5},{6,7},{5,4},{7,6},{8,9},{10,11},{9,8... | collective-permute-start | bytes 196616 | tf_op jit(solution)/shard_map/ppermute | solution.py:377
  58.7 0.0 collective-permute-done.rows_b
  58.7 1.2 %collective-permute-done.3.rows_a = f32[128,128]{1,0:T(8,128)S(1)} collective-permute-done((f32[128,128]{1,0:T(8,128)S(1)}, f32[128,128]{1,0:T(8,128)S(1)}, u32[]{:S(2)}, u32[]{:S(2)}) %collective-permute-start.3) | collective-permute-done | bytes 65568 | tf_op jit(solution)/shard_map/ppermute | solution.py:377
  59.9 0.0 collective-permute-done.1.columns_b
  59.9 0.0 collective-permute-done.2.columns_a
  59.9 6.9 %shard_map.106 = (f32[512,128]{1,0:T(8,128)}, f32[48,128]{1,0:T(8,128)S(1)}, f32[16,128]{1,0:T(8,128)S(1)}, f32[16,128]{1,0:T(8,128)S(1)}) custom-call(s32[1]{0:T(128)} %bitcast.device.me, s32[1]{0:T(128)} %bitcast.1.band, f32[512,128]{1,0:T(8,128)S(1)} %bitcast.10, f32[128,128]{1,0:T(8,128)S(1)} %collective-permute-done.rows_b, ...), custom_call_target="tpu_custom_call" | custom-call | tf_op jit(solution)/shard_map/pallas_call | solution.py:406
  66.8 9.1 %all-to-all-start.1 = ((f32[128,1,512]{2,1,0:T(1,128)}), f32[128,1,512]{2,1,0:T(1,128)S(1)}, u32[]{:S(2)}, u32[]{:S(2)}) async-start(f32[128,1,512]{2,1,0:T(1,128)} %bitcast.4), calls=%async_computation.1 | async-start | bytes 524288 | tf_op jit(solution)/shard_map/all_to_all | solution.py:417
  76.0 0.0 copy-start.6
  76.0 5.2 %collective-permute-start.4 = (f32[16,128]{1,0:T(8,128)S(1)}, f32[16,128]{1,0:T(8,128)S(1)}, u32[]{:S(2)}, u32[]{:S(2)}) collective-permute-start(f32[16,128]{1,0:T(8,128)S(1)} %get-tuple-element.43), channel_id=1, source_target_pairs={{4,8},{12,16},{20,24},{28,32},{36,40},{44,48},{52,56},{60,64},{68,... | collective-permute-start | bytes 24584 | tf_op jit(solution)/shard_map/ppermute | solution.py:377
  81.2 1.9 %collective-permute-start.5 = (f32[16,128]{1,0:T(8,128)S(1)}, f32[16,128]{1,0:T(8,128)S(1)}, u32[]{:S(2)}, u32[]{:S(2)}) collective-permute-start(f32[16,128]{1,0:T(8,128)S(1)} %get-tuple-element.44), channel_id=1, source_target_pairs={{0,4},{8,12},{16,20},{24,28},{32,36},{40,44},{48,52},{56,60},{64,6... | collective-permute-start | bytes 24584 | tf_op jit(solution)/shard_map/ppermute | solution.py:377
  83.1 0.1 select_select_fusion
  83.2 0.1 reshape.116
  83.3 1.1 %collective-permute-done.4.drift_b = f32[16,128]{1,0:T(8,128)S(1)} collective-permute-done((f32[16,128]{1,0:T(8,128)S(1)}, f32[16,128]{1,0:T(8,128)S(1)}, u32[]{:S(2)}, u32[]{:S(2)}) %collective-permute-start.4) | collective-permute-done | bytes 8224 | tf_op jit(solution)/shard_map/ppermute | solution.py:377
  84.4 1.5 %collective-permute-done.5.drift_a = f32[16,128]{1,0:T(8,128)S(1)} collective-permute-done((f32[16,128]{1,0:T(8,128)S(1)}, f32[16,128]{1,0:T(8,128)S(1)}, u32[]{:S(2)}, u32[]{:S(2)}) %collective-permute-start.5) | collective-permute-done | bytes 8224 | tf_op jit(solution)/shard_map/ppermute | solution.py:377
  85.9 12.1 %all-to-all-done.1 = f32[128,1,512]{2,1,0:T(1,128)S(1)} async-done(((f32[128,1,512]{2,1,0:T(1,128)}), f32[128,1,512]{2,1,0:T(1,128)S(1)}, u32[]{:S(2)}, u32[]{:S(2)}) %all-to-all-start.1) | async-done | bytes 262176 | tf_op jit(solution)/shard_map/all_to_all | solution.py:417
  98.0 0.2 shard_map.107
  98.2 4.2 %collective-permute-start.6 = (f32[24,384]{1,0:T(8,128)S(1)}, f32[24,384]{1,0:T(8,128)S(1)}, u32[]{:S(2)}, u32[]{:S(2)}) collective-permute-start(f32[24,384]{1,0:T(8,128)S(1)} %get-tuple-element.47), channel_id=1, source_target_pairs={{1,2},{2,1},{5,6},{6,5},{9,10},{10,9},{13,14},{14,13},{17,18},{18,... | collective-permute-start | bytes 110600 | tf_op jit(solution)/shard_map/ppermute | solution.py:377
  102.4 1.9 %collective-permute-start.7 = (f32[24,384]{1,0:T(8,128)S(1)}, f32[24,384]{1,0:T(8,128)S(1)}, u32[]{:S(2)}, u32[]{:S(2)}) collective-permute-start(f32[24,384]{1,0:T(8,128)S(1)} %get-tuple-element.48), channel_id=1, source_target_pairs={{0,1},{2,3},{1,0},{3,2},{4,5},{6,7},{5,4},{7,6},{8,9},{10,11},{9,8... | collective-permute-start | bytes 110600 | tf_op jit(solution)/shard_map/ppermute | solution.py:377
  104.3 1.4 %shard_map.108.inside = f32[9,16,384]{2,1,0:T(8,128)S(1)} custom-call(s32[1]{0:T(128)} %bitcast.device.me, f32[2304]{0:T(1024)S(1)} %copy-done.2, f32[144,384]{1,0:T(8,128)S(1)} %get-tuple-element.45.middle, f32[16,384]{1,0:T(8,128)S(1)} %get-tuple-element.46.zonal, s32[16,384]{1,0:T(8,128)S(1)} %copy-done), custom_call_target="tpu_custom_call" | custom-call | flops 3317760 | bytes 442368 | tf_op jit(solution)/shard_map/pallas_call | solution.py:441
  105.7 1.7 %shard_map.109 = (f32[9,16,384]{2,1,0:T(8,128)}, f32[2,192,64]{2,1,0:T(8,128)}) custom-call(s32[1]{0:T(128)} %bitcast.device.me, s32[1]{0:T(128)} %bitcast.1.band, f32[2304]{0:T(1024)S(1)} %copy-done.2, f32[9,16,384]{2,1,0:T(8,128)S(1)} %shard_map.108.inside, f32[24,384]{1,0:T(8,128)S(1)} %collective-permute-done.6.rows_b, ...), custom_call_target="tpu_custom_call" | custom-call | tf_op jit(solution)/shard_map/pallas_call | solution.py:449
  (16 shorter events, 0.0 us)
Async XLA Ops:
  2.6 40.1 %all-to-all-start = ((f32[128,1,512]{2,1,0:T(1,128)}), f32[128,1,512]{2,1,0:T(1,128)S(1)}, u32[]{:S(2)}, u32[]{:S(2)}) async-start(f32[128,1,512]{2,1,0:T(1,128)} %bitcast.12), calls=%async_computation | async-start | bytes 524288 | tf_op jit(solution)/shard_map/all_to_all | solution.py:390
  22.1 0.7 copy-start.4
  22.1 0.7 copy-start.5
  42.7 17.2 %copy-start.1 = (bf16[128,256]{1,0:T(8,128)(2,1)S(1)}, bf16[128,256]{1,0:T(8,128)(2,1)}, u32[]{:S(2)}) copy-start(bf16[128,256]{1,0:T(8,128)(2,1)} %constant.73.clone.stencil) | copy-start | bytes 196612
  42.7 17.2 %copy-start.3 = (f32[8,1152]{1,0:T(8,128)S(1)}, f32[8,1152]{1,0:T(8,128)}, u32[]{:S(2)}) copy-start(f32[8,1152]{1,0:T(8,128)} %constant.74.clone.values) | copy-start | bytes 110596
  43.1 16.8 %collective-permute-start.1 = (f32[288,128]{1,0:T(8,128)S(1)}, f32[288,128]{1,0:T(8,128)S(1)}, u32[]{:S(2)}, u32[]{:S(2)}) collective-permute-start(f32[288,128]{1,0:T(8,128)S(1)} %get-tuple-element.35), channel_id=1, source_target_pairs={{4,8},{12,16},{20,24},{28,32},{36,40},{44,48},{52,56},{60,64},{68,... | collective-permute-start | bytes 442376 | tf_op jit(solution)/shard_map/ppermute | solution.py:377
  46.4 13.5 %collective-permute-start.2 = (f32[288,128]{1,0:T(8,128)S(1)}, f32[288,128]{1,0:T(8,128)S(1)}, u32[]{:S(2)}, u32[]{:S(2)}) collective-permute-start(f32[288,128]{1,0:T(8,128)S(1)} %get-tuple-element.36), channel_id=1, source_target_pairs={{0,4},{8,12},{16,20},{24,28},{32,36},{40,44},{48,52},{56,60},{64,6... | collective-permute-start | bytes 442376 | tf_op jit(solution)/shard_map/ppermute | solution.py:377
  48.9 9.8 %collective-permute-start = (f32[128,128]{1,0:T(8,128)S(1)}, f32[128,128]{1,0:T(8,128)S(1)}, u32[]{:S(2)}, u32[]{:S(2)}) collective-permute-start(f32[128,128]{1,0:T(8,128)S(1)} %get-tuple-element.34), channel_id=1, source_target_pairs={{1,2},{2,1},{5,6},{6,5},{9,10},{10,9},{13,14},{14,13},{17,18},{18,... | collective-permute-start | bytes 196616 | tf_op jit(solution)/shard_map/ppermute | solution.py:377
  56.8 3.1 %collective-permute-start.3 = (f32[128,128]{1,0:T(8,128)S(1)}, f32[128,128]{1,0:T(8,128)S(1)}, u32[]{:S(2)}, u32[]{:S(2)}) collective-permute-start(f32[128,128]{1,0:T(8,128)S(1)} %get-tuple-element.37), channel_id=1, source_target_pairs={{0,1},{2,3},{1,0},{3,2},{4,5},{6,7},{5,4},{7,6},{8,9},{10,11},{9,8... | collective-permute-start | bytes 196616 | tf_op jit(solution)/shard_map/ppermute | solution.py:377
  66.8 31.2 %all-to-all-start.1 = ((f32[128,1,512]{2,1,0:T(1,128)}), f32[128,1,512]{2,1,0:T(1,128)S(1)}, u32[]{:S(2)}, u32[]{:S(2)}) async-start(f32[128,1,512]{2,1,0:T(1,128)} %bitcast.4), calls=%async_computation.1 | async-start | bytes 524288 | tf_op jit(solution)/shard_map/all_to_all | solution.py:417
  76.0 7.2 %copy-start.6 = (s32[6,32]{1,0:T(8,128)S(1)}, s32[6,32]{1,0:T(8,128)}, u32[]{:S(2)}) copy-start(s32[6,32]{1,0:T(8,128)} %param.14) | copy-start | bytes 2308
  76.0 8.4 %collective-permute-start.4 = (f32[16,128]{1,0:T(8,128)S(1)}, f32[16,128]{1,0:T(8,128)S(1)}, u32[]{:S(2)}, u32[]{:S(2)}) collective-permute-start(f32[16,128]{1,0:T(8,128)S(1)} %get-tuple-element.43), channel_id=1, source_target_pairs={{4,8},{12,16},{20,24},{28,32},{36,40},{44,48},{52,56},{60,64},{68,... | collective-permute-start | bytes 24584 | tf_op jit(solution)/shard_map/ppermute | solution.py:377
  81.2 4.7 %collective-permute-start.5 = (f32[16,128]{1,0:T(8,128)S(1)}, f32[16,128]{1,0:T(8,128)S(1)}, u32[]{:S(2)}, u32[]{:S(2)}) collective-permute-start(f32[16,128]{1,0:T(8,128)S(1)} %get-tuple-element.44), channel_id=1, source_target_pairs={{0,4},{8,12},{16,20},{24,28},{32,36},{40,44},{48,52},{56,60},{64,6... | collective-permute-start | bytes 24584 | tf_op jit(solution)/shard_map/ppermute | solution.py:377
  98.0 6.4 %copy-start = (s32[16,384]{1,0:T(8,128)S(1)}, s32[16,384]{1,0:T(8,128)}, u32[]{:S(2)}) copy-start(s32[16,384]{1,0:T(8,128)} %mask.5) | copy-start | bytes 73732
  98.0 6.4 %copy-start.2 = (f32[2304]{0:T(1024)S(1)}, f32[2304]{0:T(1024)}, u32[]{:S(2)}) copy-start(f32[2304]{0:T(1024)} %constant.75.clone.speeds) | copy-start | bytes 27652
  98.2 7.5 %collective-permute-start.6 = (f32[24,384]{1,0:T(8,128)S(1)}, f32[24,384]{1,0:T(8,128)S(1)}, u32[]{:S(2)}, u32[]{:S(2)}) collective-permute-start(f32[24,384]{1,0:T(8,128)S(1)} %get-tuple-element.47), channel_id=1, source_target_pairs={{1,2},{2,1},{5,6},{6,5},{9,10},{10,9},{13,14},{14,13},{17,18},{18,... | collective-permute-start | bytes 110600 | tf_op jit(solution)/shard_map/ppermute | solution.py:377
  102.4 3.3 %collective-permute-start.7 = (f32[24,384]{1,0:T(8,128)S(1)}, f32[24,384]{1,0:T(8,128)S(1)}, u32[]{:S(2)}, u32[]{:S(2)}) collective-permute-start(f32[24,384]{1,0:T(8,128)S(1)} %get-tuple-element.48), channel_id=1, source_target_pairs={{0,1},{2,3},{1,0},{3,2},{4,5},{6,7},{5,4},{7,6},{8,9},{10,11},{9,8... | collective-permute-start | bytes 110600 | tf_op jit(solution)/shard_map/ppermute | solution.py:377

commit v8 on v7

--- a/solution.py
+++ b/solution.py
@@ -67,9 +67,14 @@
     return lax.broadcasted_iota(jnp.int32, (rows, 128), 1)
 
 
-def split_beside(x):
-    upper = x.astype(BF16).astype(F32)
-    return (upper + pltpu.roll(x - upper, 64, 1)).astype(BF16)
+def split_into(ref, rows, x):
+    upper = x.astype(BF16)
+    ref[rows, 0:128] = upper
+    ref[rows, 128:256] = (x - upper.astype(F32)).astype(BF16)
+
+
+def joined(both):
+    return both[:, 0:128] + both[:, 128:256]
 
 
 def pack_kernel(spec, mask, current, out, mask_out, stack, turned, turned2):
@@ -172,24 +177,23 @@
     def chunk(t):
         return slice(128 * t, 128 * t + 128)
 
+    for g in range(3):
+        source[chunk(g), :] = arrived[pl.ds(g, OWNERS, stride=4), :]
+    for g in range(3, 7):
+        source[chunk(g), :] = from_west(chunk(g - 3)) if g < 5 else from_east(chunk(g - 5))
+    source[chunk(7), :] = arrived[pl.ds(3, OWNERS, stride=4), :]
     for i in range(OWN):
         acc = jnp.zeros((OWNERS, 128), F32)
         for g in range(7):
             if i == 8:
                 if g < 3:
-                    part = pltpu.roll(arrived[pl.ds(3, OWNERS, stride=4), :], (-16 * g) % 128, 1)
+                    part = pltpu.roll(source[chunk(7), :], (-16 * g) % 128, 1)
                 else:
                     side, at = (from_west, 48) if g < 5 else (from_east, 80)
                     piece = side(slice(256, 288))
                     part = jnp.concatenate([pltpu.roll(piece, (at - 32 * q) % 128, 1) for q in range(4)], axis=0)
             else:
-                if g < 3:
-                    part = arrived[pl.ds(g, OWNERS, stride=4), :]
-                elif g < 5:
-                    part = from_west(chunk(g - 3))
-                else:
-                    part = from_east(chunk(g - 5))
-                part = pltpu.roll(part, (16 * g - 16 * i) % 128, 1)
+                part = pltpu.roll(source[chunk(g), :], (16 * g - 16 * i) % 128, 1)
             acc = jnp.where(group == g, part, acc)
         held = 16 * i if i < 8 else 6
         for beyond, at in ((rows_below, 112), (rows_above, 118)):
@@ -212,17 +216,16 @@
         flux = jnp.maximum(speed, 0.0) * sums[:, 0:128] + jnp.minimum(speed, 0.0) * sums[:, 128:256]
         change = (pltpu.roll(flux, 112, 1) - flux) + pltpu.roll(flux, 64, 1)
         moved = sea * (value - change)
-        moved = jnp.where(lane < 48, moved, 0.0)
         first[chunk(t), :] = moved
-        halves[chunk(t), :] = split_beside(moved)
-
-    numbers = lax.broadcasted_iota(jnp.int32, (128, BINS), 1).astype(F32)
+        split_into(halves, chunk(t), moved)
+
+    numbers = lax.broadcasted_iota(jnp.int32, (128, BINS), 1).astype(jnp.int16)
+    one, none = jnp.ones((128, BINS), BF16), jnp.zeros((128, BINS), BF16)
 
     def gathered(col, t):
-        wide = jnp.concatenate([col[chunk(t), :]] * OWN, axis=1)
-        chosen = jnp.where(wide == numbers, 1.0, 0.0).astype(BF16)
-        both = jnp.dot(chosen, halves[...], preferred_element_type=F32)
-        return both + pltpu.roll(both, 64, 1)
+        wide = jnp.concatenate([col[chunk(t), :].astype(jnp.int32).astype(jnp.int16)] * OWN, axis=1)
+        chosen = jnp.where(wide == numbers, one, none)
+        return joined(jnp.dot(chosen, halves[...], preferred_element_type=F32))
 
     for t in range(OWN):
         ahead = gathered(plus_col, t)
@@ -231,33 +234,34 @@
         strength = jnp.broadcast_to(speeds[chunk(t), 127:128], (128, 128))
         source[chunk(t), :] = strength * (f * f * (ahead + behind) - 2.0 * f * ahead * behind)
     for t in range(OWN):
-        halves[chunk(t), :] = split_beside(source[chunk(t), :])
+        split_into(halves, chunk(t), source[chunk(t), :])
+    plus_wide = jnp.broadcast_to(plus[...], (128, BINS)).astype(jnp.int16)
+    minus_wide = jnp.broadcast_to(minus[...], (128, BINS)).astype(jnp.int16)
     for t in range(OWN):
-        names = lax.broadcasted_iota(jnp.int32, (128, BINS), 0) + 128 * t
-        hits = jnp.where(plus[...] == names, 1.0, 0.0) + jnp.where(minus[...] == names, 1.0, 0.0)
-        both = jnp.dot(hits.astype(BF16), halves[...], preferred_element_type=F32)
-        back = both + pltpu.roll(both, 64, 1)
-        m = first[chunk(t), :] + (source[chunk(t), :] - 0.5 * back)
-        middle[chunk(t), :] = jnp.where(lane < 48, m, 0.0)
+        names = (lax.broadcasted_iota(jnp.int32, (128, BINS), 0) + 128 * t).astype(jnp.int16)
+        hits = jnp.where(plus_wide == names, one, none) + jnp.where(minus_wide == names, one, none)
+        back = joined(jnp.dot(hits, halves[...], preferred_element_type=F32))
+        middle[chunk(t), :] = first[chunk(t), :] + (source[chunk(t), :] - 0.5 * back)
     for t in range(OWN):
-        halves[chunk(t), :] = split_beside(middle[chunk(t), :])
+        split_into(halves, chunk(t), middle[chunk(t), :])
     level = lax.broadcasted_iota(jnp.int32, (LEV, BINS), 0).astype(F32) + 0.5
     decay = jnp.exp(level * values[3:4, :])
     table = jnp.concatenate([decay * values[4:5, :], decay * values[5:6, :]], axis=0)
     table_upper = table.astype(BF16)
     table_lower = (table - table_upper.astype(F32)).astype(BF16)
-    sums = jnp.dot(table_upper, halves[...], preferred_element_type=F32)
-    drift = sums + pltpu.roll(sums, 64, 1) + jnp.dot(table_lower, halves[...], preferred_element_type=F32)
+    drift = joined(jnp.dot(table_upper, halves[...], preferred_element_type=F32))
+    drift = drift + jnp.dot(table_lower, halves[:, 0:128], preferred_element_type=F32)
     turned = drift.T[0:48]
     drift_out[...] = turned
     drift_a[...], drift_b[...] = swapped(odd, turned[32:48], turned[0:16])
 
+    accs = [jnp.zeros((OWNERS, 128), F32)] * COLS
+    for i in range(8):
+        value = middle[pl.ds(i, OWNERS, stride=OWN), :]
+        for c in range(COLS):
+            accs[c] = jnp.where(group == i, pltpu.roll(value, (16 * (i - c)) % 128, 1), accs[c])
     for c in range(COLS):
-        acc = jnp.zeros((OWNERS, 128), F32)
-        for i in range(8):
-            part = pltpu.roll(middle[pl.ds(i, OWNERS, stride=OWN), :], (16 * (i - c)) % 128, 1)
-            acc = jnp.where(group == i, part, acc)
-        out[pl.ds(c, OWNERS, stride=4), :] = acc
+        out[pl.ds(c, OWNERS, stride=4), :] = accs[c]
     acc = jnp.broadcast_to(flow, (OWNERS, 128))
     last = middle[pl.ds(8, OWNERS, stride=OWN), :]
     for c in range(COLS):
@@ -407,7 +411,7 @@
         points_kernel,
         out_shape=shapes((4 * OWNERS, 128), (48, 128), (16, 128), (16, 128)),
         in_specs=[smem, smem] + [vmem] * 10,
-        scratch_shapes=[big, big, big, pltpu.VMEM((BINS, 128), BF16), big, big, big],
+        scratch_shapes=[big, big, big, pltpu.VMEM((BINS, 256), BF16), big, big, big],
         compiler_params=pltpu.CompilerParams(vmem_limit_bytes=24 * 1024 * 1024),
     )(
         device, band, arrived, rows_b, columns_b, columns_a, rows_a, sea, plus, minus,

time: 108 us -> 107 us (level)
  no operation moved by 1% of the time
where the time goes in v8:
time: 107 us
  starting transfers between devices  57.4 us (54%)
  waiting for transfers between devices  35.1 us (33%)
  Pallas kernels  11.6 us (11%)
  local copies, waits for them, and re-layouts  1.5 us (1%)
    all_to_all x2, waiting for transfers between devices, on_device(): lax.all_to_all(sent.reshape(OWNERS, 1, 512), 'bins', 0, 0)  31.3 us
    ppermute x8, starting transfers between devices, swap(): return lax.ppermute(x, axis, pairs + [(j, i) for i, j in pairs])  28.8 us
    all_to_all x2, starting transfers between devices, on_device(): lax.all_to_all(sent.reshape(OWNERS, 1, 512), 'bins', 0, 0)  28.6 us
    pallas_call x1, Pallas kernels, on_device(): pl.pallas_call(points_kernel, out_shape=shapes((4 * OWNERS, 128), (48, 12...  5.98 us
    ppermute x8, waiting for transfers between devices, swap(): return lax.ppermute(x, axis, pairs + [(j, i) for i, j in pairs])  3.83 us
  transfers between devices with their start and end apart: 10, of which 5 were waited for; matrix products, arithmetic and copies ran while one was open for 1% of the time, Pallas kernels for 1%

profile of v8, /device:TPU:33, one launch (start us, length us, event | category | flops | bytes accessed | tf_op | source)
XLA Modules:
  0.0 106.6 jit_solution(2362208751628327790)
XLA Ops:
  0.6 2.0 %shard_map.104 = (f32[512,128]{1,0:T(8,128)}, f32[128,128]{1,0:T(8,128)}) custom-call(f32[9,16,384]{2,1,0:T(8,128)} %spec.1, s32[16,384]{1,0:T(8,128)} %mask.5, f32[6,32]{1,0:T(8,128)} %current.1), custom_call_target="tpu_custom_call" | custom-call | tf_op jit(solution)/shard_map/pallas_call | solution.py:386
  2.6 19.5 %all-to-all-start = ((f32[128,1,512]{2,1,0:T(1,128)}), f32[128,1,512]{2,1,0:T(1,128)S(1)}, u32[]{:S(2)}, u32[]{:S(2)}) async-start(f32[128,1,512]{2,1,0:T(1,128)} %bitcast.12), calls=%async_computation | async-start | bytes 524288 | tf_op jit(solution)/shard_map/all_to_all | solution.py:394
  22.1 0.0 copy-start.4
  22.1 0.0 copy-start.5
  22.1 0.7 copy-done.4
  22.8 0.0 copy-done.5
  22.8 0.7 constant_dynamic-slice_fusion.sea_row
  23.5 19.2 %all-to-all-done = f32[128,1,512]{2,1,0:T(1,128)S(1)} async-done(((f32[128,1,512]{2,1,0:T(1,128)}), f32[128,1,512]{2,1,0:T(1,128)S(1)}, u32[]{:S(2)}, u32[]{:S(2)}) %all-to-all-start) | async-done | bytes 262176 | tf_op jit(solution)/shard_map/all_to_all | solution.py:394
  42.7 0.4 shard_map.105
  43.1 3.3 %collective-permute-start.1 = (f32[288,128]{1,0:T(8,128)S(1)}, f32[288,128]{1,0:T(8,128)S(1)}, u32[]{:S(2)}, u32[]{:S(2)}) collective-permute-start(f32[288,128]{1,0:T(8,128)S(1)} %get-tuple-element.35), channel_id=1, source_target_pairs={{4,8},{12,16},{20,24},{28,32},{36,40},{44,48},{52,56},{60,64},{68,... | collective-permute-start | bytes 442376 | tf_op jit(solution)/shard_map/ppermute | solution.py:381
  46.4 2.5 %collective-permute-start.2 = (f32[288,128]{1,0:T(8,128)S(1)}, f32[288,128]{1,0:T(8,128)S(1)}, u32[]{:S(2)}, u32[]{:S(2)}) collective-permute-start(f32[288,128]{1,0:T(8,128)S(1)} %get-tuple-element.36), channel_id=1, source_target_pairs={{0,4},{8,12},{16,20},{24,28},{32,36},{40,44},{48,52},{56,60},{64,6... | collective-permute-start | bytes 442376 | tf_op jit(solution)/shard_map/ppermute | solution.py:381
  48.9 7.9 %collective-permute-start = (f32[128,128]{1,0:T(8,128)S(1)}, f32[128,128]{1,0:T(8,128)S(1)}, u32[]{:S(2)}, u32[]{:S(2)}) collective-permute-start(f32[128,128]{1,0:T(8,128)S(1)} %get-tuple-element.34), channel_id=1, source_target_pairs={{1,2},{2,1},{5,6},{6,5},{9,10},{10,9},{13,14},{14,13},{17,18},{18,... | collective-permute-start | bytes 196616 | tf_op jit(solution)/shard_map/ppermute | solution.py:381
  56.8 1.9 %collective-permute-start.3 = (f32[128,128]{1,0:T(8,128)S(1)}, f32[128,128]{1,0:T(8,128)S(1)}, u32[]{:S(2)}, u32[]{:S(2)}) collective-permute-start(f32[128,128]{1,0:T(8,128)S(1)} %get-tuple-element.37), channel_id=1, source_target_pairs={{0,1},{2,3},{1,0},{3,2},{4,5},{6,7},{5,4},{7,6},{8,9},{10,11},{9,8... | collective-permute-start | bytes 196616 | tf_op jit(solution)/shard_map/ppermute | solution.py:381
  58.7 0.0 collective-permute-done.rows_b
  58.7 1.2 %collective-permute-done.3.rows_a = f32[128,128]{1,0:T(8,128)S(1)} collective-permute-done((f32[128,128]{1,0:T(8,128)S(1)}, f32[128,128]{1,0:T(8,128)S(1)}, u32[]{:S(2)}, u32[]{:S(2)}) %collective-permute-start.3) | collective-permute-done | bytes 65568 | tf_op jit(solution)/shard_map/ppermute | solution.py:381
  59.9 0.0 collective-permute-done.1.columns_b
  59.9 0.0 collective-permute-done.2.columns_a
  59.9 6.0 %shard_map.106 = (f32[512,128]{1,0:T(8,128)}, f32[48,128]{1,0:T(8,128)S(1)}, f32[16,128]{1,0:T(8,128)S(1)}, f32[16,128]{1,0:T(8,128)S(1)}) custom-call(s32[1]{0:T(128)} %bitcast.device.me, s32[1]{0:T(128)} %bitcast.1.band, f32[512,128]{1,0:T(8,128)S(1)} %bitcast.10, f32[128,128]{1,0:T(8,128)S(1)} %collective-permute-done.rows_b, ...), custom_call_target="tpu_custom_call" | custom-call | tf_op jit(solution)/shard_map/pallas_call | solution.py:410
  65.9 9.1 %all-to-all-start.1 = ((f32[128,1,512]{2,1,0:T(1,128)}), f32[128,1,512]{2,1,0:T(1,128)S(1)}, u32[]{:S(2)}, u32[]{:S(2)}) async-start(f32[128,1,512]{2,1,0:T(1,128)} %bitcast.4), calls=%async_computation.1 | async-start | bytes 524288 | tf_op jit(solution)/shard_map/all_to_all | solution.py:421
  75.1 0.0 copy-start.6
  75.1 5.2 %collective-permute-start.4 = (f32[16,128]{1,0:T(8,128)S(1)}, f32[16,128]{1,0:T(8,128)S(1)}, u32[]{:S(2)}, u32[]{:S(2)}) collective-permute-start(f32[16,128]{1,0:T(8,128)S(1)} %get-tuple-element.43), channel_id=1, source_target_pairs={{4,8},{12,16},{20,24},{28,32},{36,40},{44,48},{52,56},{60,64},{68,... | collective-permute-start | bytes 24584 | tf_op jit(solution)/shard_map/ppermute | solution.py:381
  80.3 1.9 %collective-permute-start.5 = (f32[16,128]{1,0:T(8,128)S(1)}, f32[16,128]{1,0:T(8,128)S(1)}, u32[]{:S(2)}, u32[]{:S(2)}) collective-permute-start(f32[16,128]{1,0:T(8,128)S(1)} %get-tuple-element.44), channel_id=1, source_target_pairs={{0,4},{8,12},{16,20},{24,28},{32,36},{40,44},{48,52},{56,60},{64,6... | collective-permute-start | bytes 24584 | tf_op jit(solution)/shard_map/ppermute | solution.py:381
  82.2 0.1 select_select_fusion
  82.3 0.1 reshape.116
  82.4 1.1 %collective-permute-done.4.drift_b = f32[16,128]{1,0:T(8,128)S(1)} collective-permute-done((f32[16,128]{1,0:T(8,128)S(1)}, f32[16,128]{1,0:T(8,128)S(1)}, u32[]{:S(2)}, u32[]{:S(2)}) %collective-permute-start.4) | collective-permute-done | bytes 8224 | tf_op jit(solution)/shard_map/ppermute | solution.py:381
  83.5 1.5 %collective-permute-done.5.drift_a = f32[16,128]{1,0:T(8,128)S(1)} collective-permute-done((f32[16,128]{1,0:T(8,128)S(1)}, f32[16,128]{1,0:T(8,128)S(1)}, u32[]{:S(2)}, u32[]{:S(2)}) %collective-permute-start.5) | collective-permute-done | bytes 8224 | tf_op jit(solution)/shard_map/ppermute | solution.py:381
  85.0 12.1 %all-to-all-done.1 = f32[128,1,512]{2,1,0:T(1,128)S(1)} async-done(((f32[128,1,512]{2,1,0:T(1,128)}), f32[128,1,512]{2,1,0:T(1,128)S(1)}, u32[]{:S(2)}, u32[]{:S(2)}) %all-to-all-start.1) | async-done | bytes 262176 | tf_op jit(solution)/shard_map/all_to_all | solution.py:421
  97.1 0.2 shard_map.107
  97.3 4.2 %collective-permute-start.6 = (f32[24,384]{1,0:T(8,128)S(1)}, f32[24,384]{1,0:T(8,128)S(1)}, u32[]{:S(2)}, u32[]{:S(2)}) collective-permute-start(f32[24,384]{1,0:T(8,128)S(1)} %get-tuple-element.47), channel_id=1, source_target_pairs={{1,2},{2,1},{5,6},{6,5},{9,10},{10,9},{13,14},{14,13},{17,18},{18,... | collective-permute-start | bytes 110600 | tf_op jit(solution)/shard_map/ppermute | solution.py:381
  101.5 1.9 %collective-permute-start.7 = (f32[24,384]{1,0:T(8,128)S(1)}, f32[24,384]{1,0:T(8,128)S(1)}, u32[]{:S(2)}, u32[]{:S(2)}) collective-permute-start(f32[24,384]{1,0:T(8,128)S(1)} %get-tuple-element.48), channel_id=1, source_target_pairs={{0,1},{2,3},{1,0},{3,2},{4,5},{6,7},{5,4},{7,6},{8,9},{10,11},{9,8... | collective-permute-start | bytes 110600 | tf_op jit(solution)/shard_map/ppermute | solution.py:381
  103.5 1.4 %shard_map.108.inside = f32[9,16,384]{2,1,0:T(8,128)S(1)} custom-call(s32[1]{0:T(128)} %bitcast.device.me, f32[2304]{0:T(1024)S(1)} %copy-done.2, f32[144,384]{1,0:T(8,128)S(1)} %get-tuple-element.45.middle, f32[16,384]{1,0:T(8,128)S(1)} %get-tuple-element.46.zonal, s32[16,384]{1,0:T(8,128)S(1)} %copy-done), custom_call_target="tpu_custom_call" | custom-call | flops 3317760 | bytes 442368 | tf_op jit(solution)/shard_map/pallas_call | solution.py:445
  104.8 1.7 %shard_map.109 = (f32[9,16,384]{2,1,0:T(8,128)}, f32[2,192,64]{2,1,0:T(8,128)}) custom-call(s32[1]{0:T(128)} %bitcast.device.me, s32[1]{0:T(128)} %bitcast.1.band, f32[2304]{0:T(1024)S(1)} %copy-done.2, f32[9,16,384]{2,1,0:T(8,128)S(1)} %shard_map.108.inside, f32[24,384]{1,0:T(8,128)S(1)} %collective-permute-done.6.rows_b, ...), custom_call_target="tpu_custom_call" | custom-call | tf_op jit(solution)/shard_map/pallas_call | solution.py:453
  (16 shorter events, 0.0 us)
Async XLA Ops:
  2.6 40.1 %all-to-all-start = ((f32[128,1,512]{2,1,0:T(1,128)}), f32[128,1,512]{2,1,0:T(1,128)S(1)}, u32[]{:S(2)}, u32[]{:S(2)}) async-start(f32[128,1,512]{2,1,0:T(1,128)} %bitcast.12), calls=%async_computation | async-start | bytes 524288 | tf_op jit(solution)/shard_map/all_to_all | solution.py:394
  22.1 0.7 copy-start.4
  22.1 0.7 copy-start.5
  42.7 17.2 %copy-start.1 = (bf16[128,256]{1,0:T(8,128)(2,1)S(1)}, bf16[128,256]{1,0:T(8,128)(2,1)}, u32[]{:S(2)}) copy-start(bf16[128,256]{1,0:T(8,128)(2,1)} %constant.73.clone.stencil) | copy-start | bytes 196612
  42.7 17.2 %copy-start.3 = (f32[8,1152]{1,0:T(8,128)S(1)}, f32[8,1152]{1,0:T(8,128)}, u32[]{:S(2)}) copy-start(f32[8,1152]{1,0:T(8,128)} %constant.74.clone.values) | copy-start | bytes 110596
  43.1 16.8 %collective-permute-start.1 = (f32[288,128]{1,0:T(8,128)S(1)}, f32[288,128]{1,0:T(8,128)S(1)}, u32[]{:S(2)}, u32[]{:S(2)}) collective-permute-start(f32[288,128]{1,0:T(8,128)S(1)} %get-tuple-element.35), channel_id=1, source_target_pairs={{4,8},{12,16},{20,24},{28,32},{36,40},{44,48},{52,56},{60,64},{68,... | collective-permute-start | bytes 442376 | tf_op jit(solution)/shard_map/ppermute | solution.py:381
  46.4 13.5 %collective-permute-start.2 = (f32[288,128]{1,0:T(8,128)S(1)}, f32[288,128]{1,0:T(8,128)S(1)}, u32[]{:S(2)}, u32[]{:S(2)}) collective-permute-start(f32[288,128]{1,0:T(8,128)S(1)} %get-tuple-element.36), channel_id=1, source_target_pairs={{0,4},{8,12},{16,20},{24,28},{32,36},{40,44},{48,52},{56,60},{64,6... | collective-permute-start | bytes 442376 | tf_op jit(solution)/shard_map/ppermute | solution.py:381
  48.9 9.8 %collective-permute-start = (f32[128,128]{1,0:T(8,128)S(1)}, f32[128,128]{1,0:T(8,128)S(1)}, u32[]{:S(2)}, u32[]{:S(2)}) collective-permute-start(f32[128,128]{1,0:T(8,128)S(1)} %get-tuple-element.34), channel_id=1, source_target_pairs={{1,2},{2,1},{5,6},{6,5},{9,10},{10,9},{13,14},{14,13},{17,18},{18,... | collective-permute-start | bytes 196616 | tf_op jit(solution)/shard_map/ppermute | solution.py:381
  56.8 3.1 %collective-permute-start.3 = (f32[128,128]{1,0:T(8,128)S(1)}, f32[128,128]{1,0:T(8,128)S(1)}, u32[]{:S(2)}, u32[]{:S(2)}) collective-permute-start(f32[128,128]{1,0:T(8,128)S(1)} %get-tuple-element.37), channel_id=1, source_target_pairs={{0,1},{2,3},{1,0},{3,2},{4,5},{6,7},{5,4},{7,6},{8,9},{10,11},{9,8... | collective-permute-start | bytes 196616 | tf_op jit(solution)/shard_map/ppermute | solution.py:381
  65.9 31.2 %all-to-all-start.1 = ((f32[128,1,512]{2,1,0:T(1,128)}), f32[128,1,512]{2,1,0:T(1,128)S(1)}, u32[]{:S(2)}, u32[]{:S(2)}) async-start(f32[128,1,512]{2,1,0:T(1,128)} %bitcast.4), calls=%async_computation.1 | async-start | bytes 524288 | tf_op jit(solution)/shard_map/all_to_all | solution.py:421
  75.1 7.2 %copy-start.6 = (s32[6,32]{1,0:T(8,128)S(1)}, s32[6,32]{1,0:T(8,128)}, u32[]{:S(2)}) copy-start(s32[6,32]{1,0:T(8,128)} %param.14) | copy-start | bytes 2308
  75.1 8.4 %collective-permute-start.4 = (f32[16,128]{1,0:T(8,128)S(1)}, f32[16,128]{1,0:T(8,128)S(1)}, u32[]{:S(2)}, u32[]{:S(2)}) collective-permute-start(f32[16,128]{1,0:T(8,128)S(1)} %get-tuple-element.43), channel_id=1, source_target_pairs={{4,8},{12,16},{20,24},{28,32},{36,40},{44,48},{52,56},{60,64},{68,... | collective-permute-start | bytes 24584 | tf_op jit(solution)/shard_map/ppermute | solution.py:381
  80.3 4.7 %collective-permute-start.5 = (f32[16,128]{1,0:T(8,128)S(1)}, f32[16,128]{1,0:T(8,128)S(1)}, u32[]{:S(2)}, u32[]{:S(2)}) collective-permute-start(f32[16,128]{1,0:T(8,128)S(1)} %get-tuple-element.44), channel_id=1, source_target_pairs={{0,4},{8,12},{16,20},{24,28},{32,36},{40,44},{48,52},{56,60},{64,6... | collective-permute-start | bytes 24584 | tf_op jit(solution)/shard_map/ppermute | solution.py:381
  97.1 6.4 %copy-start = (s32[16,384]{1,0:T(8,128)S(1)}, s32[16,384]{1,0:T(8,128)}, u32[]{:S(2)}) copy-start(s32[16,384]{1,0:T(8,128)} %mask.5) | copy-start | bytes 73732
  97.1 6.4 %copy-start.2 = (f32[2304]{0:T(1024)S(1)}, f32[2304]{0:T(1024)}, u32[]{:S(2)}) copy-start(f32[2304]{0:T(1024)} %constant.75.clone.speeds) | copy-start | bytes 27652
  97.3 7.5 %collective-permute-start.6 = (f32[24,384]{1,0:T(8,128)S(1)}, f32[24,384]{1,0:T(8,128)S(1)}, u32[]{:S(2)}, u32[]{:S(2)}) collective-permute-start(f32[24,384]{1,0:T(8,128)S(1)} %get-tuple-element.47), channel_id=1, source_target_pairs={{1,2},{2,1},{5,6},{6,5},{9,10},{10,9},{13,14},{14,13},{17,18},{18,... | collective-permute-start | bytes 110600 | tf_op jit(solution)/shard_map/ppermute | solution.py:381
  101.5 3.3 %collective-permute-start.7 = (f32[24,384]{1,0:T(8,128)S(1)}, f32[24,384]{1,0:T(8,128)S(1)}, u32[]{:S(2)}, u32[]{:S(2)}) collective-permute-start(f32[24,384]{1,0:T(8,128)S(1)} %get-tuple-element.48), channel_id=1, source_target_pairs={{0,1},{2,3},{1,0},{3,2},{4,5},{6,7},{5,4},{7,6},{8,9},{10,11},{9,8... | collective-permute-start | bytes 110600 | tf_op jit(solution)/shard_map/ppermute | solution.py:381

commit v9 on v8

--- a/solution.py
+++ b/solution.py
@@ -144,9 +144,20 @@
     rows_a[...], rows_b[...] = swapped((band[0] & 1) == 1, *edges)
 
 
+def columns_kernel(plus, minus, values, speeds, plus_col, minus_col):
+    inner = lax.broadcasted_iota(jnp.int32, (128, 128), 0)
+    for t in range(OWN):
+        rows = slice(128 * t, 128 * t + 128)
+        part = jnp.where(inner < 64, values[0:1, rows], values[1:2, rows])
+        speeds[rows, :] = jnp.where(inner == 127, values[2:3, rows], part).T
+        for row, col in ((plus, plus_col), (minus, minus_col)):
+            column = jnp.broadcast_to(row[:, rows].astype(F32), (128, 128)).T
+            col[rows, :] = column.astype(jnp.int32).astype(jnp.int16)
+
+
 def points_kernel(
-    me, band, arrived, rows_b, columns_b, columns_a, rows_a, sea_row, plus, minus, stencil, values,
-    out, drift_out, drift_b, drift_a, first, source, middle, halves, speeds, plus_col, minus_col,
+    me, band, arrived, rows_b, columns_b, columns_a, rows_a, sea_row, plus, minus, stencil, speeds, plus_col, minus_col,
+    out, halves, first, source, middle,
 ):
     device = me[0]
     odd = (device & 1) == 1
@@ -200,7 +211,6 @@
             acc = jnp.where((lane >= at) & (lane < at + 6), pltpu.roll(beyond, (at - held) % 128, 1), acc)
         middle[pl.ds(i, OWNERS, stride=OWN), :] = acc
 
-    inner = lax.broadcasted_iota(jnp.int32, (128, 128), 0)
     for t in range(OWN):
         value = middle[chunk(t), :]
         upper_half = value.astype(BF16)
@@ -208,10 +218,6 @@
         sums = jnp.dot(upper_half, stencil[...], preferred_element_type=F32) + jnp.dot(
             lower_half, stencil[...], preferred_element_type=F32
         )
-        part = jnp.where(inner < 64, values[0:1, chunk(t)], values[1:2, chunk(t)])
-        speeds[chunk(t), :] = jnp.where(inner == 127, values[2:3, chunk(t)], part).T
-        for row, col in ((plus, plus_col), (minus, minus_col)):
-            col[chunk(t), :] = jnp.broadcast_to(row[:, chunk(t)].astype(F32), (128, 128)).T
         speed = (speeds[chunk(t), :] + faces) * (1.0 / 6.0)
         flux = jnp.maximum(speed, 0.0) * sums[:, 0:128] + jnp.minimum(speed, 0.0) * sums[:, 128:256]
         change = (pltpu.roll(flux, 112, 1) - flux) + pltpu.roll(flux, 64, 1)
@@ -223,7 +229,7 @@
     one, none = jnp.ones((128, BINS), BF16), jnp.zeros((128, BINS), BF16)
 
     def gathered(col, t):
-        wide = jnp.concatenate([col[chunk(t), :].astype(jnp.int32).astype(jnp.int16)] * OWN, axis=1)
+        wide = jnp.concatenate([col[chunk(t), :]] * OWN, axis=1)
         chosen = jnp.where(wide == numbers, one, none)
         return joined(jnp.dot(chosen, halves[...], preferred_element_type=F32))
 
@@ -244,17 +250,6 @@
         middle[chunk(t), :] = first[chunk(t), :] + (source[chunk(t), :] - 0.5 * back)
     for t in range(OWN):
         split_into(halves, chunk(t), middle[chunk(t), :])
-    level = lax.broadcasted_iota(jnp.int32, (LEV, BINS), 0).astype(F32) + 0.5
-    decay = jnp.exp(level * values[3:4, :])
-    table = jnp.concatenate([decay * values[4:5, :], decay * values[5:6, :]], axis=0)
-    table_upper = table.astype(BF16)
-    table_lower = (table - table_upper.astype(F32)).astype(BF16)
-    drift = joined(jnp.dot(table_upper, halves[...], preferred_element_type=F32))
-    drift = drift + jnp.dot(table_lower, halves[:, 0:128], preferred_element_type=F32)
-    turned = drift.T[0:48]
-    drift_out[...] = turned
-    drift_a[...], drift_b[...] = swapped(odd, turned[32:48], turned[0:16])
-
     accs = [jnp.zeros((OWNERS, 128), F32)] * COLS
     for i in range(8):
         value = middle[pl.ds(i, OWNERS, stride=OWN), :]
@@ -267,6 +262,19 @@
     for c in range(COLS):
         acc = jnp.where(group == 2 * c, pltpu.roll(last, 16 * c, 1), acc)
     out[pl.ds(3, OWNERS, stride=4), :] = acc
+
+
+def drift_kernel(me, halves, values, drift_out, drift_b, drift_a):
+    level = lax.broadcasted_iota(jnp.int32, (LEV, BINS), 0).astype(F32) + 0.5
+    decay = jnp.exp(level * values[3:4, :])
+    table = jnp.concatenate([decay * values[4:5, :], decay * values[5:6, :]], axis=0)
+    table_upper = table.astype(BF16)
+    table_lower = (table - table_upper.astype(F32)).astype(BF16)
+    drift = joined(jnp.dot(table_upper, halves[...], preferred_element_type=F32))
+    drift = drift + jnp.dot(table_lower, halves[:, 0:128], preferred_element_type=F32)
+    turned = drift.T[0:48]
+    drift_out[...] = turned
+    drift_a[...], drift_b[...] = swapped((me[0] & 1) == 1, turned[32:48], turned[0:16])
 
 
 def unpack_kernel(
@@ -394,7 +402,13 @@
     arrived = lax.all_to_all(sent.reshape(OWNERS, 1, 512), "bins", 0, 0).reshape(4 * OWNERS, 128)
     plus, minus = plus.reshape(1, BINS), minus.reshape(1, BINS)
     sea = lax.dynamic_slice(masks, (device[0], 0), (1, 128))
-    arrived, plus, minus, sea = lax.optimization_barrier((arrived, plus, minus, sea))
+    number = jax.ShapeDtypeStruct((BINS, 128), jnp.int16)
+    columns = pl.pallas_call(
+        columns_kernel,
+        out_shape=shapes((BINS, 128)) + [number, number],
+        compiler_params=grant,
+    )(plus, minus, jnp.asarray(held_values))
+    arrived, plus, minus, sea, *columns = lax.optimization_barrier((arrived, plus, minus, sea, *columns))
     rows_b, columns_b, columns_a, rows_a = pl.pallas_call(
         edges_kernel,
         out_shape=shapes((OWNERS, 128), (288, 128), (288, 128), (OWNERS, 128)),
@@ -407,18 +421,24 @@
     rows_a = swap(rows_a, "lat", 0)
 
     big = pltpu.VMEM((BINS, 128), F32)
-    sent, drift, drift_b, drift_a = pl.pallas_call(
+    sent, halves = pl.pallas_call(
         points_kernel,
-        out_shape=shapes((4 * OWNERS, 128), (48, 128), (16, 128), (16, 128)),
-        in_specs=[smem, smem] + [vmem] * 10,
-        scratch_shapes=[big, big, big, pltpu.VMEM((BINS, 256), BF16), big, big, big],
+        out_shape=[jax.ShapeDtypeStruct((4 * OWNERS, 128), F32), jax.ShapeDtypeStruct((BINS, 256), BF16)],
+        in_specs=[smem, smem] + [vmem] * 12,
+        scratch_shapes=[big, big, big],
         compiler_params=pltpu.CompilerParams(vmem_limit_bytes=24 * 1024 * 1024),
     )(
         device, band, arrived, rows_b, columns_b, columns_a, rows_a, sea, plus, minus,
-        jnp.asarray(stencil), jnp.asarray(held_values),
+        jnp.asarray(stencil), *columns,
     )
 
     arrived = lax.all_to_all(sent.reshape(OWNERS, 1, 512), "bins", 0, 0).reshape(4 * OWNERS, 128)
+    drift, drift_b, drift_a = pl.pallas_call(
+        drift_kernel,
+        out_shape=shapes((48, 128), (16, 128), (16, 128)),
+        in_specs=[smem, vmem, vmem],
+        compiler_params=grant,
+    )(device, halves, jnp.asarray(held_values))
     drift_b = swap(drift_b, "bins", 1)
     drift_a = swap(drift_a, "bins", 0)
 

time: 107 us -> 107 us (level)
    pallas_call x1 -> x3, Pallas kernels: 5.98 us -> 6.34 us  [the longest x1 5.43 us: on_device(): pl.pallas_call(points_kernel, out_shape=[jax.ShapeDtypeStruct((4 * OWNERS...]
  transfers between devices with their start and end apart: 10 -> 10, of which waited for: 5 -> 5; matrix products, arithmetic and copies ran while one was open for 1% -> 1% of each run, Pallas kernels for 1% -> 2%
where the time goes in v9:
time: 107 us; the launch traced here: 106 us
  starting transfers between devices  57.5 us (54%)
  waiting for transfers between devices  34.2 us (32%)
  Pallas kernels  12 us (11%)
  local copies, waits for them, and re-layouts  1.52 us (1%)
    all_to_all x2, waiting for transfers between devices, on_device(): lax.all_to_all(sent.reshape(OWNERS, 1, 512), 'bins', 0, 0)  30.3 us
    ppermute x8, starting transfers between devices, swap(): return lax.ppermute(x, axis, pairs + [(j, i) for i, j in pairs])  28.8 us
    all_to_all x2, starting transfers between devices, on_device(): lax.all_to_all(sent.reshape(OWNERS, 1, 512), 'bins', 0, 0)  28.7 us
    pallas_call x1, Pallas kernels, on_device(): pl.pallas_call(points_kernel, out_shape=[jax.ShapeDtypeStruct((4 * OWNERS...  5.43 us
    ppermute x8, waiting for transfers between devices, swap(): return lax.ppermute(x, axis, pairs + [(j, i) for i, j in pairs])  3.83 us
  transfers between devices with their start and end apart: 10, of which 5 were waited for; matrix products, arithmetic and copies ran while one was open for 1% of the time, Pallas kernels for 2%

profile of v9, /device:TPU:33, one launch (start us, length us, event | category | flops | bytes accessed | tf_op | source)
XLA Modules:
  0.0 106.1 jit_solution(16483125238142299109)
XLA Ops:
  0.6 2.0 %shard_map.104 = (f32[512,128]{1,0:T(8,128)}, f32[128,128]{1,0:T(8,128)}) custom-call(f32[9,16,384]{2,1,0:T(8,128)} %spec.1, s32[16,384]{1,0:T(8,128)} %mask.5, f32[6,32]{1,0:T(8,128)} %current.1), custom_call_target="tpu_custom_call" | custom-call | tf_op jit(solution)/shard_map/pallas_call | solution.py:394
  2.6 19.6 %all-to-all-start = ((f32[128,1,512]{2,1,0:T(1,128)}), f32[128,1,512]{2,1,0:T(1,128)S(1)}, u32[]{:S(2)}, u32[]{:S(2)}) async-start(f32[128,1,512]{2,1,0:T(1,128)} %bitcast.12), calls=%async_computation | async-start | bytes 524288 | tf_op jit(solution)/shard_map/all_to_all | solution.py:402
  22.2 0.0 copy-start.1
  22.3 0.7 copy-done.1
  23.0 0.5 shard_map.105
  23.5 0.7 constant_dynamic-slice_fusion.sea_row
  24.2 18.6 %all-to-all-done = f32[128,1,512]{2,1,0:T(1,128)S(1)} async-done(((f32[128,1,512]{2,1,0:T(1,128)}), f32[128,1,512]{2,1,0:T(1,128)S(1)}, u32[]{:S(2)}, u32[]{:S(2)}) %all-to-all-start) | async-done | bytes 262176 | tf_op jit(solution)/shard_map/all_to_all | solution.py:402
  42.9 0.4 shard_map.106
  43.2 3.3 %collective-permute-start.1 = (f32[288,128]{1,0:T(8,128)S(1)}, f32[288,128]{1,0:T(8,128)S(1)}, u32[]{:S(2)}, u32[]{:S(2)}) collective-permute-start(f32[288,128]{1,0:T(8,128)S(1)} %get-tuple-element.45), channel_id=1, source_target_pairs={{4,8},{12,16},{20,24},{28,32},{36,40},{44,48},{52,56},{60,64},{68,... | collective-permute-start | bytes 442376 | tf_op jit(solution)/shard_map/ppermute | solution.py:389
  46.5 2.5 %collective-permute-start.2 = (f32[288,128]{1,0:T(8,128)S(1)}, f32[288,128]{1,0:T(8,128)S(1)}, u32[]{:S(2)}, u32[]{:S(2)}) collective-permute-start(f32[288,128]{1,0:T(8,128)S(1)} %get-tuple-element.46), channel_id=1, source_target_pairs={{0,4},{8,12},{16,20},{24,28},{32,36},{40,44},{48,52},{56,60},{64,6... | collective-permute-start | bytes 442376 | tf_op jit(solution)/shard_map/ppermute | solution.py:389
  49.0 7.9 %collective-permute-start = (f32[128,128]{1,0:T(8,128)S(1)}, f32[128,128]{1,0:T(8,128)S(1)}, u32[]{:S(2)}, u32[]{:S(2)}) collective-permute-start(f32[128,128]{1,0:T(8,128)S(1)} %get-tuple-element.44), channel_id=1, source_target_pairs={{1,2},{2,1},{5,6},{6,5},{9,10},{10,9},{13,14},{14,13},{17,18},{18,... | collective-permute-start | bytes 196616 | tf_op jit(solution)/shard_map/ppermute | solution.py:389
  56.9 1.9 %collective-permute-start.3 = (f32[128,128]{1,0:T(8,128)S(1)}, f32[128,128]{1,0:T(8,128)S(1)}, u32[]{:S(2)}, u32[]{:S(2)}) collective-permute-start(f32[128,128]{1,0:T(8,128)S(1)} %get-tuple-element.47), channel_id=1, source_target_pairs={{0,1},{2,3},{1,0},{3,2},{4,5},{6,7},{5,4},{7,6},{8,9},{10,11},{9,8... | collective-permute-start | bytes 196616 | tf_op jit(solution)/shard_map/ppermute | solution.py:389
  58.8 0.0 collective-permute-done.rows_b
  58.8 1.2 %collective-permute-done.3.rows_a = f32[128,128]{1,0:T(8,128)S(1)} collective-permute-done((f32[128,128]{1,0:T(8,128)S(1)}, f32[128,128]{1,0:T(8,128)S(1)}, u32[]{:S(2)}, u32[]{:S(2)}) %collective-permute-start.3) | collective-permute-done | bytes 65568 | tf_op jit(solution)/shard_map/ppermute | solution.py:389
  60.1 0.0 collective-permute-done.1.columns_b
  60.1 5.4 %shard_map.107 = (f32[512,128]{1,0:T(8,128)}, bf16[1152,256]{1,0:T(8,128)(2,1)S(1)}) custom-call(s32[1]{0:T(128)} %bitcast.device.me, s32[1]{0:T(128)} %bitcast.1.band, f32[512,128]{1,0:T(8,128)S(1)} %bitcast.10, f32[128,128]{1,0:T(8,128)S(1)} %collective-permute-done.rows_b, f32[288,128]{1,0:T(8,128)S(1)} %collective-permute-done.1.columns_b, ...), custom_call_target="tpu_custom_call" | custom-call | tf_op jit(solution)/shard_map/pallas_call | solution.py:424
  65.5 9.1 %all-to-all-start.1 = ((f32[128,1,512]{2,1,0:T(1,128)}), f32[128,1,512]{2,1,0:T(1,128)S(1)}, u32[]{:S(2)}, u32[]{:S(2)}) async-start(f32[128,1,512]{2,1,0:T(1,128)} %bitcast.4), calls=%async_computation.1 | async-start | bytes 524288 | tf_op jit(solution)/shard_map/all_to_all | solution.py:435
  74.7 0.0 copy-start.6
  74.7 0.4 shard_map.108
  75.0 5.2 %collective-permute-start.4 = (f32[16,128]{1,0:T(8,128)S(1)}, f32[16,128]{1,0:T(8,128)S(1)}, u32[]{:S(2)}, u32[]{:S(2)}) collective-permute-start(f32[16,128]{1,0:T(8,128)S(1)} %get-tuple-element.57), channel_id=1, source_target_pairs={{4,8},{12,16},{20,24},{28,32},{36,40},{44,48},{52,56},{60,64},{68,... | collective-permute-start | bytes 24584 | tf_op jit(solution)/shard_map/ppermute | solution.py:389
  80.3 1.9 %collective-permute-start.5 = (f32[16,128]{1,0:T(8,128)S(1)}, f32[16,128]{1,0:T(8,128)S(1)}, u32[]{:S(2)}, u32[]{:S(2)}) collective-permute-start(f32[16,128]{1,0:T(8,128)S(1)} %get-tuple-element.58), channel_id=1, source_target_pairs={{0,4},{8,12},{16,20},{24,28},{32,36},{40,44},{48,52},{56,60},{64,6... | collective-permute-start | bytes 24584 | tf_op jit(solution)/shard_map/ppermute | solution.py:389
  82.2 0.1 select_select_fusion
  82.3 0.1 reshape.116
  82.4 0.8 collective-permute-done.4.drift_b
  83.1 1.8 %collective-permute-done.5.drift_a = f32[16,128]{1,0:T(8,128)S(1)} collective-permute-done((f32[16,128]{1,0:T(8,128)S(1)}, f32[16,128]{1,0:T(8,128)S(1)}, u32[]{:S(2)}, u32[]{:S(2)}) %collective-permute-start.5) | collective-permute-done | bytes 8224 | tf_op jit(solution)/shard_map/ppermute | solution.py:389
  85.0 11.7 %all-to-all-done.1 = f32[128,1,512]{2,1,0:T(1,128)S(1)} async-done(((f32[128,1,512]{2,1,0:T(1,128)}), f32[128,1,512]{2,1,0:T(1,128)S(1)}, u32[]{:S(2)}, u32[]{:S(2)}) %all-to-all-start.1) | async-done | bytes 262176 | tf_op jit(solution)/shard_map/all_to_all | solution.py:435
  96.6 0.2 shard_map.109
  96.9 4.2 %collective-permute-start.6 = (f32[24,384]{1,0:T(8,128)S(1)}, f32[24,384]{1,0:T(8,128)S(1)}, u32[]{:S(2)}, u32[]{:S(2)}) collective-permute-start(f32[24,384]{1,0:T(8,128)S(1)} %get-tuple-element.61), channel_id=1, source_target_pairs={{1,2},{2,1},{5,6},{6,5},{9,10},{10,9},{13,14},{14,13},{17,18},{18,... | collective-permute-start | bytes 110600 | tf_op jit(solution)/shard_map/ppermute | solution.py:389
  101.1 1.9 %collective-permute-start.7 = (f32[24,384]{1,0:T(8,128)S(1)}, f32[24,384]{1,0:T(8,128)S(1)}, u32[]{:S(2)}, u32[]{:S(2)}) collective-permute-start(f32[24,384]{1,0:T(8,128)S(1)} %get-tuple-element.62), channel_id=1, source_target_pairs={{0,1},{2,3},{1,0},{3,2},{4,5},{6,7},{5,4},{7,6},{8,9},{10,11},{9,8... | collective-permute-start | bytes 110600 | tf_op jit(solution)/shard_map/ppermute | solution.py:389
  103.0 1.4 %shard_map.110.inside = f32[9,16,384]{2,1,0:T(8,128)S(1)} custom-call(s32[1]{0:T(128)} %bitcast.device.me, f32[2304]{0:T(1024)S(1)} %copy-done.3, f32[144,384]{1,0:T(8,128)S(1)} %get-tuple-element.59.middle, f32[16,384]{1,0:T(8,128)S(1)} %get-tuple-element.60.zonal, s32[16,384]{1,0:T(8,128)S(1)} %copy-done), custom_call_target="tpu_custom_call" | custom-call | flops 3317760 | bytes 442368 | tf_op jit(solution)/shard_map/pallas_call | solution.py:465
  104.4 0.0 collective-permute-done.6.rows_b
  104.4 1.7 %shard_map.111 = (f32[9,16,384]{2,1,0:T(8,128)}, f32[2,192,64]{2,1,0:T(8,128)}) custom-call(s32[1]{0:T(128)} %bitcast.device.me, s32[1]{0:T(128)} %bitcast.1.band, f32[2304]{0:T(1024)S(1)} %copy-done.3, f32[9,16,384]{2,1,0:T(8,128)S(1)} %shard_map.110.inside, f32[24,384]{1,0:T(8,128)S(1)} %collective-permute-done.6.rows_b, ...), custom_call_target="tpu_custom_call" | custom-call | tf_op jit(solution)/shard_map/pallas_call | solution.py:473
  (18 shorter events, 0.0 us)
Async XLA Ops:
  2.6 19.6 %copy-start.4 = (s32[1152]{0:T(1024)S(1)}, s32[1152]{0:T(1024)}, u32[]{:S(2)}) copy-start(s32[1152]{0:T(1024)} %param.12) | copy-start | bytes 13828
  2.6 19.6 %copy-start.5 = (s32[1152]{0:T(1024)S(1)}, s32[1152]{0:T(1024)}, u32[]{:S(2)}) copy-start(s32[1152]{0:T(1024)} %param.13) | copy-start | bytes 13828
  2.6 40.2 %all-to-all-start = ((f32[128,1,512]{2,1,0:T(1,128)}), f32[128,1,512]{2,1,0:T(1,128)S(1)}, u32[]{:S(2)}, u32[]{:S(2)}) async-start(f32[128,1,512]{2,1,0:T(1,128)} %bitcast.12), calls=%async_computation | async-start | bytes 524288 | tf_op jit(solution)/shard_map/all_to_all | solution.py:402
  22.2 0.8 copy-start.1
  42.9 17.2 %copy-start.2 = (bf16[128,256]{1,0:T(8,128)(2,1)S(1)}, bf16[128,256]{1,0:T(8,128)(2,1)}, u32[]{:S(2)}) copy-start(bf16[128,256]{1,0:T(8,128)(2,1)} %constant.74.clone.stencil) | copy-start | bytes 196612
  43.2 16.8 %collective-permute-start.1 = (f32[288,128]{1,0:T(8,128)S(1)}, f32[288,128]{1,0:T(8,128)S(1)}, u32[]{:S(2)}, u32[]{:S(2)}) collective-permute-start(f32[288,128]{1,0:T(8,128)S(1)} %get-tuple-element.45), channel_id=1, source_target_pairs={{4,8},{12,16},{20,24},{28,32},{36,40},{44,48},{52,56},{60,64},{68,... | collective-permute-start | bytes 442376 | tf_op jit(solution)/shard_map/ppermute | solution.py:389
  46.5 13.5 %collective-permute-start.2 = (f32[288,128]{1,0:T(8,128)S(1)}, f32[288,128]{1,0:T(8,128)S(1)}, u32[]{:S(2)}, u32[]{:S(2)}) collective-permute-start(f32[288,128]{1,0:T(8,128)S(1)} %get-tuple-element.46), channel_id=1, source_target_pairs={{0,4},{8,12},{16,20},{24,28},{32,36},{40,44},{48,52},{56,60},{64,6... | collective-permute-start | bytes 442376 | tf_op jit(solution)/shard_map/ppermute | solution.py:389
  49.0 9.8 %collective-permute-start = (f32[128,128]{1,0:T(8,128)S(1)}, f32[128,128]{1,0:T(8,128)S(1)}, u32[]{:S(2)}, u32[]{:S(2)}) collective-permute-start(f32[128,128]{1,0:T(8,128)S(1)} %get-tuple-element.44), channel_id=1, source_target_pairs={{1,2},{2,1},{5,6},{6,5},{9,10},{10,9},{13,14},{14,13},{17,18},{18,... | collective-permute-start | bytes 196616 | tf_op jit(solution)/shard_map/ppermute | solution.py:389
  56.9 3.1 %collective-permute-start.3 = (f32[128,128]{1,0:T(8,128)S(1)}, f32[128,128]{1,0:T(8,128)S(1)}, u32[]{:S(2)}, u32[]{:S(2)}) collective-permute-start(f32[128,128]{1,0:T(8,128)S(1)} %get-tuple-element.47), channel_id=1, source_target_pairs={{0,1},{2,3},{1,0},{3,2},{4,5},{6,7},{5,4},{7,6},{8,9},{10,11},{9,8... | collective-permute-start | bytes 196616 | tf_op jit(solution)/shard_map/ppermute | solution.py:389
  65.5 31.1 %all-to-all-start.1 = ((f32[128,1,512]{2,1,0:T(1,128)}), f32[128,1,512]{2,1,0:T(1,128)S(1)}, u32[]{:S(2)}, u32[]{:S(2)}) async-start(f32[128,1,512]{2,1,0:T(1,128)} %bitcast.4), calls=%async_computation.1 | async-start | bytes 524288 | tf_op jit(solution)/shard_map/all_to_all | solution.py:435
  74.7 7.5 %copy-start.6 = (s32[6,32]{1,0:T(8,128)S(1)}, s32[6,32]{1,0:T(8,128)}, u32[]{:S(2)}) copy-start(s32[6,32]{1,0:T(8,128)} %param.14) | copy-start | bytes 2308
  75.0 8.1 %collective-permute-start.4 = (f32[16,128]{1,0:T(8,128)S(1)}, f32[16,128]{1,0:T(8,128)S(1)}, u32[]{:S(2)}, u32[]{:S(2)}) collective-permute-start(f32[16,128]{1,0:T(8,128)S(1)} %get-tuple-element.57), channel_id=1, source_target_pairs={{4,8},{12,16},{20,24},{28,32},{36,40},{44,48},{52,56},{60,64},{68,... | collective-permute-start | bytes 24584 | tf_op jit(solution)/shard_map/ppermute | solution.py:389
  80.3 4.7 %collective-permute-start.5 = (f32[16,128]{1,0:T(8,128)S(1)}, f32[16,128]{1,0:T(8,128)S(1)}, u32[]{:S(2)}, u32[]{:S(2)}) collective-permute-start(f32[16,128]{1,0:T(8,128)S(1)} %get-tuple-element.58), channel_id=1, source_target_pairs={{0,4},{8,12},{16,20},{24,28},{32,36},{40,44},{48,52},{56,60},{64,6... | collective-permute-start | bytes 24584 | tf_op jit(solution)/shard_map/ppermute | solution.py:389
  96.6 6.4 %copy-start = (s32[16,384]{1,0:T(8,128)S(1)}, s32[16,384]{1,0:T(8,128)}, u32[]{:S(2)}) copy-start(s32[16,384]{1,0:T(8,128)} %mask.5) | copy-start | bytes 73732
  96.6 6.4 %copy-start.3 = (f32[2304]{0:T(1024)S(1)}, f32[2304]{0:T(1024)}, u32[]{:S(2)}) copy-start(f32[2304]{0:T(1024)} %constant.75.clone.speeds) | copy-start | bytes 27652
  96.9 7.5 %collective-permute-start.6 = (f32[24,384]{1,0:T(8,128)S(1)}, f32[24,384]{1,0:T(8,128)S(1)}, u32[]{:S(2)}, u32[]{:S(2)}) collective-permute-start(f32[24,384]{1,0:T(8,128)S(1)} %get-tuple-element.61), channel_id=1, source_target_pairs={{1,2},{2,1},{5,6},{6,5},{9,10},{10,9},{13,14},{14,13},{17,18},{18,... | collective-permute-start | bytes 110600 | tf_op jit(solution)/shard_map/ppermute | solution.py:389
  101.1 3.3 %collective-permute-start.7 = (f32[24,384]{1,0:T(8,128)S(1)}, f32[24,384]{1,0:T(8,128)S(1)}, u32[]{:S(2)}, u32[]{:S(2)}) collective-permute-start(f32[24,384]{1,0:T(8,128)S(1)} %get-tuple-element.62), channel_id=1, source_target_pairs={{0,1},{2,3},{1,0},{3,2},{4,5},{6,7},{5,4},{7,6},{8,9},{10,11},{9,8... | collective-permute-start | bytes 110600 | tf_op jit(solution)/shard_map/ppermute | solution.py:389

commit v10 on v9

--- a/solution.py
+++ b/solution.py
@@ -301,7 +301,9 @@
     rows_a[...], rows_b[...] = swapped((band[0] & 1) == 1, high[...], low[...])
 
 
-def inside_kernel(me, speeds, middle, zonal, mask, out, rows):
+def final_kernel(
+    me, band, speeds, middle, zonal, rows_b, rows_a, mask, drift, place, out, stokes, near, low, high, rows
+):
     first_bin = me[0] * OWN
     sea = mask[...].astype(F32)
     column = lax.broadcasted_iota(jnp.int32, (ROWS, NLON), 1)
@@ -313,11 +315,12 @@
     flow = zonal[...]
     lower_flow = 0.5 * (beside(flow, -1) + flow)
     upper_flow = 0.5 * (flow + beside(flow, 1))
-    rows[0:8, :] = jnp.zeros((8, NLON), F32)
-    rows[24:32, :] = jnp.zeros((8, NLON), F32)
+    low[...], high[...] = swapped((band[0] & 1) == 1, rows_b[...], rows_a[...])
     for i in range(OWN):
         f = middle[16 * i : 16 * i + 16, :]
         rows[8:24, :] = f
+        rows[6:8, :] = low[2 * i : 2 * i + 2, :]
+        rows[24:26, :] = high[2 * i : 2 * i + 2, :]
         along_x = speeds[first_bin + i]
         along_y = speeds[BINS + first_bin + i]
         r2, r1, u1, u2 = rows[6:22, :], rows[7:23, :], rows[9:25, :], rows[10:26, :]
@@ -336,23 +339,6 @@
             jnp.maximum(speed, 0.0) * (5.0 * a1 + 2.0 * f - a2) + jnp.minimum(speed, 0.0) * (2.0 * a1 + 5.0 * f - b1)
         )
         out[i] = sea * (f - change)
-
-
-def final_kernel(me, band, speeds, inside, rows_b, rows_a, mask, drift, place, out, stokes, near, low, high):
-    first_bin = me[0] * OWN
-    sea = mask[...].astype(F32)
-    low[...], high[...] = swapped((band[0] & 1) == 1, rows_b[...], rows_a[...])
-    out[...] = inside[...]
-    for i in range(OWN):
-        along_y = speeds[BINS + first_bin + i]
-        forward = jnp.maximum(along_y, 0.0) * (1.0 / 6.0)
-        backward = jnp.minimum(along_y, 0.0) * (1.0 / 6.0)
-        r2, r1 = low[2 * i : 2 * i + 1, :], low[2 * i + 1 : 2 * i + 2, :]
-        u1, u2 = high[2 * i : 2 * i + 1, :], high[2 * i + 1 : 2 * i + 2, :]
-        lower = jnp.concatenate([forward * (r2 - 6.0 * r1) - backward * (2.0 * r1), forward * r1], axis=0)
-        upper = jnp.concatenate([-backward * u1, forward * (2.0 * u1) + backward * (6.0 * u1 - u2)], axis=0)
-        out[i, 0:2, :] = inside[i, 0:2, :] - sea[0:2] * lower
-        out[i, 14:16, :] = inside[i, 14:16, :] - sea[14:16] * upper
 
     near[0:80, :] = drift[...]
     near[80:128, :] = jnp.zeros((48, 128), F32)
@@ -462,21 +448,13 @@
     place = jnp.where(row < 0, 80 + col, jnp.where(row > 15, 88 + col, 16 * col + row))
     place = jnp.pad(place.reshape(1, 192), ((0, 0), (0, 64))).astype(F32)
     speed_refs = jnp.asarray(speed_list)
-    inside = pl.pallas_call(
-        inside_kernel,
-        out_shape=jax.ShapeDtypeStruct((OWN, ROWS, NLON), F32),
-        in_specs=[smem, smem] + [vmem] * 3,
-        scratch_shapes=[pltpu.VMEM((32, NLON), F32)],
-        compiler_params=grant,
-        cost_estimate=pl.CostEstimate(flops=60 * OWN * ROWS * NLON, bytes_accessed=8 * OWN * ROWS * NLON, transcendentals=0),
-    )(device, speed_refs, middle, zonal_all, sea_mask)
     second, stokes = pl.pallas_call(
         final_kernel,
         out_shape=shapes((OWN, ROWS, NLON), (2, 192, 64)),
-        in_specs=[smem, smem, smem] + [vmem] * 6,
-        scratch_shapes=[pltpu.VMEM((128, 128), F32), pltpu.VMEM((24, NLON), F32), pltpu.VMEM((24, NLON), F32)],
+        in_specs=[smem, smem, smem] + [vmem] * 7,
+        scratch_shapes=[pltpu.VMEM((128, 128), F32)] + [pltpu.VMEM((24, NLON), F32)] * 2 + [pltpu.VMEM((32, NLON), F32)],
         compiler_params=grant,
-    )(device, band, speed_refs, inside, rows_b, rows_a, sea_mask, near, place)
+    )(device, band, speed_refs, middle, zonal_all, rows_b, rows_a, sea_mask, near, place)
     return second, stokes.reshape(2, 6, 32, LEV).transpose(0, 3, 1, 2)
 
 

time: 107 us -> 107 us (level)
  waiting for transfers between devices: 34.2 us -> 35.3 us
    pallas_call x1 -> x0, Pallas kernels: 1.35 us -> none  [on_device(): pl.pallas_call(inside_kernel, out_shape=jax.ShapeDtypeStruct((OWN, ROWS,...]
    ppermute x8, waiting for transfers between devices: 3.83 us -> 4.99 us  [swap(): return lax.ppermute(x, axis, pairs + [(j, i) for i, j in pairs])]
  transfers between devices with their start and end apart: 10 -> 10, of which waited for: 5 -> 7; matrix products, arithmetic and copies ran while one was open for 1% -> 1% of each run, Pallas kernels for 2% -> 1%
where the time goes in v10:
time: 107 us; the launch traced here: 106 us
  starting transfers between devices  57.5 us (54%)
  waiting for transfers between devices  35.3 us (33%)
  Pallas kernels  11.1 us (10%)
  local copies, waits for them, and re-layouts  1.52 us (1%)
    all_to_all x2, waiting for transfers between devices, on_device(): lax.all_to_all(sent.reshape(OWNERS, 1, 512), 'bins', 0, 0)  30.3 us
    ppermute x8, starting transfers between devices, swap(): return lax.ppermute(x, axis, pairs + [(j, i) for i, j in pairs])  28.8 us
    all_to_all x2, starting transfers between devices, on_device(): lax.all_to_all(sent.reshape(OWNERS, 1, 512), 'bins', 0, 0)  28.7 us
    pallas_call x1, Pallas kernels, on_device(): pl.pallas_call(points_kernel, out_shape=[jax.ShapeDtypeStruct((4 * OWNERS...  5.43 us
    ppermute x8, waiting for transfers between devices, swap(): return lax.ppermute(x, axis, pairs + [(j, i) for i, j in pairs])  4.99 us
    pallas_call x1, Pallas kernels, on_device(): pl.pallas_call(final_kernel, out_shape=shapes((OWN, ROWS, NLON), (2, 192,...  2.18 us
  transfers between devices with their start and end apart: 10, of which 7 were waited for; matrix products, arithmetic and copies ran while one was open for 1% of the time, Pallas kernels for 1%

profile of v10, /device:TPU:33, one launch (start us, length us, event | category | flops | bytes accessed | tf_op | source)
XLA Modules:
  0.0 106.4 jit_solution(12401546396885981779)
XLA Ops:
  0.6 2.0 %shard_map.104 = (f32[512,128]{1,0:T(8,128)}, f32[128,128]{1,0:T(8,128)}) custom-call(f32[9,16,384]{2,1,0:T(8,128)} %spec.1, s32[16,384]{1,0:T(8,128)} %mask.3, f32[6,32]{1,0:T(8,128)} %current.1), custom_call_target="tpu_custom_call" | custom-call | tf_op jit(solution)/shard_map/pallas_call | solution.py:380
  2.6 19.6 %all-to-all-start = ((f32[128,1,512]{2,1,0:T(1,128)}), f32[128,1,512]{2,1,0:T(1,128)S(1)}, u32[]{:S(2)}, u32[]{:S(2)}) async-start(f32[128,1,512]{2,1,0:T(1,128)} %bitcast.12), calls=%async_computation | async-start | bytes 524288 | tf_op jit(solution)/shard_map/all_to_all | solution.py:388
  22.2 0.0 copy-start
  22.3 0.7 copy-done
  23.0 0.5 shard_map.105
  23.5 0.7 constant_dynamic-slice_fusion.sea_row
  24.2 18.6 %all-to-all-done = f32[128,1,512]{2,1,0:T(1,128)S(1)} async-done(((f32[128,1,512]{2,1,0:T(1,128)}), f32[128,1,512]{2,1,0:T(1,128)S(1)}, u32[]{:S(2)}, u32[]{:S(2)}) %all-to-all-start) | async-done | bytes 262176 | tf_op jit(solution)/shard_map/all_to_all | solution.py:388
  42.9 0.4 shard_map.106
  43.2 3.3 %collective-permute-start.1 = (f32[288,128]{1,0:T(8,128)S(1)}, f32[288,128]{1,0:T(8,128)S(1)}, u32[]{:S(2)}, u32[]{:S(2)}) collective-permute-start(f32[288,128]{1,0:T(8,128)S(1)} %get-tuple-element.45), channel_id=1, source_target_pairs={{4,8},{12,16},{20,24},{28,32},{36,40},{44,48},{52,56},{60,64},{68,... | collective-permute-start | bytes 442376 | tf_op jit(solution)/shard_map/ppermute | solution.py:375
  46.5 2.5 %collective-permute-start.2 = (f32[288,128]{1,0:T(8,128)S(1)}, f32[288,128]{1,0:T(8,128)S(1)}, u32[]{:S(2)}, u32[]{:S(2)}) collective-permute-start(f32[288,128]{1,0:T(8,128)S(1)} %get-tuple-element.46), channel_id=1, source_target_pairs={{0,4},{8,12},{16,20},{24,28},{32,36},{40,44},{48,52},{56,60},{64,6... | collective-permute-start | bytes 442376 | tf_op jit(solution)/shard_map/ppermute | solution.py:375
  49.0 7.9 %collective-permute-start = (f32[128,128]{1,0:T(8,128)S(1)}, f32[128,128]{1,0:T(8,128)S(1)}, u32[]{:S(2)}, u32[]{:S(2)}) collective-permute-start(f32[128,128]{1,0:T(8,128)S(1)} %get-tuple-element.44), channel_id=1, source_target_pairs={{1,2},{2,1},{5,6},{6,5},{9,10},{10,9},{13,14},{14,13},{17,18},{18,... | collective-permute-start | bytes 196616 | tf_op jit(solution)/shard_map/ppermute | solution.py:375
  56.9 1.9 %collective-permute-start.3 = (f32[128,128]{1,0:T(8,128)S(1)}, f32[128,128]{1,0:T(8,128)S(1)}, u32[]{:S(2)}, u32[]{:S(2)}) collective-permute-start(f32[128,128]{1,0:T(8,128)S(1)} %get-tuple-element.47), channel_id=1, source_target_pairs={{0,1},{2,3},{1,0},{3,2},{4,5},{6,7},{5,4},{7,6},{8,9},{10,11},{9,8... | collective-permute-start | bytes 196616 | tf_op jit(solution)/shard_map/ppermute | solution.py:375
  58.8 0.0 collective-permute-done.rows_b
  58.8 1.2 %collective-permute-done.3.rows_a = f32[128,128]{1,0:T(8,128)S(1)} collective-permute-done((f32[128,128]{1,0:T(8,128)S(1)}, f32[128,128]{1,0:T(8,128)S(1)}, u32[]{:S(2)}, u32[]{:S(2)}) %collective-permute-start.3) | collective-permute-done | bytes 65568 | tf_op jit(solution)/shard_map/ppermute | solution.py:375
  60.1 0.0 collective-permute-done.1.columns_b
  60.1 5.4 %shard_map.107 = (f32[512,128]{1,0:T(8,128)}, bf16[1152,256]{1,0:T(8,128)(2,1)S(1)}) custom-call(s32[1]{0:T(128)} %bitcast.device.me, s32[1]{0:T(128)} %bitcast.1.band, f32[512,128]{1,0:T(8,128)S(1)} %bitcast.10, f32[128,128]{1,0:T(8,128)S(1)} %collective-permute-done.rows_b, f32[288,128]{1,0:T(8,128)S(1)} %collective-permute-done.1.columns_b, ...), custom_call_target="tpu_custom_call" | custom-call | tf_op jit(solution)/shard_map/pallas_call | solution.py:410
  65.5 9.1 %all-to-all-start.1 = ((f32[128,1,512]{2,1,0:T(1,128)}), f32[128,1,512]{2,1,0:T(1,128)S(1)}, u32[]{:S(2)}, u32[]{:S(2)}) async-start(f32[128,1,512]{2,1,0:T(1,128)} %bitcast.4), calls=%async_computation.1 | async-start | bytes 524288 | tf_op jit(solution)/shard_map/all_to_all | solution.py:421
  74.7 0.0 copy-start.6
  74.7 0.4 shard_map.108
  75.0 5.2 %collective-permute-start.4 = (f32[16,128]{1,0:T(8,128)S(1)}, f32[16,128]{1,0:T(8,128)S(1)}, u32[]{:S(2)}, u32[]{:S(2)}) collective-permute-start(f32[16,128]{1,0:T(8,128)S(1)} %get-tuple-element.57), channel_id=1, source_target_pairs={{4,8},{12,16},{20,24},{28,32},{36,40},{44,48},{52,56},{60,64},{68,... | collective-permute-start | bytes 24584 | tf_op jit(solution)/shard_map/ppermute | solution.py:375
  80.3 1.9 %collective-permute-start.5 = (f32[16,128]{1,0:T(8,128)S(1)}, f32[16,128]{1,0:T(8,128)S(1)}, u32[]{:S(2)}, u32[]{:S(2)}) collective-permute-start(f32[16,128]{1,0:T(8,128)S(1)} %get-tuple-element.58), channel_id=1, source_target_pairs={{0,4},{8,12},{16,20},{24,28},{32,36},{40,44},{48,52},{56,60},{64,6... | collective-permute-start | bytes 24584 | tf_op jit(solution)/shard_map/ppermute | solution.py:375
  82.2 0.1 select_select_fusion
  82.3 0.1 reshape.116
  82.4 0.8 collective-permute-done.4.drift_b
  83.1 1.8 %collective-permute-done.5.drift_a = f32[16,128]{1,0:T(8,128)S(1)} collective-permute-done((f32[16,128]{1,0:T(8,128)S(1)}, f32[16,128]{1,0:T(8,128)S(1)}, u32[]{:S(2)}, u32[]{:S(2)}) %collective-permute-start.5) | collective-permute-done | bytes 8224 | tf_op jit(solution)/shard_map/ppermute | solution.py:375
  85.0 11.7 %all-to-all-done.1 = f32[128,1,512]{2,1,0:T(1,128)S(1)} async-done(((f32[128,1,512]{2,1,0:T(1,128)}), f32[128,1,512]{2,1,0:T(1,128)S(1)}, u32[]{:S(2)}, u32[]{:S(2)}) %all-to-all-start.1) | async-done | bytes 262176 | tf_op jit(solution)/shard_map/all_to_all | solution.py:421
  96.7 0.2 shard_map.109
  96.9 4.2 %collective-permute-start.6 = (f32[24,384]{1,0:T(8,128)S(1)}, f32[24,384]{1,0:T(8,128)S(1)}, u32[]{:S(2)}, u32[]{:S(2)}) collective-permute-start(f32[24,384]{1,0:T(8,128)S(1)} %get-tuple-element.61), channel_id=1, source_target_pairs={{1,2},{2,1},{5,6},{6,5},{9,10},{10,9},{13,14},{14,13},{17,18},{18,... | collective-permute-start | bytes 110600 | tf_op jit(solution)/shard_map/ppermute | solution.py:375
  101.1 1.9 %collective-permute-start.7 = (f32[24,384]{1,0:T(8,128)S(1)}, f32[24,384]{1,0:T(8,128)S(1)}, u32[]{:S(2)}, u32[]{:S(2)}) collective-permute-start(f32[24,384]{1,0:T(8,128)S(1)} %get-tuple-element.62), channel_id=1, source_target_pairs={{0,1},{2,3},{1,0},{3,2},{4,5},{6,7},{5,4},{7,6},{8,9},{10,11},{9,8... | collective-permute-start | bytes 110600 | tf_op jit(solution)/shard_map/ppermute | solution.py:375
  103.0 0.7 collective-permute-done.6.rows_b
  103.7 0.5 collective-permute-done.7.rows_a
  104.2 2.2 %shard_map.110 = (f32[9,16,384]{2,1,0:T(8,128)}, f32[2,192,64]{2,1,0:T(8,128)}) custom-call(s32[1]{0:T(128)} %bitcast.device.me, s32[1]{0:T(128)} %bitcast.1.band, f32[2304]{0:T(1024)S(1)} %copy-done.3, f32[144,384]{1,0:T(8,128)S(1)} %get-tuple-element.59.middle, f32[16,384]{1,0:T(8,128)S(1)} %get-tuple-element.60.zonal, ...), custom_call_target="tpu_custom_call" | custom-call | tf_op jit(solution)/shard_map/pallas_call | solution.py:451
  (17 shorter events, 0.0 us)
Async XLA Ops:
  2.6 19.6 %copy-start.4 = (s32[1152]{0:T(1024)S(1)}, s32[1152]{0:T(1024)}, u32[]{:S(2)}) copy-start(s32[1152]{0:T(1024)} %param.12) | copy-start | bytes 13828
  2.6 19.6 %copy-start.5 = (s32[1152]{0:T(1024)S(1)}, s32[1152]{0:T(1024)}, u32[]{:S(2)}) copy-start(s32[1152]{0:T(1024)} %param.13) | copy-start | bytes 13828
  2.6 40.2 %all-to-all-start = ((f32[128,1,512]{2,1,0:T(1,128)}), f32[128,1,512]{2,1,0:T(1,128)S(1)}, u32[]{:S(2)}, u32[]{:S(2)}) async-start(f32[128,1,512]{2,1,0:T(1,128)} %bitcast.12), calls=%async_computation | async-start | bytes 524288 | tf_op jit(solution)/shard_map/all_to_all | solution.py:388
  22.2 0.8 copy-start
  42.9 17.2 %copy-start.2 = (bf16[128,256]{1,0:T(8,128)(2,1)S(1)}, bf16[128,256]{1,0:T(8,128)(2,1)}, u32[]{:S(2)}) copy-start(bf16[128,256]{1,0:T(8,128)(2,1)} %constant.74.clone.stencil) | copy-start | bytes 196612
  43.2 16.8 %collective-permute-start.1 = (f32[288,128]{1,0:T(8,128)S(1)}, f32[288,128]{1,0:T(8,128)S(1)}, u32[]{:S(2)}, u32[]{:S(2)}) collective-permute-start(f32[288,128]{1,0:T(8,128)S(1)} %get-tuple-element.45), channel_id=1, source_target_pairs={{4,8},{12,16},{20,24},{28,32},{36,40},{44,48},{52,56},{60,64},{68,... | collective-permute-start | bytes 442376 | tf_op jit(solution)/shard_map/ppermute | solution.py:375
  46.5 13.5 %collective-permute-start.2 = (f32[288,128]{1,0:T(8,128)S(1)}, f32[288,128]{1,0:T(8,128)S(1)}, u32[]{:S(2)}, u32[]{:S(2)}) collective-permute-start(f32[288,128]{1,0:T(8,128)S(1)} %get-tuple-element.46), channel_id=1, source_target_pairs={{0,4},{8,12},{16,20},{24,28},{32,36},{40,44},{48,52},{56,60},{64,6... | collective-permute-start | bytes 442376 | tf_op jit(solution)/shard_map/ppermute | solution.py:375
  49.0 9.8 %collective-permute-start = (f32[128,128]{1,0:T(8,128)S(1)}, f32[128,128]{1,0:T(8,128)S(1)}, u32[]{:S(2)}, u32[]{:S(2)}) collective-permute-start(f32[128,128]{1,0:T(8,128)S(1)} %get-tuple-element.44), channel_id=1, source_target_pairs={{1,2},{2,1},{5,6},{6,5},{9,10},{10,9},{13,14},{14,13},{17,18},{18,... | collective-permute-start | bytes 196616 | tf_op jit(solution)/shard_map/ppermute | solution.py:375
  56.9 3.1 %collective-permute-start.3 = (f32[128,128]{1,0:T(8,128)S(1)}, f32[128,128]{1,0:T(8,128)S(1)}, u32[]{:S(2)}, u32[]{:S(2)}) collective-permute-start(f32[128,128]{1,0:T(8,128)S(1)} %get-tuple-element.47), channel_id=1, source_target_pairs={{0,1},{2,3},{1,0},{3,2},{4,5},{6,7},{5,4},{7,6},{8,9},{10,11},{9,8... | collective-permute-start | bytes 196616 | tf_op jit(solution)/shard_map/ppermute | solution.py:375
  65.5 31.1 %all-to-all-start.1 = ((f32[128,1,512]{2,1,0:T(1,128)}), f32[128,1,512]{2,1,0:T(1,128)S(1)}, u32[]{:S(2)}, u32[]{:S(2)}) async-start(f32[128,1,512]{2,1,0:T(1,128)} %bitcast.4), calls=%async_computation.1 | async-start | bytes 524288 | tf_op jit(solution)/shard_map/all_to_all | solution.py:421
  74.7 7.5 %copy-start.6 = (s32[6,32]{1,0:T(8,128)S(1)}, s32[6,32]{1,0:T(8,128)}, u32[]{:S(2)}) copy-start(s32[6,32]{1,0:T(8,128)} %param.14) | copy-start | bytes 2308
  75.0 8.1 %collective-permute-start.4 = (f32[16,128]{1,0:T(8,128)S(1)}, f32[16,128]{1,0:T(8,128)S(1)}, u32[]{:S(2)}, u32[]{:S(2)}) collective-permute-start(f32[16,128]{1,0:T(8,128)S(1)} %get-tuple-element.57), channel_id=1, source_target_pairs={{4,8},{12,16},{20,24},{28,32},{36,40},{44,48},{52,56},{60,64},{68,... | collective-permute-start | bytes 24584 | tf_op jit(solution)/shard_map/ppermute | solution.py:375
  80.3 4.7 %collective-permute-start.5 = (f32[16,128]{1,0:T(8,128)S(1)}, f32[16,128]{1,0:T(8,128)S(1)}, u32[]{:S(2)}, u32[]{:S(2)}) collective-permute-start(f32[16,128]{1,0:T(8,128)S(1)} %get-tuple-element.58), channel_id=1, source_target_pairs={{0,4},{8,12},{16,20},{24,28},{32,36},{40,44},{48,52},{56,60},{64,6... | collective-permute-start | bytes 24584 | tf_op jit(solution)/shard_map/ppermute | solution.py:375
  96.6 7.5 %copy-start.1 = (s32[16,384]{1,0:T(8,128)S(1)}, s32[16,384]{1,0:T(8,128)}, u32[]{:S(2)}) copy-start(s32[16,384]{1,0:T(8,128)} %mask.3) | copy-start | bytes 73732
  96.7 7.5 %copy-start.3 = (f32[2304]{0:T(1024)S(1)}, f32[2304]{0:T(1024)}, u32[]{:S(2)}) copy-start(f32[2304]{0:T(1024)} %constant.75.clone.speeds) | copy-start | bytes 27652
  96.9 6.8 %collective-permute-start.6 = (f32[24,384]{1,0:T(8,128)S(1)}, f32[24,384]{1,0:T(8,128)S(1)}, u32[]{:S(2)}, u32[]{:S(2)}) collective-permute-start(f32[24,384]{1,0:T(8,128)S(1)} %get-tuple-element.61), channel_id=1, source_target_pairs={{1,2},{2,1},{5,6},{6,5},{9,10},{10,9},{13,14},{14,13},{17,18},{18,... | collective-permute-start | bytes 110600 | tf_op jit(solution)/shard_map/ppermute | solution.py:375
  101.1 3.1 %collective-permute-start.7 = (f32[24,384]{1,0:T(8,128)S(1)}, f32[24,384]{1,0:T(8,128)S(1)}, u32[]{:S(2)}, u32[]{:S(2)}) collective-permute-start(f32[24,384]{1,0:T(8,128)S(1)} %get-tuple-element.62), channel_id=1, source_target_pairs={{0,1},{2,3},{1,0},{3,2},{4,5},{6,7},{5,4},{7,6},{8,9},{10,11},{9,8... | collective-permute-start | bytes 110600 | tf_op jit(solution)/shard_map/ppermute | solution.py:375
